TPU v7x, 256 devices: a whole 4x4x8 slice. The times are simulated.
256 devices in a mesh: ctx: 32 (over y, z), head: 8 (over x, core).
Axes of the slice: x: 4, y: 4, z: 8, core: 2. Of those that a mesh axis runs over, the one named last changes fastest.
Arguments:
- queries: bfloat16 [16384, 40, 128], P(('ctx', 'head')), may hold values from -40 to 40
- keys: bfloat16 [16384, 8, 128], P(('ctx', 'head')), may hold values from -6 to 6
- values: bfloat16 [16384, 8, 128], P(('ctx', 'head')), may hold values from -6 to 6
- out_grad: bfloat16 [16384, 40, 128], P(('ctx', 'head')), may hold values from -6 to 6
- ancestors: int32 [128, 16], replicated, may hold values from -1 to 126, as said below
- parents: int32 [128, 128], P('ctx'), may hold values from 0 to 126, as said below
Outputs:
- attended: bfloat16 [16384, 40, 128], P(('ctx', 'head'))
- query_grad: bfloat16 [16384, 40, 128], P(('ctx', 'head'))
- key_grad: bfloat16 [16384, 8, 128], P(('ctx', 'head'))
- value_grad: bfloat16 [16384, 8, 128], P(('ctx', 'head'))
Inputs may be any that keep to these rules, and one draw needn't show every extreme that they name: Row b holds block b's ancestor blocks, the root first and one a depth, then -1. Block 0 is the root; every other row begins with 0. Every ancestor of block b is block b - 1 or an ancestor of block b - 1. The last block has exactly 16 ancestors. parents[b, 0] = 0 and parents[b, t] < t for t > 0; parents[b, 127] = 126.
All inputs are finite; a program needn't handle non-finite values.
Results may differ from a plain program's by a relative error of at most 0.017.
The roundings to bfloat16 on the way count: a program that leaves them out, or rounds other values in their place, can miss the bound.
Values may be sent and summed in bfloat16 or wider, within the bound.
No kernel may reach another device: no remote copies, remote signals or barrier semaphores. Data moves between devices by JAX's collectives and lax.ppermute only.
A program may use at most 192 MiB of HBM per device.

v0:
```python
import math

import jax
import jax.numpy as jnp
from jax import lax
from jax.sharding import PartitionSpec as P

HD = 128
GROUP = 5
BLK = 128


def tree_reach(parents):
    block_width = parents.shape[-1]
    parent_hops = (parents[..., None] == jnp.arange(block_width, dtype=jnp.int32)).astype(
        jnp.float32
    )
    reached = jnp.minimum(jnp.eye(block_width, dtype=jnp.float32) + parent_hops, 1.0)
    for repeat_no in range(max(1, (block_width - 1).bit_length())):
        reached = jnp.minimum(
            jnp.einsum("bts,bsu->btu", reached, reached, precision=lax.Precision.HIGHEST), 1.0
        )
    return reached


def body(queries, keys, values, out_grad, ancestors, parents):
    query_here, grad_here, keys_here, values_here = (
        lax.all_to_all(queries, "head", split_axis=1, concat_axis=0, tiled=True),
        lax.all_to_all(out_grad, "head", split_axis=1, concat_axis=0, tiled=True),
        lax.all_to_all(keys, "head", split_axis=1, concat_axis=0, tiled=True),
        lax.all_to_all(values, "head", split_axis=1, concat_axis=0, tiled=True),
    )
    tokens_here = query_here.shape[0]
    groups_here = keys_here.shape[1]
    blocks_here = tokens_here // BLK
    score_scale = 1.0 / math.sqrt(HD)
    query_blocks = query_here.reshape(blocks_here, BLK, groups_here, GROUP, HD)
    grad_blocks = grad_here.reshape(blocks_here, BLK, groups_here, GROUP, HD)
    key_blocks = keys_here.reshape(blocks_here, BLK, groups_here, HD)
    value_blocks = values_here.reshape(blocks_here, BLK, groups_here, HD)
    first_block = lax.axis_index("ctx") * blocks_here
    my_lists = lax.dynamic_slice_in_dim(ancestors, first_block, blocks_here, 0)
    listed = my_lists >= 0
    listed_float = listed.astype(jnp.float32)
    depth_each = jnp.sum(listed.astype(jnp.int32), axis=1)
    loop_count = jnp.max(depth_each)
    within_mask = tree_reach(parents) > 0.5
    pool_keys, pool_values = (
        lax.all_gather(key_blocks, "ctx", axis=0, tiled=True),
        lax.all_gather(value_blocks, "ctx", axis=0, tiled=True),
    )
    slot_index = jnp.where(listed, my_lists, 0)
    own_index = first_block + jnp.arange(blocks_here, dtype=jnp.int32)

    def fetch(position):
        chosen = slot_index[:, position]
        seen = jnp.broadcast_to(listed[:, position][:, None, None], (blocks_here, BLK, BLK))
        return (pool_keys[chosen], pool_values[chosen], seen, chosen)

    def scores_of(key_part, seen):
        raw_scores = (
            jnp.einsum(
                "iqgrd,ikgd->igrqk", query_blocks, key_part, preferred_element_type=jnp.float32
            )
            * score_scale
        )
        return jnp.where(seen[:, None, None], raw_scores, -jnp.inf)

    diag_scores = scores_of(key_blocks, within_mask)
    start_max = jnp.max(diag_scores, axis=-1)
    start_total = jnp.sum(jnp.exp(diag_scores - start_max[..., None]), axis=-1)

    def first_pass(position, carry):
        running_max, running_total = carry
        fetched = fetch(position)
        scores = scores_of(fetched[0], fetched[2])
        updated = jnp.maximum(running_max, jnp.max(scores, axis=-1))
        running_total = running_total * jnp.exp(running_max - updated) + jnp.sum(
            jnp.exp(scores - updated[..., None]), axis=-1
        )
        return (updated, running_total)

    row_max, row_total = lax.fori_loop(0, loop_count, first_pass, (start_max, start_total))

    def probs_of(scores):
        probs = jnp.exp(scores - row_max[..., None]) / row_total[..., None]
        return (probs, probs.astype(jnp.bfloat16))

    start_sum = jnp.einsum(
        "igrqk,ikgd->iqgrd",
        probs_of(diag_scores)[1],
        value_blocks,
        preferred_element_type=jnp.float32,
    )

    def second_pass(position, attended_sum):
        fetched = fetch(position)
        weights = probs_of(scores_of(fetched[0], fetched[2]))[1]
        return attended_sum + jnp.einsum(
            "igrqk,ikgd->iqgrd", weights, fetched[1], preferred_element_type=jnp.float32
        )

    attended = lax.fori_loop(0, loop_count, second_pass, start_sum).astype(jnp.bfloat16)
    delta = jnp.einsum(
        "iqgrd,iqgrd->igrq", grad_blocks, attended, preferred_element_type=jnp.float32
    )

    def gradients(key_part, value_part, seen):
        probs, weights = probs_of(scores_of(key_part, seen))
        dprob = jnp.einsum(
            "iqgrd,ikgd->igrqk", grad_blocks, value_part, preferred_element_type=jnp.float32
        )
        dscore = (probs * (dprob - delta[..., None])).astype(jnp.bfloat16)
        query_part = (
            jnp.einsum("igrqk,ikgd->iqgrd", dscore, key_part, preferred_element_type=jnp.float32)
            * score_scale
        )
        key_part_grad = (
            jnp.einsum(
                "igrqk,iqgrd->ikgd", dscore, query_blocks, preferred_element_type=jnp.float32
            )
            * score_scale
        )
        value_part_grad = jnp.einsum(
            "igrqk,iqgrd->ikgd", weights, grad_blocks, preferred_element_type=jnp.float32
        )
        return (query_part, key_part_grad, value_part_grad)

    diag_grads = gradients(key_blocks, value_blocks, within_mask)
    key_pool_grad = jnp.zeros(pool_keys.shape, jnp.float32).at[own_index].add(diag_grads[1])
    value_pool_grad = jnp.zeros(pool_values.shape, jnp.float32).at[own_index].add(diag_grads[2])

    def third_pass(position, carry):
        query_acc, key_acc, value_acc = carry
        fetched = fetch(position)
        parts = gradients(fetched[0], fetched[1], fetched[2])
        weight_rows = listed_float[:, position][:, None, None, None]
        return (
            query_acc + parts[0],
            key_acc.at[fetched[3]].add(parts[1] * weight_rows),
            value_acc.at[fetched[3]].add(parts[2] * weight_rows),
        )

    query_acc, key_pool_grad, value_pool_grad = lax.fori_loop(
        0, loop_count, third_pass, (diag_grads[0], key_pool_grad, value_pool_grad)
    )
    key_local, value_local = (
        lax.psum_scatter(
            key_pool_grad.astype(jnp.bfloat16), "ctx", scatter_dimension=0, tiled=True
        ).astype(jnp.float32),
        lax.psum_scatter(
            value_pool_grad.astype(jnp.bfloat16), "ctx", scatter_dimension=0, tiled=True
        ).astype(jnp.float32),
    )
    heads_here = groups_here * GROUP
    attended_out = attended.reshape(tokens_here, heads_here, HD)
    query_grad = query_acc.astype(jnp.bfloat16).reshape(tokens_here, heads_here, HD)
    key_grad = key_local.astype(jnp.bfloat16).reshape(tokens_here, groups_here, HD)
    value_grad = value_local.astype(jnp.bfloat16).reshape(tokens_here, groups_here, HD)
    results = (
        lax.all_to_all(attended_out, "head", split_axis=0, concat_axis=1, tiled=True),
        lax.all_to_all(query_grad, "head", split_axis=0, concat_axis=1, tiled=True),
        lax.all_to_all(key_grad, "head", split_axis=0, concat_axis=1, tiled=True),
        lax.all_to_all(value_grad, "head", split_axis=0, concat_axis=1, tiled=True),
    )
    return (results[0], results[1], results[2], results[3])


def solution(mesh):
    placed = (
        P(("ctx", "head"), None, None),
        P(("ctx", "head"), None, None),
        P(("ctx", "head"), None, None),
        P(("ctx", "head"), None, None),
        P(),
        P("ctx", None),
    )
    return jax.shard_map(
        body,
        mesh=mesh,
        in_specs=placed,
        out_specs=(
            P(("ctx", "head"), None, None),
            P(("ctx", "head"), None, None),
            P(("ctx", "head"), None, None),
            P(("ctx", "head"), None, None),
        ),
        check_vma=False,
    )
```

profile of v0, /device:TPU:1, one launch (start us, length us, event | category | flops | bytes accessed | tf_op | source)
XLA Modules:
  0.0 1152.9 jit_solution(9307850168558788434)
XLA Ops:
  8.2 11.6 %all_to_all.132 = bf16[64,8,128]{2,0,1:T(8,128)(2,1)} all-to-all(bf16[64,8,128]{2,0,1:T(8,128)(2,1)S(1)} %copy.105), channel_id=1, replica_groups=mesh['ctx'=32,'head'=8] {'head'}, dimensions={1} | all-to-all | bytes 262144 | tf_op jit(solution)/shard_map/all_to_all | solution.py:30
  19.8 1.6 copy.113
  21.4 4.1 all-to-all-start.2
  26.5 4.3 all-to-all-done.2
  30.8 4.3 all-to-all-start.1
  39.3 6.8 all-to-all-done.1
  46.0 4.3 all-to-all-start.4
  53.6 7.7 all-to-all-done.4
  63.8 36.0 %all-gather.3.cloned.1.call-done = bf16[128,128,1,128]{3,1,2,0:T(8,128)(2,1)} async-done(((bf16[4,128,1,128]{3,1,2,0:T(8,128)(2,1)}), bf16[128,128,1,128]{3,1,2,0:T(8,128)(2,1)}) %all-gather.3.cloned.1.call-update) | async-done | bytes 4194320 | tf_op jit(solution)/shard_map/all_gather | solution.py:49
  99.8 16.6 %while.36 = (s32[]{:T(128)}, f32[4,1,5,128]{3,2,0,1:T(8,128)S(1)}, f32[4,1,5,128]{3,2,0,1:T(8,128)S(1)}, s32[]{:T(128)}, pred[4,16]{0,1:T(8,128)(4,1)}, /*index=...) while((s32[]{:T(128)}, f32[4,1,5,128]{3,2,0,1:T(8,128)S(1)}, ...), condition=%wide.region_7.8_spmd, body=%wide.region_4.7_spmd.sunk | while | flops 85530640 | bytes 3807459 | solution.py:83
  101.1 2.8 gather_fusion
  106.5 2.8 gather_fusion
  111.8 2.8 gather_fusion
  116.4 2.8 convolution_bitcast_fusion.5
  119.2 2.8 copy.116
  122.0 2.4 convolution_bitcast_fusion.6
  124.4 57.7 %all-gather.5.cloned.1.call-done = bf16[128,128,1,128]{3,1,2,0:T(8,128)(2,1)} async-done(((bf16[4,128,1,128]{3,1,2,0:T(8,128)(2,1)}), bf16[128,128,1,128]{3,1,2,0:T(8,128)(2,1)}) %all-gather.5.cloned.1.call-update) | async-done | bytes 4194320 | tf_op jit(solution)/shard_map/all_gather | solution.py:50
  182.1 32.1 %while.37 = (s32[]{:T(128)}, f32[4,128,1,5,128]{1,4,3,0,2:T(8,128)}, s32[]{:T(128)}, s32[4,16]{0,1:T(8,128)}, bf16[128,128,1,128]{3,1,0,2:T(8,128)(2,1)}, /*inde...) while((s32[]{:T(128)}, ...), condition=%wide.region_9.10_spmd, body=%wide.region_8.9_spmd.sunk | while | flops 169739280 | bytes 4088067 | solution.py:103
  183.3 2.8 gather_fusion.1
  186.1 2.8 gather_fusion.2
  189.5 3.1 fusion.130
  193.8 2.8 gather_fusion.1
  196.6 2.8 gather_fusion.2
  200.0 3.1 fusion.130
  204.3 2.8 gather_fusion.1
  207.1 2.8 gather_fusion.2
  210.5 3.1 fusion.130
  214.7 1.6 copy.120
  218.0 1.3 fusion.57
  220.0 1.5 copy.131
  221.6 4.3 broadcast.165.clone.1
  225.9 2.3 scatter_fusion.3
  228.2 4.3 broadcast.165.clone
  232.5 2.3 scatter_fusion.2
  234.8 56.8 %while.38 = (s32[]{:T(128)}, f32[4,128,1,5,128]{1,4,3,0,2:T(8,128)}, f32[128,128,1,128]{3,1,0,2:T(8,128)}, f32[128,128,1,128]{3,1,0,2:T(8,128)}, s32[]{:T(128)},...) while((s32[]{:T(128)}, ...), condition=%wide.region_15.16_spmd, body=%wide.region_12.15_spmd.sunk | while | flops 422970368 | bytes 14797407 | solution.py:144
  236.3 2.8 gather_fusion.3
  240.1 2.8 gather_fusion.4
  244.9 2.4 scatter_fusion
  248.3 2.4 scatter_fusion.1
  250.8 2.9 fusion.144
  255.0 2.8 gather_fusion.3
  258.9 2.8 gather_fusion.4
  263.6 2.4 scatter_fusion
  267.0 2.4 scatter_fusion.1
  269.4 2.9 fusion.144
  273.6 2.8 gather_fusion.3
  277.5 2.8 gather_fusion.4
  282.2 2.4 scatter_fusion
  285.6 2.4 scatter_fusion.1
  288.1 2.9 fusion.144
  291.6 6.3 convert_element_type.56
  298.0 6.3 convert_element_type.57
  306.0 1.5 copy.137
  307.4 7.7 all-to-all-start.5
  315.1 1.5 copy.121
  316.7 13.6 %all-to-all-done.5 = bf16[512,5,128]{2,1,0:T(8,128)(2,1)S(1)} async-done(((bf16[512,5,128]{2,1,0:T(8,128)(2,1)}), bf16[512,5,128]{2,1,0:T(8,128)(2,1)S(1)}, u32[]{:S(2)}, u32[]{:S(2)}) %all-to-all-start.5) | async-done | bytes 655392 | tf_op jit(solution)/shard_map/all_to_all | solution.py:162
  330.2 4.3 all-to-all-start.3
  334.6 569.8 %reduce-scatter.3.cloned.1.call-done = bf16[4,128,1,128]{3,1,0,2:T(8,128)(2,1)} async-done(((bf16[128,128,1,128]{3,1,0,2:T(8,128)(2,1)}), bf16[4,128,1,128]{3,1,0,2:T(8,128)(2,1)}) %reduce-scatter.3.cloned.1.call-update) | async-done | bytes 131088 | tf_op jit(solution)/shard_map/reduce_scatter | solution.py:148
  904.9 1.6 reduce.6
  907.2 10.1 all-to-all-start.6
  917.3 210.6 %reduce-scatter.5.cloned.1.call-done = bf16[4,128,1,128]{3,1,0,2:T(8,128)(2,1)} async-done(((bf16[128,128,1,128]{3,1,0,2:T(8,128)(2,1)}), bf16[4,128,1,128]{3,1,0,2:T(8,128)(2,1)}) %reduce-scatter.5.cloned.1.call-update) | async-done | bytes 131088 | tf_op jit(solution)/shard_map/reduce_scatter | solution.py:151
  1127.9 1.6 reduce.7
  1130.1 10.1 all-to-all-start.7
  1144.0 1.5 all-to-all-done.7
  (171 shorter events, 46.8 us)
Async XLA Ops:
  7.2 18.4 %copy-start.7 = (bf16[64,40,128]{2,1,0:T(8,128)(2,1)S(1)}, bf16[64,40,128]{2,1,0:T(8,128)(2,1)}, u32[]{:S(2)}) copy-start(bf16[64,40,128]{2,1,0:T(8,128)(2,1)} %param.12) | copy-start | bytes 1966084
  7.2 92.6 %all-gather.3.cloned.1.call-start = ((), (), s32[]{:S(2)}) async-start(), calls=%async_computation.10 | async-start | bytes 4325376 | tf_op jit(solution)/shard_map/all_gather | solution.py:49
  21.4 9.4 all-to-all-start.2
  25.5 10.3 copy-start.22
  30.8 4.3 copy-start.16
  30.8 15.2 %all-to-all-start.1 = ((bf16[64,40,128]{2,0,1:T(8,128)(2,1)}), bf16[64,40,128]{2,0,1:T(8,128)(2,1)S(1)}, u32[]{:S(2)}, u32[]{:S(2)}) async-start(bf16[64,40,128]{2,0,1:T(8,128)(2,1)} %copy.106), calls=%async_computation.1 | async-start | bytes 1310720 | tf_op jit(solution)/shard_map/all_to_all | solution.py:28
  35.1 146.9 %all-gather.5.cloned.1.call-start = ((), (), s32[]{:S(2)}) async-start(), calls=%async_computation.11 | async-start | bytes 4325376 | tf_op jit(solution)/shard_map/all_gather | solution.py:50
  35.9 1.6 copy-start.8
  38.9 12.0 %copy-start.20 = (s32[128,16]{0,1:T(8,128)S(1)}, s32[128,16]{0,1:T(8,128)}, u32[]{:S(2)}) copy-start(s32[128,16]{0,1:T(8,128)} %param.16) | copy-start | bytes 24580
  46.0 15.2 %all-to-all-start.4 = ((bf16[64,40,128]{2,0,1:T(8,128)(2,1)}), bf16[64,40,128]{2,0,1:T(8,128)(2,1)S(1)}, u32[]{:S(2)}, u32[]{:S(2)}) async-start(bf16[64,40,128]{2,0,1:T(8,128)(2,1)} %copy.124), calls=%async_computation.4 | async-start | bytes 1310720 | tf_op jit(solution)/shard_map/all_to_all | solution.py:29
  50.4 854.0 %reduce-scatter.3.cloned.1.call-start = ((), (), s32[]{:S(2)}) async-start(), calls=%async_computation.12 | async-start | bytes 4325376 | tf_op jit(solution)/shard_map/reduce_scatter | solution.py:148
  51.6 9.7 copy-start.21
  61.3 0.9 copy-start.6
  62.6 1.1 copy-start.4
  99.8 16.6 %copy-start.17 = (bf16[64,8,128]{2,0,1:T(8,128)(2,1)S(1)}, bf16[64,8,128]{2,0,1:T(8,128)(2,1)}, u32[]{:S(2)}) copy-start(bf16[64,8,128]{2,0,1:T(8,128)(2,1)} %copy-done.16) | copy-start | bytes 393220
  214.1 0.6 copy-start.12
  214.7 2.1 copy-start.13
  216.4 2.9 copy-start.2
  216.4 1.6 copy-start.5
  218.0 1.4 copy-start.9
  221.6 4.3 copy-start.18
  221.6 4.3 copy-start.23
  228.2 6.6 copy-start.10
  228.2 6.6 copy-start.14
  236.3 3.9 copy-start.19
  239.0 1.1 copy-start.1
  250.7 3.0 copy-start.11
  250.8 3.0 copy-start.15
  255.0 3.9 copy-start.19
  257.8 1.1 copy-start.1
  269.4 3.0 copy-start.11
  269.4 3.0 copy-start.15
  273.6 3.9 copy-start.19
  276.4 1.1 copy-start.1
  288.1 3.0 copy-start.11
  288.1 3.0 copy-start.15
  297.9 829.9 %reduce-scatter.5.cloned.1.call-start = ((), (), s32[]{:S(2)}) async-start(), calls=%async_computation.13 | async-start | bytes 4325376 | tf_op jit(solution)/shard_map/reduce_scatter | solution.py:151
  304.3 1.3 copy-start
  307.4 7.7 copy-start.3
  307.4 22.8 %all-to-all-start.5 = ((bf16[512,5,128]{2,1,0:T(8,128)(2,1)}), bf16[512,5,128]{2,1,0:T(8,128)(2,1)S(1)}, u32[]{:S(2)}, u32[]{:S(2)}) async-start(bf16[512,5,128]{2,1,0:T(8,128)(2,1)} %copy.137), calls=%async_computation.5 | async-start | bytes 2097152 | tf_op jit(solution)/shard_map/all_to_all | solution.py:162
  330.2 576.9 %all-to-all-start.3 = ((bf16[512,5,128]{2,1,0:T(8,128)(2,1)}), bf16[512,5,128]{2,1,0:T(8,128)(2,1)S(1)}, u32[]{:S(2)}, u32[]{:S(2)}) async-start(bf16[512,5,128]{2,1,0:T(8,128)(2,1)} %copy.121), calls=%async_computation.3 | async-start | bytes 2097152 | tf_op jit(solution)/shard_map/all_to_all | solution.py:161
  907.2 222.9 %all-to-all-start.6 = ((bf16[8,2,4096]{2,1,0:T(2,128)(2,1)}), bf16[8,2,4096]{2,1,0:T(2,128)(2,1)S(1)}, u32[]{:S(2)}, u32[]{:S(2)}) async-start(bf16[8,2,4096]{2,1,0:T(2,128)(2,1)} %reshape.346), calls=%async_computation.7 | async-start | bytes 262144 | tf_op jit(solution)/shard_map/all_to_all | solution.py:163
  1130.1 15.4 %all-to-all-start.7 = ((bf16[8,2,4096]{2,1,0:T(2,128)(2,1)}), bf16[8,2,4096]{2,1,0:T(2,128)(2,1)S(1)}, u32[]{:S(2)}, u32[]{:S(2)}) async-start(bf16[8,2,4096]{2,1,0:T(2,128)(2,1)} %reshape.348), calls=%async_computation.9 | async-start | bytes 262144 | tf_op jit(solution)/shard_map/all_to_all | solution.py:164
Sparse Core Ops, SparseCore 0:
  19.9 79.8 all-gather.2
  103.0 79.0 all-gather.4
  298.1 606.2 reduce-scatter.2
  908.6 219.1 reduce-scatter.4
where the time goes:
time: 1160 us; the launch traced here: 1150 us
  waiting for transfers between devices  909 us (78%)
  local copies, waits for them, and re-layouts  81.2 us (7%)
  other arithmetic  48.8 us (4%)
  starting transfers between devices  45 us (4%)
  matrix products  35.8 us (3%)
  between operations  14.1 us (1%)
  blocking collectives  11.6 us (1%)
    reduce_scatter x1, waiting for transfers between devices, body(): lax.psum_scatter(key_pool_grad.astype(jnp.bfloat16), 'ctx', scatter_dimen...  570 us
    reduce_scatter x1, waiting for transfers between devices, body(): lax.psum_scatter(value_pool_grad.astype(jnp.bfloat16), 'ctx', scatter_dim...  211 us
    all_gather x1, waiting for transfers between devices, body(): lax.all_gather(value_blocks, 'ctx', axis=0, tiled=True)  57.7 us
    gather x15, local copies, waits for them, and re-layouts, fetch(): return (pool_keys[chosen], pool_values[chosen], seen, chosen)  41.4 us
    all_gather x1, waiting for transfers between devices, body(): lax.all_gather(key_blocks, 'ctx', axis=0, tiled=True)  36 us
  transfers between devices with their start and end apart: 11, of which 9 were waited for; matrix products, arithmetic and copies ran while one was open for 4% of the time, Pallas kernels for 0%

commit v1 on v0

v1 whole, which is shorter than its diff:
```python
import math

import jax
import jax.numpy as jnp
from jax import lax
from jax.experimental import pallas as pl
from jax.experimental.pallas import tpu as pltpu
from jax.sharding import Mesh, PartitionSpec as P

HD = 128
GROUP = 5
BLK = 128
NBL = 4
MAXD = 16
QN = GROUP * BLK
SCALE = 1.0 / math.sqrt(HD)
LOG2E = 1.0 / math.log(2.0)
NEG = -1e30
NPAIR = MAXD // 2 + NBL // 2
OWNP = MAXD // 2


def tree_reach_t(parents):
    block_width = parents.shape[-1]
    hops = parents[:, None, :] == jnp.arange(block_width, dtype=jnp.int32)[None, :, None]
    eye = jnp.eye(block_width, dtype=jnp.bool_)[None]
    reached = (hops | eye).astype(jnp.bfloat16)
    for _ in range(max(1, (block_width - 1).bit_length())):
        product = jnp.einsum("bts,bsu->btu", reached, reached, preferred_element_type=jnp.float32)
        reached = jnp.minimum(product, 1.0).astype(jnp.bfloat16)
    return reached.astype(jnp.float32)


def dot(a, b, dims):
    return lax.dot_general(a, b, (dims, ((), ())), preferred_element_type=jnp.float32)


def kernel(
    info_ref, q_ref, g_ref, own_ref, pool_ref, within_ref,
    o_ref, dq_ref, grad_ref,
    k_s, v_s, kt_s, vt_s, s_s, w_s, dk_s, dv_s,
):
    grad_ref[...] = jnp.zeros_like(grad_ref)
    dk_s[...] = jnp.zeros_like(dk_s)
    dv_s[...] = jnp.zeros_like(dv_s)
    remote = info_ref[0, 0]
    pairs = (remote + 1) // 2

    def take(p, half, kv):
        k = kv[:, 0].reshape(BLK, HD)
        v = kv[:, 1].reshape(BLK, HD)
        k_s[p, half * BLK:(half + 1) * BLK, :] = k
        v_s[p, half * BLK:(half + 1) * BLK, :] = v
        kt_s[p, :, half * BLK:(half + 1) * BLK] = k.T
        vt_s[p, :, half * BLK:(half + 1) * BLK] = v.T

    for j in range(NBL):
        take(OWNP + j // 2, j % 2, own_ref[j])

    def load_pair(p, carry):
        for half in range(2):
            block = info_ref[1, 2 * p + half]
            take(p, half, pool_ref[block])
        return carry

    lax.fori_loop(0, pairs, load_pair, 0)

    for i in range(NBL):
        rows = pl.ds(i * BLK, BLK)
        count = info_ref[2 + i, 0]
        my_pairs = (count + 1) // 2
        q = jnp.concatenate([q_ref[rows, r * HD:(r + 1) * HD] for r in range(GROUP)], axis=0)
        g = jnp.concatenate([g_ref[rows, r * HD:(r + 1) * HD] for r in range(GROUP)], axis=0)
        qt = q.T
        gt = g.T
        row_id = lax.broadcasted_iota(jnp.int32, (2 * BLK, 1), 0)

        def fold(x, op):
            y = x.reshape(-1, 8, QN)
            return op(y, axis=0)

        def scores(p, mx):
            raw = dot(k_s[p], qt, ((1,), (0,))) * (SCALE * LOG2E)
            limit = jnp.where(2 * p + 1 < count, 2 * BLK, BLK)
            s = raw + jnp.where(row_id < limit, 0.0, NEG)
            s_s[p] = s
            return jnp.maximum(mx, fold(s, jnp.max))

        mx = lax.fori_loop(0, my_pairs, scores, jnp.full((8, QN), NEG, jnp.float32))
        own_pairs = i // 2 + 1
        for op in range(own_pairs):
            raw = dot(k_s[OWNP + op], qt, ((1,), (0,))) * (SCALE * LOG2E)
            parts = []
            for half in range(2):
                j = 2 * op + half
                piece = raw[half * BLK:(half + 1) * BLK]
                if j < i:
                    piece = piece + jnp.where(info_ref[2 + i, 1 + j] > 0, 0.0, NEG)
                elif j == i:
                    bias = jnp.where(within_ref[i] > 0.5, 0.0, NEG)
                    piece = piece + jnp.concatenate([bias] * GROUP, axis=1)
                else:
                    piece = jnp.full_like(piece, NEG)
                parts.append(piece)
            s = jnp.concatenate(parts, axis=0)
            s_s[OWNP + op] = s
            mx = jnp.maximum(mx, fold(s, jnp.max))
        m = jnp.max(mx, axis=0, keepdims=True)

        def expo(p, total):
            e = jnp.exp2(s_s[p] - m)
            s_s[p] = e
            return total + fold(e, jnp.sum)

        total = lax.fori_loop(0, my_pairs, expo, jnp.zeros((8, QN), jnp.float32))
        for op in range(own_pairs):
            total = expo(OWNP + op, total)
        inv = 1.0 / jnp.sum(total, axis=0, keepdims=True)

        def attend(p, acc):
            prob = s_s[p] * inv
            s_s[p] = prob
            w = prob.astype(jnp.bfloat16)
            dv_s[p] += dot(w, g, ((1,), (0,)))
            return acc + dot(vt_s[p], w, ((1,), (0,)))

        acc = lax.fori_loop(0, my_pairs, attend, jnp.zeros((HD, QN), jnp.float32))
        for op in range(own_pairs):
            acc = attend(OWNP + op, acc)
        ot = acc.astype(jnp.bfloat16)
        delta = jnp.sum(gt.astype(jnp.float32) * ot.astype(jnp.float32), axis=0, keepdims=True)
        for r in range(GROUP):
            o_ref[rows, r * HD:(r + 1) * HD] = ot[:, r * BLK:(r + 1) * BLK].T

        def back(p, acc):
            dprob = dot(v_s[p], gt, ((1,), (0,)))
            ds = (s_s[p] * (dprob - delta)).astype(jnp.bfloat16)
            dk_s[p] += dot(ds, q, ((1,), (0,)))
            return acc + dot(kt_s[p], ds, ((1,), (0,)))

        acc = lax.fori_loop(0, my_pairs, back, jnp.zeros((HD, QN), jnp.float32))
        for op in range(own_pairs):
            acc = back(OWNP + op, acc)
        dqt = (acc * SCALE).astype(jnp.bfloat16)
        for r in range(GROUP):
            dq_ref[rows, r * HD:(r + 1) * HD] = dqt[:, r * BLK:(r + 1) * BLK].T

    def put(block, p, half):
        dk = dk_s[p, pl.ds(half * BLK, BLK), :] * SCALE
        dv = dv_s[p, pl.ds(half * BLK, BLK), :]
        grad_ref[block, :, 0] = dk.astype(jnp.bfloat16).reshape(2, BLK // 2, HD)
        grad_ref[block, :, 1] = dv.astype(jnp.bfloat16).reshape(2, BLK // 2, HD)

    for j in range(NBL):
        put(info_ref[0, 1] + j, OWNP + j // 2, j % 2)

    def put_pair(p, carry):
        put(info_ref[1, 2 * p], p, 0)

        @pl.when(2 * p + 1 < remote)
        def _():
            put(info_ref[1, 2 * p + 1], p, 1)

        return carry

    lax.fori_loop(0, pairs, put_pair, 0)


def info_of(ancestors):
    first = lax.axis_index("ctx") * NBL
    lists = lax.dynamic_slice_in_dim(ancestors, first, NBL, 0)
    remote = jnp.sum(((lists >= 0) & (lists < first)).astype(jnp.int32), axis=1)
    own = first + jnp.arange(NBL, dtype=jnp.int32)
    flags = jnp.any(lists[:, None, :] == own[None, :, None], axis=2).astype(jnp.int32)
    width = MAXD
    head = jnp.zeros((1, width), jnp.int32).at[0, 0].set(remote[0]).at[0, 1].set(first)
    slots = jnp.maximum(lists[:1], 0)
    rest = jnp.concatenate([remote[:, None], flags, jnp.zeros((NBL, width - 1 - NBL), jnp.int32)], axis=1)
    return jnp.concatenate([head, slots, rest], axis=0)


def body(queries, keys, values, out_grad, ancestors, parents):
    tokens = queries.shape[0]
    groups = keys.shape[1]
    kv = jnp.stack([keys, values]).transpose(2, 0, 1, 3)
    kv = lax.all_to_all(kv, "head", split_axis=0, concat_axis=0, tiled=True)
    own = kv.reshape(NBL, 2, 2, BLK // 2, HD)
    pool = lax.all_gather(own, "ctx", axis=0, tiled=True)
    q = lax.all_to_all(queries.reshape(tokens, -1), "head", split_axis=1, concat_axis=0, tiled=True)
    g = lax.all_to_all(out_grad.reshape(tokens, -1), "head", split_axis=1, concat_axis=0, tiled=True)
    within = tree_reach_t(parents)
    info = info_of(ancestors)
    vmem = pl.BlockSpec(memory_space=pltpu.VMEM)
    smem = pl.BlockSpec(memory_space=pltpu.SMEM)
    o, dq, grad = pl.pallas_call(
        kernel,
        out_shape=(
            jax.ShapeDtypeStruct(q.shape, jnp.bfloat16),
            jax.ShapeDtypeStruct(q.shape, jnp.bfloat16),
            jax.ShapeDtypeStruct(pool.shape, jnp.bfloat16),
        ),
        in_specs=[smem] + [vmem] * 5,
        out_specs=(vmem,) * 3,
        scratch_shapes=[
            pltpu.VMEM((NPAIR, 2 * BLK, HD), jnp.bfloat16),
            pltpu.VMEM((NPAIR, 2 * BLK, HD), jnp.bfloat16),
            pltpu.VMEM((NPAIR, HD, 2 * BLK), jnp.bfloat16),
            pltpu.VMEM((NPAIR, HD, 2 * BLK), jnp.bfloat16),
            pltpu.VMEM((NPAIR, 2 * BLK, QN), jnp.float32),
            pltpu.VMEM((8, 128), jnp.bfloat16),
            pltpu.VMEM((NPAIR, 2 * BLK, HD), jnp.float32),
            pltpu.VMEM((NPAIR, 2 * BLK, HD), jnp.float32),
        ],
        compiler_params=pltpu.CompilerParams(vmem_limit_bytes=56 << 20),
    )(info, q, g, own, pool, within)
    grad = grad.reshape(4, 8, NBL, 2, 2, BLK // 2, HD)
    y_groups = [[y * 8 + z for y in range(4)] for z in range(8)]
    z_groups = [[y * 8 + z for z in range(8)] for y in range(4)]
    grad = lax.psum_scatter(grad, "ctx", scatter_dimension=1, axis_index_groups=z_groups, tiled=False)
    grad = lax.psum_scatter(grad, "ctx", scatter_dimension=0, axis_index_groups=y_groups, tiled=False)
    grad = grad.reshape(groups, 2, BLK // 2, HD)
    grad = lax.all_to_all(grad, "head", split_axis=0, concat_axis=0, tiled=True)
    grad = grad.transpose(1, 2, 0, 3)
    o = lax.all_to_all(o, "head", split_axis=0, concat_axis=1, tiled=True)
    dq = lax.all_to_all(dq, "head", split_axis=0, concat_axis=1, tiled=True)
    shape = queries.shape
    return (o.reshape(shape), dq.reshape(shape), grad[0], grad[1])


def solution(mesh):
    rows = P(("ctx", "head"), None, None)
    return jax.shard_map(
        body,
        mesh=mesh,
        in_specs=(rows, rows, rows, rows, P(), P("ctx", None)),
        out_specs=(rows, rows, rows, rows),
        check_vma=False,
    )
```

time: 1160 us -> 407 us (0.35)
  waiting for transfers between devices: 909 us -> 297 us
  local copies, waits for them, and re-layouts: 81.2 us -> 16.9 us
  other arithmetic: 48.8 us -> 4.24 us
  matrix products: 35.8 us -> 2 us
  starting transfers between devices: 45 us -> 13.1 us
  blocking collectives: 11.6 us -> 42.6 us
  Pallas kernels: 0 us -> 15.4 us
    reduce_scatter x2 -> x1, waiting for transfers between devices: 780 us -> 0.01 us  [body(): lax.psum_scatter(grad, 'ctx', scatter_dimension=0, axis_index_groups=y_gr...]
    unnamed x4, waiting for transfers between devices: 0.77 us -> 218 us
    gather x15 -> x0, local copies, waits for them, and re-layouts: 41.4 us -> none  [fetch(): return (pool_keys[chosen], pool_values[chosen], seen, chosen)]
    dot_general x34 -> x4, matrix products: 35.8 us -> 2 us  [tree_reach_t(): jnp.einsum('bts,bsu->btu', reached, reached, preferred_element_type=jnp.f...]
    all_to_all x7 -> x3, starting transfers between devices: 44.9 us -> 13 us  [the longest x1 4.48 us: body(): lax.all_to_all(queries.reshape(tokens, -1), 'head', split_axis=1, concat_...]
    all_to_all x1 -> x3, blocking collectives: 11.6 us -> 42.6 us  [the longest x1 15.7 us: body(): o = lax.all_to_all(o, 'head', split_axis=0, concat_axis=1, tiled=True)]
    all_gather x2 -> x1, waiting for transfers between devices: 93.7 us -> 65.8 us  [body(): pool = lax.all_gather(own, 'ctx', axis=0, tiled=True)]
    all_to_all x7 -> x3, waiting for transfers between devices: 33.8 us -> 13.2 us  [the longest x1 8.99 us: body(): lax.all_to_all(out_grad.reshape(tokens, -1), 'head', split_axis=1, concat...]
  transfers between devices with their start and end apart: 11 -> 6, of which waited for: 9 -> 5; matrix products, arithmetic and copies ran while one was open for 4% -> 4% of each run, Pallas kernels for 0% -> 0%
where the time goes in v1:
time: 407 us; the launch traced here: 405 us
  waiting for transfers between devices  297 us (73%)
  blocking collectives  42.6 us (10%)
  local copies, waits for them, and re-layouts  16.9 us (4%)
  Pallas kernels  15.4 us (4%)
  between operations  14.5 us (4%)
  starting transfers between devices  13.1 us (3%)
  other arithmetic  4.24 us (1%)
    unnamed x4, waiting for transfers between devices  218 us
    all_gather x1, waiting for transfers between devices, body(): pool = lax.all_gather(own, 'ctx', axis=0, tiled=True)  65.8 us
    all_to_all x1, blocking collectives, body(): o = lax.all_to_all(o, 'head', split_axis=0, concat_axis=1, tiled=True)  15.7 us
    pallas_call x1, Pallas kernels, body(): pl.pallas_call(kernel, out_shape=(jax.ShapeDtypeStruct(q.shape, jnp.bfloa...  15.4 us
    all_to_all x1, blocking collectives, body(): dq = lax.all_to_all(dq, 'head', split_axis=0, concat_axis=1, tiled=True)  14.1 us
    all_to_all x1, blocking collectives, body(): kv = lax.all_to_all(kv, 'head', split_axis=0, concat_axis=0, tiled=True)  12.8 us
    all_to_all x1, waiting for transfers between devices, body(): lax.all_to_all(out_grad.reshape(tokens, -1), 'head', split_axis=1, concat...  8.99 us
  transfers between devices with their start and end apart: 6, of which 5 were waited for; matrix products, arithmetic and copies ran while one was open for 4% of the time, Pallas kernels for 0%

profile of v1, /device:TPU:1, one launch (start us, length us, event | category | flops | bytes accessed | tf_op | source)
XLA Modules:
  0.0 405.3 jit_solution(12340229155727916427)
XLA Ops:
  7.2 0.0 copy-start
  7.2 0.0 copy-start.5
  7.2 0.0 all-gather.2.cloned.1.call-start
  7.2 1.0 copy_bitcast_fusion
  8.3 12.8 %all_to_all.80 = bf16[8,2,64,128]{3,2,1,0:T(8,128)(2,1)} all-to-all(bf16[8,2,64,128]{3,2,1,0:T(8,128)(2,1)S(1)} %maximum_bitcast_fusion), channel_id=1, replica_groups=mesh['ctx'=32,'head'=8] {'head'}, dimensions={0} | all-to-all | bytes 524288 | tf_op jit(solution)/shard_map/all_to_all | solution.py:186
  21.1 0.0 all-gather.2.cloned.1.call-update
  21.1 1.6 all_to_all.58
  22.7 0.9 copy.30
  23.6 4.5 %all-to-all-start = ((bf16[64,8,640]{2,0,1:T(8,128)(2,1)}), bf16[64,8,640]{2,0,1:T(8,128)(2,1)S(1)}, u32[]{:S(2)}, u32[]{:S(2)}) async-start(bf16[64,8,640]{2,0,1:T(8,128)(2,1)} %copy.30), calls=%async_computation | async-start | bytes 1310720 | tf_op jit(solution)/shard_map/all_to_all | solution.py:189
  28.1 0.0 copy-done
  28.1 0.1 constant_dynamic-slice_fusion.1
  28.2 0.1 copy.40
  28.3 0.7 slice.48
  28.9 0.6 compare_reduce_fusion.2
  29.6 0.1 convert_reduce_fusion
  30.3 0.1 copy.29
  30.4 0.2 compare_reduce_fusion
  30.7 1.6 all_to_all.62
  32.3 0.9 copy.31
  33.2 0.6 compare_reduce_fusion.1
  33.8 1.9 fusion.21
  35.7 1.4 scatter.9
  37.2 0.0 copy-done.5
  37.2 0.4 fusion.1
  37.6 0.4 fusion.3
  38.0 1.1 all-to-all-done
  39.0 0.0 copy-start.1
  39.0 4.3 %all-to-all-start.1 = ((bf16[64,8,640]{2,0,1:T(8,128)(2,1)}), bf16[64,8,640]{2,0,1:T(8,128)(2,1)S(1)}, u32[]{:S(2)}, u32[]{:S(2)}) async-start(bf16[64,8,640]{2,0,1:T(8,128)(2,1)} %copy.31), calls=%async_computation.1 | async-start | bytes 1310720 | tf_op jit(solution)/shard_map/all_to_all | solution.py:190
  43.3 0.0 all-reduce.4.cloned.1.call-start
  43.3 0.7 add_add_fusion.info_ref
  44.0 0.4 fusion.5
  44.4 0.9 fusion.7.within_ref
  45.2 9.0 %all-to-all-done.1 = bf16[64,8,640]{2,0,1:T(8,128)(2,1)S(1)} async-done(((bf16[64,8,640]{2,0,1:T(8,128)(2,1)}), bf16[64,8,640]{2,0,1:T(8,128)(2,1)S(1)}, u32[]{:S(2)}, u32[]{:S(2)}) %all-to-all-start.1) | async-done | bytes 655392 | tf_op jit(solution)/shard_map/all_to_all | solution.py:190
  54.2 0.0 copy-start.2
  54.2 65.8 %all-gather.2.cloned.1.call-done.pool_ref = bf16[128,2,2,64,128]{4,3,2,1,0:T(8,128)(2,1)} async-done(((bf16[4,2,2,64,128]{4,3,2,1,0:T(8,128)(2,1)}), bf16[128,2,2,64,128]{4,3,2,1,0:T(8,128)(2,1)}) %all-gather.2.cloned.1.call-update) | async-done | bytes 8388624 | tf_op jit(solution)/shard_map/all_gather | solution.py:188
  120.1 0.0 copy-done.1
  120.1 0.0 copy-done.2
  120.1 0.0 copy-start.6
  120.1 15.4 %shard_map.93 = (bf16[512,640]{1,0:T(8,128)(2,1)}, bf16[512,640]{1,0:T(8,128)(2,1)}, bf16[128,2,2,64,128]{4,3,2,1,0:T(8,128)(2,1)}) custom-call(s32[6,16]{1,0:T(8,128)} %add_add_fusion.info_ref, bf16[512,640]{1,0:T(8,128)(2,1)} %bitcast.47, bf16[512,640]{1,0:T(8,128)(2,1)} %bitcast.48, bf16[4,2,2,64,128]{4,3,2,1,0:T(8,128)(2,1)} %bitcast.52, ...), custom_call_target="tpu_custom_call" | custom-call | tf_op jit(solution)/shard_map/pallas_call | solution.py:195
  135.4 0.0 copy-start.4
  135.5 0.0 copy-start.3
  135.5 0.0 all-reduce.4.cloned.1.call-update
  135.5 0.0 reduce-scatter.5.cloned.1.call-start
  135.5 0.0 copy-done.6
  135.5 0.6 dynamic-slice.16
  136.1 217.5 %all-reduce.4.cloned.1.call-done = bf16[4,8,4,2,2,64,128]{6,5,4,3,2,1,0:T(8,128)(2,1)} async-done(((bf16[4,8,4,2,2,64,128]{6,5,4,3,2,1,0:T(8,128)(2,1)}), bf16[4,8,4,2,2,64,128]{6,5,4,3,2,1,0:T(8,128)(2,1)}) %all-reduce.4.cloned.1.call-update) | async-done | bytes 8388624
  353.6 3.0 dynamic-slice_bitcast_fusion
  356.6 0.0 reduce-scatter.5.cloned.1.call-update
  356.7 0.0 copy-done.4
  356.7 15.7 %all_to_all.81 = bf16[8,64,640]{2,1,0:T(8,128)(2,1)S(1)} all-to-all(bf16[8,64,640]{2,1,0:T(8,128)(2,1)S(1)} %bitcast.55), channel_id=1, replica_groups=mesh['ctx'=32,'head'=8] {'head'}, dimensions={0} | all-to-all | bytes 1310720 | tf_op jit(solution)/shard_map/all_to_all | solution.py:224
  372.4 0.0 copy-done.3
  372.4 14.1 %all_to_all.82 = bf16[8,64,640]{2,1,0:T(8,128)(2,1)S(1)} all-to-all(bf16[8,64,640]{2,1,0:T(8,128)(2,1)S(1)} %bitcast.54), channel_id=1, replica_groups=mesh['ctx'=32,'head'=8] {'head'}, dimensions={0} | all-to-all | bytes 1310720 | tf_op jit(solution)/shard_map/all_to_all | solution.py:225
  386.5 0.0 reduce-scatter.5.cloned.1.call-done
  386.5 4.2 %all-to-all-start.5 = ((bf16[8,2,64,128]{3,2,1,0:T(8,128)(2,1)}), bf16[8,2,64,128]{3,2,1,0:T(8,128)(2,1)S(1)}, u32[]{:S(2)}, u32[]{:S(2)}) async-start(bf16[8,2,64,128]{3,2,1,0:T(8,128)(2,1)} %bitcast.56), calls=%async_computation.6 | async-start | bytes 524288 | tf_op jit(solution)/shard_map/all_to_all | solution.py:222
  390.7 0.4 copy.34
  391.1 1.3 reshape.121
  392.4 0.4 copy.35
  392.8 1.3 reshape.122
  394.1 3.2 all-to-all-done.5
  397.2 0.7 copy.36
  398.0 0.7 copy.37
  (9 shorter events, 0.1 us)
Async XLA Ops:
  7.2 20.9 %copy-start = (s32[128,16]{0,1:T(8,128)S(1)}, s32[128,16]{0,1:T(8,128)}, u32[]{:S(2)}) copy-start(s32[128,16]{0,1:T(8,128)} %param.14) | copy-start | bytes 24580
  7.2 30.0 %copy-start.5 = (s32[4,128]{1,0:T(4,128)S(1)}, s32[4,128]{1,0:T(4,128)}, u32[]{:S(2)}) copy-start(s32[4,128]{1,0:T(4,128)} %param.15) | copy-start | bytes 6148
  7.2 112.9 %all-gather.2.cloned.1.call-start = ((), (), s32[]{:S(2)}) async-start(), calls=%async_computation.7 | async-start | bytes 8650752 | tf_op jit(solution)/shard_map/all_gather | solution.py:188
  23.6 15.4 %all-to-all-start = ((bf16[64,8,640]{2,0,1:T(8,128)(2,1)}), bf16[64,8,640]{2,0,1:T(8,128)(2,1)S(1)}, u32[]{:S(2)}, u32[]{:S(2)}) async-start(bf16[64,8,640]{2,0,1:T(8,128)(2,1)} %copy.30), calls=%async_computation | async-start | bytes 1310720 | tf_op jit(solution)/shard_map/all_to_all | solution.py:189
  39.0 81.1 %copy-start.1 = (bf16[64,8,640]{2,0,1:T(8,128)(2,1)}, bf16[64,8,640]{2,0,1:T(8,128)(2,1)S(1)}, u32[]{:S(2)}) copy-start(bf16[64,8,640]{2,0,1:T(8,128)(2,1)S(1)} %all-to-all-done) | copy-start | bytes 1966084
  39.0 15.2 %all-to-all-start.1 = ((bf16[64,8,640]{2,0,1:T(8,128)(2,1)}), bf16[64,8,640]{2,0,1:T(8,128)(2,1)S(1)}, u32[]{:S(2)}, u32[]{:S(2)}) async-start(bf16[64,8,640]{2,0,1:T(8,128)(2,1)} %copy.31), calls=%async_computation.1 | async-start | bytes 1310720 | tf_op jit(solution)/shard_map/all_to_all | solution.py:190
  43.3 310.3 %all-reduce.4.cloned.1.call-start = ((), (), s32[]{:S(2)}) async-start(), calls=%async_computation.9 | async-start | bytes 16777216
  54.2 65.9 %copy-start.2 = (bf16[64,8,640]{2,0,1:T(8,128)(2,1)}, bf16[64,8,640]{2,0,1:T(8,128)(2,1)S(1)}, u32[]{:S(2)}) copy-start(bf16[64,8,640]{2,0,1:T(8,128)(2,1)S(1)} %all-to-all-done.1) | copy-start | bytes 1966084
  120.1 15.4 %copy-start.6 = (u32[256]{0:T(256)S(1)}, u32[256]{0:T(256)}, u32[]{:S(2)}) copy-start(u32[256]{0:T(256)} %constant.80) | copy-start | bytes 3076
  135.4 221.2 %copy-start.4 = (bf16[512,640]{1,0:T(8,128)(2,1)S(1)}, bf16[512,640]{1,0:T(8,128)(2,1)}, u32[]{:S(2)}) copy-start(bf16[512,640]{1,0:T(8,128)(2,1)} %get-tuple-element.31) | copy-start | bytes 1966084
  135.5 236.9 %copy-start.3 = (bf16[512,640]{1,0:T(8,128)(2,1)S(1)}, bf16[512,640]{1,0:T(8,128)(2,1)}, u32[]{:S(2)}) copy-start(bf16[512,640]{1,0:T(8,128)(2,1)} %get-tuple-element.32) | copy-start | bytes 1966084
  135.5 251.0 %reduce-scatter.5.cloned.1.call-start = ((), (), s32[]{:S(2)}) async-start(), calls=%async_computation.8 | async-start | bytes 1310720 | tf_op jit(solution)/shard_map/reduce_scatter | solution.py:220
  386.5 10.7 %all-to-all-start.5 = ((bf16[8,2,64,128]{3,2,1,0:T(8,128)(2,1)}), bf16[8,2,64,128]{3,2,1,0:T(8,128)(2,1)S(1)}, u32[]{:S(2)}, u32[]{:S(2)}) async-start(bf16[8,2,64,128]{3,2,1,0:T(8,128)(2,1)} %bitcast.56), calls=%async_computation.6 | async-start | bytes 524288 | tf_op jit(solution)/shard_map/all_to_all | solution.py:222
Sparse Core Ops, SparseCore 0:
  21.2 98.8 all-gather.1
  135.6 217.9 all-reduce.3
  356.8 22.7 reduce-scatter.4

commit v2 on v1

--- a/solution.py
+++ b/solution.py
@@ -5,7 +5,7 @@
 from jax import lax
 from jax.experimental import pallas as pl
 from jax.experimental.pallas import tpu as pltpu
-from jax.sharding import Mesh, PartitionSpec as P
+from jax.sharding import PartitionSpec as P
 
 HD = 128
 GROUP = 5
@@ -36,15 +36,18 @@
 
 
 def kernel(
-    info_ref, q_ref, g_ref, own_ref, pool_ref, within_ref,
-    o_ref, dq_ref, grad_ref,
-    k_s, v_s, kt_s, vt_s, s_s, w_s, dk_s, dv_s,
+    info_ref, q_ref, g_ref, own_ref, row_ref, cross_ref, within_ref,
+    o_ref, dq_ref, row_grad_ref, cross_grad_ref,
+    k_s, v_s, kt_s, vt_s, s_s, dk_s, dv_s,
 ):
-    grad_ref[...] = jnp.zeros_like(grad_ref)
+    row_grad_ref[...] = jnp.zeros_like(row_grad_ref)
+    cross_grad_ref[...] = jnp.zeros_like(cross_grad_ref)
     dk_s[...] = jnp.zeros_like(dk_s)
     dv_s[...] = jnp.zeros_like(dv_s)
     remote = info_ref[0, 0]
     pairs = (remote + 1) // 2
+    row_first = info_ref[0, 2]
+    crossing = info_ref[0, 3]
 
     def take(p, half, kv):
         k = kv[:, 0].reshape(BLK, HD)
@@ -59,8 +62,16 @@
 
     def load_pair(p, carry):
         for half in range(2):
-            block = info_ref[1, 2 * p + half]
-            take(p, half, pool_ref[block])
+            slot = 2 * p + half
+
+            @pl.when(slot < crossing)
+            def _():
+                take(p, half, cross_ref[slot])
+
+            @pl.when(slot >= crossing)
+            def _():
+                take(p, half, row_ref[jnp.maximum(info_ref[1, slot] - row_first, 0)])
+
         return carry
 
     lax.fori_loop(0, pairs, load_pair, 0)
@@ -145,84 +156,177 @@
         for r in range(GROUP):
             dq_ref[rows, r * HD:(r + 1) * HD] = dqt[:, r * BLK:(r + 1) * BLK].T
 
-    def put(block, p, half):
+    def put(out_ref, place, p, half):
         dk = dk_s[p, pl.ds(half * BLK, BLK), :] * SCALE
         dv = dv_s[p, pl.ds(half * BLK, BLK), :]
-        grad_ref[block, :, 0] = dk.astype(jnp.bfloat16).reshape(2, BLK // 2, HD)
-        grad_ref[block, :, 1] = dv.astype(jnp.bfloat16).reshape(2, BLK // 2, HD)
+        out_ref[place, :, 0] = dk.astype(jnp.bfloat16).reshape(2, BLK // 2, HD)
+        out_ref[place, :, 1] = dv.astype(jnp.bfloat16).reshape(2, BLK // 2, HD)
 
     for j in range(NBL):
-        put(info_ref[0, 1] + j, OWNP + j // 2, j % 2)
+        put(row_grad_ref, info_ref[0, 1] - row_first + j, OWNP + j // 2, j % 2)
 
     def put_pair(p, carry):
-        put(info_ref[1, 2 * p], p, 0)
-
-        @pl.when(2 * p + 1 < remote)
-        def _():
-            put(info_ref[1, 2 * p + 1], p, 1)
+        for half in range(2):
+            slot = 2 * p + half
+
+            @pl.when(slot < crossing)
+            def _():
+                put(cross_grad_ref, slot, p, half)
+
+            @pl.when((slot >= crossing) & (slot < remote))
+            def _():
+                put(row_grad_ref, jnp.maximum(info_ref[1, slot] - row_first, 0), p, half)
 
         return carry
 
     lax.fori_loop(0, pairs, put_pair, 0)
 
 
-def info_of(ancestors):
-    first = lax.axis_index("ctx") * NBL
+def pick_kernel(index_ref, from_ref, out_ref):
+    out_ref[...] = from_ref[...]
+
+
+def pick(index, pool):
+    count = index.shape[0]
+    block = (1,) + pool.shape[1:]
+    return pl.pallas_call(
+        pick_kernel,
+        out_shape=jax.ShapeDtypeStruct((count,) + pool.shape[1:], pool.dtype),
+        grid_spec=pltpu.PrefetchScalarGridSpec(
+            num_scalar_prefetch=1,
+            grid=(count,),
+            in_specs=[pl.BlockSpec(block, lambda i, index_ref: (index_ref[i], 0, 0, 0, 0))],
+            out_specs=pl.BlockSpec(block, lambda i, index_ref: (i, 0, 0, 0, 0)),
+        ),
+    )(index, pool)
+
+
+def merge_kernel(place_ref, valid_ref, row_ref, *rest):
+    parts, out_ref = rest[:-1], rest[-1]
+    out_ref[...] = row_ref[...]
+    for k, part in enumerate(parts):
+        for s in range(part.shape[0]):
+            at = k * part.shape[0] + s
+
+            @pl.when(valid_ref[at] > 0)
+            def _():
+                place = place_ref[at]
+                both = out_ref[place].astype(jnp.float32) + part[s].astype(jnp.float32)
+                out_ref[place] = both.astype(jnp.bfloat16)
+
+
+YN = 4
+ZN = 8
+ROW = ZN * NBL
+SLOTS = MAXD // ZN
+Z_GROUPS = [[y * ZN + z for z in range(ZN)] for y in range(YN)]
+
+
+def up(x, k):
+    pairs = [(y * ZN + z, (y + k) * ZN + z) for y in range(YN - k) for z in range(ZN)]
+    return lax.ppermute(x, "ctx", pairs)
+
+
+def down(x, k):
+    pairs = [((y + k) * ZN + z, y * ZN + z) for y in range(YN - k) for z in range(ZN)]
+    return lax.ppermute(x, "ctx", pairs)
+
+
+def info_of(ancestors, c, y):
+    first = c * NBL
+    row_first = y * ROW
     lists = lax.dynamic_slice_in_dim(ancestors, first, NBL, 0)
     remote = jnp.sum(((lists >= 0) & (lists < first)).astype(jnp.int32), axis=1)
+    crossing = jnp.sum(((lists[0] >= 0) & (lists[0] < row_first)).astype(jnp.int32))
     own = first + jnp.arange(NBL, dtype=jnp.int32)
     flags = jnp.any(lists[:, None, :] == own[None, :, None], axis=2).astype(jnp.int32)
-    width = MAXD
-    head = jnp.zeros((1, width), jnp.int32).at[0, 0].set(remote[0]).at[0, 1].set(first)
-    slots = jnp.maximum(lists[:1], 0)
-    rest = jnp.concatenate([remote[:, None], flags, jnp.zeros((NBL, width - 1 - NBL), jnp.int32)], axis=1)
-    return jnp.concatenate([head, slots, rest], axis=0)
+    head = jnp.concatenate(
+        [jnp.stack([remote[0], first, row_first, crossing]), jnp.zeros((MAXD - 4,), jnp.int32)]
+    )[None]
+    rest = jnp.concatenate([remote[:, None], flags, jnp.zeros((NBL, MAXD - 1 - NBL), jnp.int32)], axis=1)
+    return jnp.concatenate([head, lists[:1], rest], axis=0)
 
 
 def body(queries, keys, values, out_grad, ancestors, parents):
     tokens = queries.shape[0]
     groups = keys.shape[1]
+    c = lax.axis_index("ctx")
+    y = c // ZN
+    z = c % ZN
+    row_lists = ancestors[::ROW]
+    slots = lax.dynamic_slice_in_dim(row_lists, z * SLOTS, SLOTS, 1)
+    slot_rows = jnp.where(slots >= 0, slots // ROW, -1)
+    my_rows = lax.dynamic_index_in_dim(slot_rows, y, 0, keepdims=False)
+
     kv = jnp.stack([keys, values]).transpose(2, 0, 1, 3)
     kv = lax.all_to_all(kv, "head", split_axis=0, concat_axis=0, tiled=True)
     own = kv.reshape(NBL, 2, 2, BLK // 2, HD)
-    pool = lax.all_gather(own, "ctx", axis=0, tiled=True)
+    row = lax.all_gather(own, "ctx", axis=0, axis_index_groups=Z_GROUPS, tiled=True)
     q = lax.all_to_all(queries.reshape(tokens, -1), "head", split_axis=1, concat_axis=0, tiled=True)
     g = lax.all_to_all(out_grad.reshape(tokens, -1), "head", split_axis=1, concat_axis=0, tiled=True)
+
+    wanted = jnp.clip(slots[1:] - y * ROW, 0, ROW - 1).reshape(-1)
+    sent = pick(wanted, row).reshape((YN - 1, SLOTS) + own.shape[1:])
+    mine = jnp.zeros((SLOTS,) + own.shape[1:], own.dtype)
+    for k in range(1, YN):
+        part = lax.dynamic_index_in_dim(sent, jnp.clip(y + k - 1, 0, YN - 2), 0, keepdims=False)
+        here = (my_rows == y - k)[:, None, None, None, None]
+        mine = jnp.where(here, up(part, k), mine)
+    cross = lax.all_gather(mine, "ctx", axis=0, axis_index_groups=Z_GROUPS, tiled=True)
+
     within = tree_reach_t(parents)
-    info = info_of(ancestors)
+    info = info_of(ancestors, c, y)
     vmem = pl.BlockSpec(memory_space=pltpu.VMEM)
     smem = pl.BlockSpec(memory_space=pltpu.SMEM)
-    o, dq, grad = pl.pallas_call(
+    o, dq, row_grad, cross_grad = pl.pallas_call(
         kernel,
         out_shape=(
             jax.ShapeDtypeStruct(q.shape, jnp.bfloat16),
             jax.ShapeDtypeStruct(q.shape, jnp.bfloat16),
-            jax.ShapeDtypeStruct(pool.shape, jnp.bfloat16),
+            jax.ShapeDtypeStruct(row.shape, jnp.bfloat16),
+            jax.ShapeDtypeStruct(cross.shape, jnp.bfloat16),
         ),
-        in_specs=[smem] + [vmem] * 5,
-        out_specs=(vmem,) * 3,
+        in_specs=[smem] + [vmem] * 6,
+        out_specs=(vmem,) * 4,
         scratch_shapes=[
             pltpu.VMEM((NPAIR, 2 * BLK, HD), jnp.bfloat16),
             pltpu.VMEM((NPAIR, 2 * BLK, HD), jnp.bfloat16),
             pltpu.VMEM((NPAIR, HD, 2 * BLK), jnp.bfloat16),
             pltpu.VMEM((NPAIR, HD, 2 * BLK), jnp.bfloat16),
             pltpu.VMEM((NPAIR, 2 * BLK, QN), jnp.float32),
-            pltpu.VMEM((8, 128), jnp.bfloat16),
             pltpu.VMEM((NPAIR, 2 * BLK, HD), jnp.float32),
             pltpu.VMEM((NPAIR, 2 * BLK, HD), jnp.float32),
         ],
         compiler_params=pltpu.CompilerParams(vmem_limit_bytes=56 << 20),
-    )(info, q, g, own, pool, within)
-    grad = grad.reshape(4, 8, NBL, 2, 2, BLK // 2, HD)
-    y_groups = [[y * 8 + z for y in range(4)] for z in range(8)]
-    z_groups = [[y * 8 + z for z in range(8)] for y in range(4)]
-    grad = lax.psum_scatter(grad, "ctx", scatter_dimension=1, axis_index_groups=z_groups, tiled=False)
-    grad = lax.psum_scatter(grad, "ctx", scatter_dimension=0, axis_index_groups=y_groups, tiled=False)
+    )(info, q, g, own, row, cross, within)
+
+    cross_grad = lax.psum_scatter(
+        cross_grad, "ctx", scatter_dimension=0, axis_index_groups=Z_GROUPS, tiled=True
+    )
+    o = lax.all_to_all(o, "head", split_axis=0, concat_axis=1, tiled=True)
+    dq = lax.all_to_all(dq, "head", split_axis=0, concat_axis=1, tiled=True)
+    cross_grad, o, dq = lax.optimization_barrier((cross_grad, o, dq))
+    places, valids, parts = [], [], []
+    for k in range(1, YN):
+        parts.append(down(cross_grad, k))
+        above = jnp.minimum(y + k, YN - 1)
+        theirs = lax.dynamic_index_in_dim(slots, above, 0, keepdims=False)
+        valid = (theirs >= 0) & (theirs // ROW == y) & (y + k < YN)
+        places.append(jnp.where(valid, theirs - y * ROW, 0))
+        valids.append(valid.astype(jnp.int32))
+    row_grad = pl.pallas_call(
+        merge_kernel,
+        out_shape=jax.ShapeDtypeStruct(row_grad.shape, row_grad.dtype),
+        in_specs=[smem, smem] + [vmem] * YN,
+        out_specs=vmem,
+        compiler_params=pltpu.CompilerParams(vmem_limit_bytes=24 << 20),
+    )(jnp.concatenate(places), jnp.concatenate(valids), row_grad, *parts)
+    grad = lax.psum_scatter(
+        row_grad, "ctx", scatter_dimension=0, axis_index_groups=Z_GROUPS, tiled=True
+    )
     grad = grad.reshape(groups, 2, BLK // 2, HD)
     grad = lax.all_to_all(grad, "head", split_axis=0, concat_axis=0, tiled=True)
     grad = grad.transpose(1, 2, 0, 3)
-    o = lax.all_to_all(o, "head", split_axis=0, concat_axis=1, tiled=True)
-    dq = lax.all_to_all(dq, "head", split_axis=0, concat_axis=1, tiled=True)
     shape = queries.shape
     return (o.reshape(shape), dq.reshape(shape), grad[0], grad[1])
 

time: 407 us -> 276 us (0.68)
  waiting for transfers between devices: 297 us -> 152 us
  starting transfers between devices: 13.1 us -> 39.1 us
  blocking collectives: 42.6 us -> 32.8 us
  local copies, waits for them, and re-layouts: 16.9 us -> 12 us
    unnamed x4, waiting for transfers between devices: 218 us -> 0.07 us
    reduce_scatter x1 -> x2, waiting for transfers between devices: 0.01 us -> 77.3 us  [the longest x1 43.5 us: body(): lax.psum_scatter(row_grad, 'ctx', scatter_dimension=0, axis_index_groups=...]
    all_gather x1 -> x2, waiting for transfers between devices: 65.8 us -> 38 us  [the longest x1 36.7 us: body(): lax.all_gather(own, 'ctx', axis=0, axis_index_groups=Z_GROUPS, tiled=True)]
    all_to_all x1 -> x0, blocking collectives: 14.1 us -> none  [body(): dq = lax.all_to_all(dq, 'head', split_axis=0, concat_axis=1, tiled=True)]
    ppermute x0 -> x6, starting transfers between devices: none -> 11.6 us  [the longest x3 7.7 us: up(): return lax.ppermute(x, 'ctx', pairs)]
    all_to_all x0 -> x1, waiting for transfers between devices: none -> 9.73 us  [body(): dq = lax.all_to_all(dq, 'head', split_axis=0, concat_axis=1, tiled=True)]
    pallas_call x0 -> x2, Pallas kernels: none -> 6.64 us  [the longest x1 4.52 us: pick(): pl.pallas_call(pick_kernel, out_shape=jax.ShapeDtypeStruct((count,) + poo...]
    ppermute x0 -> x6, waiting for transfers between devices: none -> 6.36 us  [the longest x3 4.68 us: down(): return lax.ppermute(x, 'ctx', pairs)]
  transfers between devices with their start and end apart: 6 -> 14, of which waited for: 5 -> 12; matrix products, arithmetic and copies ran while one was open for 4% -> 4% of each run, Pallas kernels for 0% -> 0%
where the time goes in v2:
time: 276 us; the launch traced here: 273 us
  waiting for transfers between devices  152 us (55%)
  starting transfers between devices  39.1 us (14%)
  blocking collectives  32.8 us (12%)
  Pallas kernels  18.3 us (7%)
  between operations  14 us (5%)
  local copies, waits for them, and re-layouts  12 us (4%)
  other arithmetic  2.99 us (1%)
    reduce_scatter x1, waiting for transfers between devices, body(): lax.psum_scatter(row_grad, 'ctx', scatter_dimension=0, axis_index_groups=...  43.5 us
    all_gather x1, waiting for transfers between devices, body(): lax.all_gather(own, 'ctx', axis=0, axis_index_groups=Z_GROUPS, tiled=True)  36.7 us
    reduce_scatter x1, waiting for transfers between devices, body(): lax.psum_scatter(cross_grad, 'ctx', scatter_dimension=0, axis_index_group...  33.8 us
    all_to_all x1, blocking collectives, body(): o = lax.all_to_all(o, 'head', split_axis=0, concat_axis=1, tiled=True)  20 us
    all_to_all x1, blocking collectives, body(): kv = lax.all_to_all(kv, 'head', split_axis=0, concat_axis=0, tiled=True)  12.8 us
    pallas_call x1, Pallas kernels, body(): pl.pallas_call(kernel, out_shape=(jax.ShapeDtypeStruct(q.shape, jnp.bfloa...  11.7 us
    all_to_all x1, starting transfers between devices, body(): lax.all_to_all(queries.reshape(tokens, -1), 'head', split_axis=1, concat_...  9.9 us
    all_to_all x1, waiting for transfers between devices, body(): dq = lax.all_to_all(dq, 'head', split_axis=0, concat_axis=1, tiled=True)  9.73 us
  transfers between devices with their start and end apart: 14, of which 12 were waited for; matrix products, arithmetic and copies ran while one was open for 4% of the time, Pallas kernels for 0%

profile of v2, /device:TPU:1, one launch (start us, length us, event | category | flops | bytes accessed | tf_op | source)
XLA Modules:
  0.0 272.9 jit_solution(4949767680538012392)
XLA Ops:
  7.2 0.0 all-gather.3.cloned.1.call-start
  7.2 1.0 copy_bitcast_fusion
  8.3 12.8 %all_to_all.86 = bf16[8,2,64,128]{3,2,1,0:T(8,128)(2,1)} all-to-all(bf16[8,2,64,128]{3,2,1,0:T(8,128)(2,1)S(1)} %maximum_bitcast_fusion), channel_id=1, replica_groups=mesh['ctx'=32,'head'=8] {'head'}, dimensions={0} | all-to-all | bytes 524288 | tf_op jit(solution)/shard_map/all_to_all | solution.py:262
  21.1 0.0 all-gather.3.cloned.1.call-update
  21.1 0.0 all-gather.5.cloned.1.call-start
  21.2 0.8 slice.22
  22.0 0.1 subtract_clamp_fusion
  22.1 0.1 copy.43
  22.2 0.6 reshape.83.index_ref
  22.8 36.7 %all-gather.3.cloned.1.call-done.from_ref.row_ref = bf16[32,2,2,64,128]{4,3,2,1,0:T(8,128)(2,1)} async-done(((bf16[4,2,2,64,128]{4,3,2,1,0:T(8,128)(2,1)}), bf16[32,2,2,64,128]{4,3,2,1,0:T(8,128)(2,1)}) %all-gather.3.cloned.1.call-update) | async-done | bytes 2097168 | tf_op jit(solution)/shard_map/all_gather | solution.py:264
  59.5 4.5 %shard_map.93 = bf16[6,2,2,64,128]{4,3,2,1,0:T(8,128)(2,1)} custom-call(s32[6]{0:T(128)} %reshape.83.index_ref, bf16[32,2,2,64,128]{4,3,2,1,0:T(8,128)(2,1)} %all-gather.3.cloned.1.call-done.from_ref.row_ref), custom_call_target="tpu_custom_call" | custom-call | tf_op jit(solution)/shard_map/pallas_call | solution.py:192
  64.1 1.1 dynamic-slice_bitcast_fusion
  65.1 3.1 %collective-permute-start.2 = (bf16[2,2,2,64,128]{4,3,2,1,0:T(8,128)(2,1)S(1)}, bf16[2,2,2,64,128]{4,3,2,1,0:T(8,128)(2,1)S(1)}, u32[]{:S(2)}, u32[]{:S(2)}) collective-permute-start(bf16[2,2,2,64,128]{4,3,2,1,0:T(8,128)(2,1)S(1)} %get-tuple-element.40), channel_id=1, source_target_pairs={{0,64},{8,72},{16,80},{24,88},{32,96},{40,104},{48,112},{56,120},{... | collective-permute-start | bytes 393224 | tf_op jit(solution)/shard_map/ppermute | solution.py:227
  68.3 3.3 %collective-permute-start.1 = (bf16[2,2,2,64,128]{4,3,2,1,0:T(8,128)(2,1)S(1)}, bf16[2,2,2,64,128]{4,3,2,1,0:T(8,128)(2,1)S(1)}, u32[]{:S(2)}, u32[]{:S(2)}) collective-permute-start(bf16[2,2,2,64,128]{4,3,2,1,0:T(8,128)(2,1)S(1)} %get-tuple-element.41), channel_id=1, source_target_pairs={{0,128},{8,136},{16,144},{24,152},{32,160},{40,168},{48,176},{56,1... | collective-permute-start | bytes 393224 | tf_op jit(solution)/shard_map/ppermute | solution.py:227
  71.5 1.3 collective-permute-start
  72.9 0.2 compare_reduce_fusion.3
  73.1 0.4 collective-permute-done.1
  73.5 1.3 collective-permute-done
  74.8 0.7 select_select_fusion
  75.6 0.5 all_to_all.62
  76.0 0.9 copy.39
  77.0 9.9 %all-to-all-start = ((bf16[64,8,640]{2,0,1:T(8,128)(2,1)}), bf16[64,8,640]{2,0,1:T(8,128)(2,1)S(1)}, u32[]{:S(2)}, u32[]{:S(2)}) async-start(bf16[64,8,640]{2,0,1:T(8,128)(2,1)} %copy.39), calls=%async_computation | async-start | bytes 1310720 | tf_op jit(solution)/shard_map/all_to_all | solution.py:265
  86.9 0.1 constant_dynamic-slice_fusion.2
  86.9 0.1 copy.48
  87.0 0.1 convert_reduce_fusion
  87.1 0.1 copy.38
  87.2 0.2 compare_reduce_fusion
  87.5 0.5 all_to_all.66
  88.0 0.9 copy.40
  88.9 0.7 fusion.18
  89.6 0.8 concatenate.17
  90.4 0.4 fusion.1
  90.8 0.4 fusion.3
  91.2 6.6 %all-to-all-done = bf16[64,8,640]{2,0,1:T(8,128)(2,1)S(1)} async-done(((bf16[64,8,640]{2,0,1:T(8,128)(2,1)}), bf16[64,8,640]{2,0,1:T(8,128)(2,1)S(1)}, u32[]{:S(2)}, u32[]{:S(2)}) %all-to-all-start) | async-done | bytes 655392 | tf_op jit(solution)/shard_map/all_to_all | solution.py:265
  97.7 4.3 %all-to-all-start.1 = ((bf16[64,8,640]{2,0,1:T(8,128)(2,1)}), bf16[64,8,640]{2,0,1:T(8,128)(2,1)S(1)}, u32[]{:S(2)}, u32[]{:S(2)}) async-start(bf16[64,8,640]{2,0,1:T(8,128)(2,1)} %copy.40), calls=%async_computation.1 | async-start | bytes 1310720 | tf_op jit(solution)/shard_map/all_to_all | solution.py:266
  102.1 0.7 add_add_fusion.info_ref
  102.7 0.4 fusion.5
  103.1 0.9 fusion.7.within_ref
  104.0 9.0 %all-to-all-done.1 = bf16[64,8,640]{2,0,1:T(8,128)(2,1)S(1)} async-done(((bf16[64,8,640]{2,0,1:T(8,128)(2,1)}), bf16[64,8,640]{2,0,1:T(8,128)(2,1)S(1)}, u32[]{:S(2)}, u32[]{:S(2)}) %all-to-all-start.1) | async-done | bytes 655392 | tf_op jit(solution)/shard_map/all_to_all | solution.py:266
  113.0 1.2 all-gather.5.cloned.1.call-done.cross_ref
  114.2 11.7 %shard_map.94 = (bf16[512,640]{1,0:T(8,128)(2,1)}, bf16[512,640]{1,0:T(8,128)(2,1)}, bf16[32,2,2,64,128]{4,3,2,1,0:T(8,128)(2,1)}, bf16[16,2,2,64,128]{4,3,2,1,0:T(8,128)(2,1)}) custom-call(s32[6,16]{1,0:T(8,128)} %add_add_fusion.info_ref, bf16[512,640]{1,0:T(8,128)(2,1)} %bitcast.54, bf16[512,640]{1,0:T(8,128)(2,1)} %bitcast.55, ...), custom_call_target="tpu_custom_call" | custom-call | tf_op jit(solution)/shard_map/pallas_call | solution.py:281
  125.9 0.0 reduce-scatter.3.cloned.1.call-update
  125.9 20.0 %all_to_all.87 = bf16[8,64,640]{2,1,0:T(8,128)(2,1)S(1)} all-to-all(bf16[8,64,640]{2,1,0:T(8,128)(2,1)} %bitcast.63), channel_id=1, replica_groups=mesh['ctx'=32,'head'=8] {'head'}, dimensions={0} | all-to-all | bytes 1310720 | tf_op jit(solution)/shard_map/all_to_all | solution.py:306
  145.9 4.4 %all-to-all-start.4 = ((bf16[8,64,640]{2,1,0:T(8,128)(2,1)}), bf16[8,64,640]{2,1,0:T(8,128)(2,1)S(1)}, u32[]{:S(2)}, u32[]{:S(2)}) async-start(bf16[8,64,640]{2,1,0:T(8,128)(2,1)} %bitcast.60), calls=%async_computation.5 | async-start | bytes 1310720 | tf_op jit(solution)/shard_map/all_to_all | solution.py:307
  150.4 0.2 dynamic-slice_reduce_fusion.2
  150.6 0.9 copy.49
  151.5 9.7 %all-to-all-done.4 = bf16[8,64,640]{2,1,0:T(8,128)(2,1)S(1)} async-done(((bf16[8,64,640]{2,1,0:T(8,128)(2,1)}), bf16[8,64,640]{2,1,0:T(8,128)(2,1)S(1)}, u32[]{:S(2)}, u32[]{:S(2)}) %all-to-all-start.4) | async-done | bytes 655392 | tf_op jit(solution)/shard_map/all_to_all | solution.py:307
  161.3 0.1 copy.50
  161.3 33.8 %reduce-scatter.3.cloned.1.call-done = bf16[2,2,2,64,128]{4,3,2,1,0:T(8,128)(2,1)} async-done(((bf16[16,2,2,64,128]{4,3,2,1,0:T(8,128)(2,1)}), bf16[2,2,2,64,128]{4,3,2,1,0:T(8,128)(2,1)}) %reduce-scatter.3.cloned.1.call-update) | async-done | bytes 131088 | tf_op jit(solution)/shard_map/reduce_scatter | solution.py:303
  195.2 1.3 collective-permute-start.5
  196.5 1.3 collective-permute-start.4
  197.8 1.3 collective-permute-start.3
  199.1 0.1 add_convert_fusion.valid_ref
  199.1 0.1 pad_add_fusion.place_ref
  199.2 3.1 %collective-permute-done.5.rest_2_ = bf16[2,2,2,64,128]{4,3,2,1,0:T(8,128)(2,1)S(1)} collective-permute-done((bf16[2,2,2,64,128]{4,3,2,1,0:T(8,128)(2,1)}, bf16[2,2,2,64,128]{4,3,2,1,0:T(8,128)(2,1)S(1)}, u32[]{:S(2)}, u32[]{:S(2)}) %collective-permute-start.5) | collective-permute-done | bytes 131104 | tf_op jit(solution)/shard_map/ppermute | solution.py:232
  202.3 1.6 collective-permute-done.4.rest_1_
  203.9 2.1 shard_map.95
  206.0 43.5 %reduce-scatter.5.cloned.1.call-done = bf16[4,2,2,64,128]{4,3,2,1,0:T(8,128)(2,1)} async-done(((bf16[32,2,2,64,128]{4,3,2,1,0:T(8,128)(2,1)}), bf16[4,2,2,64,128]{4,3,2,1,0:T(8,128)(2,1)}) %reduce-scatter.5.cloned.1.call-update) | async-done | bytes 262160 | tf_op jit(solution)/shard_map/reduce_scatter | solution.py:324
  249.5 8.8 %all-to-all-start.5 = ((bf16[8,2,64,128]{3,2,1,0:T(8,128)(2,1)}), bf16[8,2,64,128]{3,2,1,0:T(8,128)(2,1)S(1)}, u32[]{:S(2)}, u32[]{:S(2)}) async-start(bf16[8,2,64,128]{3,2,1,0:T(8,128)(2,1)} %bitcast.64), calls=%async_computation.7 | async-start | bytes 524288 | tf_op jit(solution)/shard_map/all_to_all | solution.py:328
  258.3 0.9 copy.51
  259.3 0.9 copy.52
  260.2 4.6 %all-to-all-done.5 = bf16[8,2,64,128]{3,2,1,0:T(8,128)(2,1)S(1)} async-done(((bf16[8,2,64,128]{3,2,1,0:T(8,128)(2,1)}), bf16[8,2,64,128]{3,2,1,0:T(8,128)(2,1)S(1)}, u32[]{:S(2)}, u32[]{:S(2)}) %all-to-all-start.5) | async-done | bytes 262176 | tf_op jit(solution)/shard_map/all_to_all | solution.py:328
  264.8 0.7 copy.47
  265.6 0.7 copy.46
  (32 shorter events, 0.2 us)
Async XLA Ops:
  7.2 52.4 %all-gather.3.cloned.1.call-start = ((), (), s32[]{:S(2)}) async-start(), calls=%async_computation.8 | async-start | bytes 2359296 | tf_op jit(solution)/shard_map/all_gather | solution.py:264
  21.1 54.5 %copy-start.4 = (bf16[64,40,128]{2,1,0:T(8,128)(2,1)S(1)}, bf16[64,40,128]{2,1,0:T(8,128)(2,1)}, u32[]{:S(2)}) copy-start(bf16[64,40,128]{2,1,0:T(8,128)(2,1)} %param.6) | copy-start | bytes 1966084
  21.1 93.1 %all-gather.5.cloned.1.call-start = ((), (), s32[]{:S(2)}) async-start(), calls=%async_computation.9 | async-start | bytes 1179648 | tf_op jit(solution)/shard_map/all_gather | solution.py:275
  65.1 8.0 %collective-permute-start.2 = (bf16[2,2,2,64,128]{4,3,2,1,0:T(8,128)(2,1)S(1)}, bf16[2,2,2,64,128]{4,3,2,1,0:T(8,128)(2,1)S(1)}, u32[]{:S(2)}, u32[]{:S(2)}) collective-permute-start(bf16[2,2,2,64,128]{4,3,2,1,0:T(8,128)(2,1)S(1)} %get-tuple-element.40), channel_id=1, source_target_pairs={{0,64},{8,72},{16,80},{24,88},{32,96},{40,104},{48,112},{56,120},{... | collective-permute-start | bytes 393224 | tf_op jit(solution)/shard_map/ppermute | solution.py:227
  68.3 5.2 %collective-permute-start.1 = (bf16[2,2,2,64,128]{4,3,2,1,0:T(8,128)(2,1)S(1)}, bf16[2,2,2,64,128]{4,3,2,1,0:T(8,128)(2,1)S(1)}, u32[]{:S(2)}, u32[]{:S(2)}) collective-permute-start(bf16[2,2,2,64,128]{4,3,2,1,0:T(8,128)(2,1)S(1)} %get-tuple-element.41), channel_id=1, source_target_pairs={{0,128},{8,136},{16,144},{24,152},{32,160},{40,168},{48,176},{56,1... | collective-permute-start | bytes 393224 | tf_op jit(solution)/shard_map/ppermute | solution.py:227
  71.5 3.2 %collective-permute-start = (bf16[2,2,2,64,128]{4,3,2,1,0:T(8,128)(2,1)S(1)}, bf16[2,2,2,64,128]{4,3,2,1,0:T(8,128)(2,1)S(1)}, u32[]{:S(2)}, u32[]{:S(2)}) collective-permute-start(bf16[2,2,2,64,128]{4,3,2,1,0:T(8,128)(2,1)S(1)} %get-tuple-element.42), channel_id=1, source_target_pairs={{0,192},{8,200},{16,208},{24,216},{32,224},{40,232},{48,240},{56,2... | collective-permute-start | bytes 393224 | tf_op jit(solution)/shard_map/ppermute | solution.py:227
  75.5 11.3 %copy-start.6 = (s32[128,16]{0,1:T(8,128)S(1)}, s32[128,16]{0,1:T(8,128)}, u32[]{:S(2)}) copy-start(s32[128,16]{0,1:T(8,128)} %param.10) | copy-start | bytes 24580
  75.5 11.9 %copy-start.5 = (bf16[64,40,128]{2,1,0:T(8,128)(2,1)S(1)}, bf16[64,40,128]{2,1,0:T(8,128)(2,1)}, u32[]{:S(2)}) copy-start(bf16[64,40,128]{2,1,0:T(8,128)(2,1)} %param.9) | copy-start | bytes 1966084
  77.0 13.4 %copy-start.7 = (s32[4,128]{1,0:T(4,128)S(1)}, s32[4,128]{1,0:T(4,128)}, u32[]{:S(2)}) copy-start(s32[4,128]{1,0:T(4,128)} %param.11) | copy-start | bytes 6148
  77.0 20.8 %all-to-all-start = ((bf16[64,8,640]{2,0,1:T(8,128)(2,1)}), bf16[64,8,640]{2,0,1:T(8,128)(2,1)S(1)}, u32[]{:S(2)}, u32[]{:S(2)}) async-start(bf16[64,8,640]{2,0,1:T(8,128)(2,1)} %copy.39), calls=%async_computation | async-start | bytes 1310720 | tf_op jit(solution)/shard_map/all_to_all | solution.py:265
  97.7 16.5 %copy-start.2 = (bf16[64,8,640]{2,0,1:T(8,128)(2,1)}, bf16[64,8,640]{2,0,1:T(8,128)(2,1)S(1)}, u32[]{:S(2)}) copy-start(bf16[64,8,640]{2,0,1:T(8,128)(2,1)S(1)} %all-to-all-done) | copy-start | bytes 1966084
  97.7 15.2 %all-to-all-start.1 = ((bf16[64,8,640]{2,0,1:T(8,128)(2,1)}), bf16[64,8,640]{2,0,1:T(8,128)(2,1)S(1)}, u32[]{:S(2)}, u32[]{:S(2)}) async-start(bf16[64,8,640]{2,0,1:T(8,128)(2,1)} %copy.40), calls=%async_computation.1 | async-start | bytes 1310720 | tf_op jit(solution)/shard_map/all_to_all | solution.py:266
  102.1 93.1 %reduce-scatter.3.cloned.1.call-start = ((), (), s32[]{:S(2)}) async-start(), calls=%async_computation.10 | async-start | bytes 1179648 | tf_op jit(solution)/shard_map/reduce_scatter | solution.py:303
  113.0 1.2 copy-start.3
  145.9 58.0 %copy-start = (bf16[32,2,2,64,128]{4,3,2,1,0:T(8,128)(2,1)S(1)}, bf16[32,2,2,64,128]{4,3,2,1,0:T(8,128)(2,1)}, u32[]{:S(2)}) copy-start(bf16[32,2,2,64,128]{4,3,2,1,0:T(8,128)(2,1)} %get-tuple-element.16.row_ref) | copy-start | bytes 6291460
  145.9 15.3 %all-to-all-start.4 = ((bf16[8,64,640]{2,1,0:T(8,128)(2,1)}), bf16[8,64,640]{2,1,0:T(8,128)(2,1)S(1)}, u32[]{:S(2)}, u32[]{:S(2)}) async-start(bf16[8,64,640]{2,1,0:T(8,128)(2,1)} %bitcast.60), calls=%async_computation.5 | async-start | bytes 1310720 | tf_op jit(solution)/shard_map/all_to_all | solution.py:307
  150.4 99.1 %reduce-scatter.5.cloned.1.call-start = ((), (), s32[]{:S(2)}) async-start(), calls=%async_computation.11 | async-start | bytes 2359296 | tf_op jit(solution)/shard_map/reduce_scatter | solution.py:324
  195.2 7.1 %collective-permute-start.5 = (bf16[2,2,2,64,128]{4,3,2,1,0:T(8,128)(2,1)}, bf16[2,2,2,64,128]{4,3,2,1,0:T(8,128)(2,1)S(1)}, u32[]{:S(2)}, u32[]{:S(2)}) collective-permute-start(bf16[2,2,2,64,128]{4,3,2,1,0:T(8,128)(2,1)} %reduce-scatter.3.cloned.1.call-done), channel_id=1, source_target_pairs={{192,0},{200,8},{208,16},{216,24},{224,32},{232,40},{240,48},{248,... | collective-permute-start | bytes 393224 | tf_op jit(solution)/shard_map/ppermute | solution.py:232
  196.5 7.4 %collective-permute-start.4 = (bf16[2,2,2,64,128]{4,3,2,1,0:T(8,128)(2,1)}, bf16[2,2,2,64,128]{4,3,2,1,0:T(8,128)(2,1)S(1)}, u32[]{:S(2)}, u32[]{:S(2)}) collective-permute-start(bf16[2,2,2,64,128]{4,3,2,1,0:T(8,128)(2,1)} %reduce-scatter.3.cloned.1.call-done), channel_id=1, source_target_pairs={{128,0},{136,8},{144,16},{152,24},{160,32},{168,40},{176,48},{184,... | collective-permute-start | bytes 393224 | tf_op jit(solution)/shard_map/ppermute | solution.py:232
  197.8 6.1 %collective-permute-start.3 = (bf16[2,2,2,64,128]{4,3,2,1,0:T(8,128)(2,1)}, bf16[2,2,2,64,128]{4,3,2,1,0:T(8,128)(2,1)S(1)}, u32[]{:S(2)}, u32[]{:S(2)}) collective-permute-start(bf16[2,2,2,64,128]{4,3,2,1,0:T(8,128)(2,1)} %reduce-scatter.3.cloned.1.call-done), channel_id=1, source_target_pairs={{64,0},{72,8},{80,16},{88,24},{96,32},{104,40},{112,48},{120,56},{... | collective-permute-start | bytes 393224 | tf_op jit(solution)/shard_map/ppermute | solution.py:232
  206.0 52.3 %copy-start.1 = (bf16[8,8,8,640]{3,2,0,1:T(8,128)(2,1)S(1)}, bf16[8,8,8,640]{3,2,0,1:T(8,128)(2,1)}, u32[]{:S(2)}) copy-start(bf16[8,8,8,640]{3,2,0,1:T(8,128)(2,1)} %copy.49) | copy-start | bytes 1966084
  249.5 15.3 %all-to-all-start.5 = ((bf16[8,2,64,128]{3,2,1,0:T(8,128)(2,1)}), bf16[8,2,64,128]{3,2,1,0:T(8,128)(2,1)S(1)}, u32[]{:S(2)}, u32[]{:S(2)}) async-start(bf16[8,2,64,128]{3,2,1,0:T(8,128)(2,1)} %bitcast.64), calls=%async_computation.7 | async-start | bytes 524288 | tf_op jit(solution)/shard_map/all_to_all | solution.py:328
Sparse Core Ops, SparseCore 0:
  21.2 38.2 all-gather.2
  75.7 38.4 all-gather.4
  126.0 69.0 reduce-scatter.2
  206.2 43.2 reduce-scatter.4

commit v3 on v2

v3 whole, which is shorter than its diff:
```python
import math

import jax
import jax.numpy as jnp
from jax import lax
from jax.experimental import pallas as pl
from jax.experimental.pallas import tpu as pltpu
from jax.sharding import PartitionSpec as P

HD = 128
GROUP = 5
BLK = 128
NBL = 4
MAXD = 16
QN = GROUP * BLK
SCALE = 1.0 / math.sqrt(HD)
LOG2E = 1.0 / math.log(2.0)
NEG = -1e30
NPAIR = MAXD // 2 + NBL // 2
OWNP = MAXD // 2


def tree_reach_t(parents):
    block_width = parents.shape[-1]
    hops = parents[:, None, :] == jnp.arange(block_width, dtype=jnp.int32)[None, :, None]
    eye = jnp.eye(block_width, dtype=jnp.bool_)[None]
    reached = (hops | eye).astype(jnp.bfloat16)
    for _ in range(max(1, (block_width - 1).bit_length())):
        product = jnp.einsum("bts,bsu->btu", reached, reached, preferred_element_type=jnp.float32)
        reached = jnp.minimum(product, 1.0).astype(jnp.bfloat16)
    return reached.astype(jnp.float32)


def dot(a, b, dims):
    return lax.dot_general(a, b, (dims, ((), ())), preferred_element_type=jnp.float32)


def kernel(
    info_ref, q_ref, g_ref, own_ref, row_ref, mine_ref, next_ref, last_ref, far_ref, near_ref, within_ref,
    o_ref, dq_ref, row_grad_ref, mine_grad_ref, next_grad_ref, last_grad_ref, far_grad_ref, near_grad_ref,
    k_s, v_s, kt_s, vt_s, s_s, dk_s, dv_s, acc_s, cross_s, cross_grad_s,
):
    row_grad_ref[...] = jnp.zeros_like(row_grad_ref)
    cross_grad_s[...] = jnp.zeros_like(cross_grad_s)
    at = 0
    for ref in (mine_ref, next_ref, last_ref, far_ref, near_ref):
        cross_s[at:at + ref.shape[0]] = ref[...]
        at += ref.shape[0]
    dk_s[...] = jnp.zeros_like(dk_s)
    dv_s[...] = jnp.zeros_like(dv_s)
    remote = info_ref[0, 0]
    pairs = (remote + 1) // 2
    row_first = info_ref[0, 2]
    crossing = info_ref[0, 3]

    def place_of(slot):
        return info_ref[6, slot]


    def take(p, half, kv):
        k = kv[:, 0].reshape(BLK, HD)
        v = kv[:, 1].reshape(BLK, HD)
        k_s[p, half * BLK:(half + 1) * BLK, :] = k
        v_s[p, half * BLK:(half + 1) * BLK, :] = v
        kt_s[p, :, half * BLK:(half + 1) * BLK] = k.T
        vt_s[p, :, half * BLK:(half + 1) * BLK] = v.T

    for j in range(NBL):
        take(OWNP + j // 2, j % 2, own_ref[j])

    def load_pair(p, carry):
        for half in range(2):
            slot = 2 * p + half

            @pl.when(slot < crossing)
            def _():
                take(p, half, cross_s[place_of(slot)])

            @pl.when(slot >= crossing)
            def _():
                take(p, half, row_ref[jnp.maximum(info_ref[1, slot] - row_first, 0)])

        return carry

    lax.fori_loop(0, pairs, load_pair, 0)

    row_id = lax.broadcasted_iota(jnp.int32, (2 * BLK, 1), 0)
    wide = 2 * QN

    def fold(x, op):
        return op(x.reshape(-1, 8, x.shape[-1]), axis=0)

    for u in range(NBL // 2):
        lo, hi = 2 * u, 2 * u + 1
        first, second = info_ref[2 + lo, 0], info_ref[2 + hi, 0]
        my_pairs = (first + 1) // 2
        spans = [(i, r) for i in (lo, hi) for r in range(GROUP)]

        def gather(ref):
            return jnp.concatenate(
                [ref[i * BLK:(i + 1) * BLK, r * HD:(r + 1) * HD] for i, r in spans], axis=0
            )

        q = gather(q_ref)
        g = gather(g_ref)
        qt = q.T
        gt = g.T

        def scores(p, mx):
            raw = dot(k_s[p], qt, ((1,), (0,))) * (SCALE * LOG2E)
            bias = [jnp.where(row_id + 2 * BLK * p < BLK * n, 0.0, NEG) for n in (first, second)]
            s = jnp.concatenate([raw[:, :QN] + bias[0], raw[:, QN:] + bias[1]], axis=1)
            s_s[p] = s
            return jnp.maximum(mx, fold(s, jnp.max))

        mx = lax.fori_loop(0, my_pairs, scores, jnp.full((8, wide), NEG, jnp.float32))
        for op in range(u + 1):
            raw = dot(k_s[OWNP + op], qt, ((1,), (0,))) * (SCALE * LOG2E)
            parts = []
            for half in range(2):
                j = 2 * op + half
                pieces = []
                for at, i in enumerate((lo, hi)):
                    piece = raw[half * BLK:(half + 1) * BLK, at * QN:(at + 1) * QN]
                    if j < i:
                        piece = piece + jnp.where(info_ref[2 + i, 1 + j] > 0, 0.0, NEG)
                    elif j == i:
                        bias = jnp.where(within_ref[i] > 0.5, 0.0, NEG)
                        piece = piece + jnp.concatenate([bias] * GROUP, axis=1)
                    else:
                        piece = jnp.full_like(piece, NEG)
                    pieces.append(piece)
                parts.append(jnp.concatenate(pieces, axis=1))
            s = jnp.concatenate(parts, axis=0)
            s_s[OWNP + op] = s
            mx = jnp.maximum(mx, fold(s, jnp.max))
        m = jnp.max(mx, axis=0, keepdims=True)

        def expo(p, total):
            e = jnp.exp2(s_s[p] - m)
            s_s[p] = e
            return total + fold(e, jnp.sum)

        total = lax.fori_loop(0, my_pairs, expo, jnp.zeros((8, wide), jnp.float32))
        for op in range(u + 1):
            total = expo(OWNP + op, total)
        inv = 1.0 / jnp.sum(total, axis=0, keepdims=True)

        def attend(p, acc):
            prob = s_s[p] * inv
            s_s[p] = prob
            w = prob.astype(jnp.bfloat16)
            dv_s[p] += dot(w, g, ((1,), (0,)))
            acc_s[...] += dot(vt_s[p], w, ((1,), (0,)))
            return acc

        acc_s[...] = jnp.zeros_like(acc_s)
        lax.fori_loop(0, my_pairs, attend, 0)
        for op in range(u + 1):
            attend(OWNP + op, 0)
        acc = acc_s[...]
        ot = acc.astype(jnp.bfloat16)
        delta = jnp.sum(gt.astype(jnp.float32) * ot.astype(jnp.float32), axis=0, keepdims=True)
        for at, (i, r) in enumerate(spans):
            o_ref[i * BLK:(i + 1) * BLK, r * HD:(r + 1) * HD] = ot[:, at * BLK:(at + 1) * BLK].T

        def back(p, acc):
            dprob = dot(v_s[p], gt, ((1,), (0,)))
            ds = (s_s[p] * (dprob - delta)).astype(jnp.bfloat16)
            dk_s[p] += dot(ds, q, ((1,), (0,)))
            acc_s[...] += dot(kt_s[p], ds, ((1,), (0,)))
            return acc

        acc_s[...] = jnp.zeros_like(acc_s)
        lax.fori_loop(0, my_pairs, back, 0)
        for op in range(u + 1):
            back(OWNP + op, 0)
        acc = acc_s[...]
        dqt = (acc * SCALE).astype(jnp.bfloat16)
        for at, (i, r) in enumerate(spans):
            dq_ref[i * BLK:(i + 1) * BLK, r * HD:(r + 1) * HD] = dqt[:, at * BLK:(at + 1) * BLK].T

    def put(out_ref, place, p, half):
        dk = dk_s[p, pl.ds(half * BLK, BLK), :] * SCALE
        dv = dv_s[p, pl.ds(half * BLK, BLK), :]
        out_ref[place, :, 0] = dk.astype(jnp.bfloat16).reshape(2, BLK // 2, HD)
        out_ref[place, :, 1] = dv.astype(jnp.bfloat16).reshape(2, BLK // 2, HD)

    for j in range(NBL):
        put(row_grad_ref, info_ref[0, 1] - row_first + j, OWNP + j // 2, j % 2)

    def put_pair(p, carry):
        for half in range(2):
            slot = 2 * p + half

            @pl.when(slot < crossing)
            def _():
                put(cross_grad_s, place_of(slot), p, half)

            @pl.when((slot >= crossing) & (slot < remote))
            def _():
                put(row_grad_ref, jnp.maximum(info_ref[1, slot] - row_first, 0), p, half)

        return carry

    lax.fori_loop(0, pairs, put_pair, 0)
    at = 0
    for ref in (mine_grad_ref, next_grad_ref, last_grad_ref, far_grad_ref, near_grad_ref):
        ref[...] = cross_grad_s[at:at + ref.shape[0]]
        at += ref.shape[0]


def attention(info, q, g, own, row, cross, within):
    vmem = pl.BlockSpec(memory_space=pltpu.VMEM)
    smem = pl.BlockSpec(memory_space=pltpu.SMEM)
    like = [jax.ShapeDtypeStruct(a.shape, jnp.bfloat16) for a in (q, q, row, *cross)]
    return pl.pallas_call(
        kernel,
        out_shape=tuple(like),
        in_specs=[smem] + [vmem] * (5 + len(cross)),
        out_specs=(vmem,) * len(like),
        scratch_shapes=[
            pltpu.VMEM((NPAIR, 2 * BLK, HD), jnp.bfloat16),
            pltpu.VMEM((NPAIR, 2 * BLK, HD), jnp.bfloat16),
            pltpu.VMEM((NPAIR, HD, 2 * BLK), jnp.bfloat16),
            pltpu.VMEM((NPAIR, HD, 2 * BLK), jnp.bfloat16),
            pltpu.VMEM((NPAIR, 2 * BLK, 2 * QN), jnp.float32),
            pltpu.VMEM((NPAIR, 2 * BLK, HD), jnp.float32),
            pltpu.VMEM((NPAIR, 2 * BLK, HD), jnp.float32),
            pltpu.VMEM((HD, 2 * QN), jnp.float32),
            pltpu.VMEM((MAXD,) + own.shape[1:], jnp.bfloat16),
            pltpu.VMEM((MAXD,) + own.shape[1:], jnp.bfloat16),
        ],
        compiler_params=pltpu.CompilerParams(vmem_limit_bytes=56 << 20),
    )(info, q, g, own, row, *cross, within)


def pick_kernel(index_ref, from_ref, *outs):
    for k, out in enumerate(outs):
        for s in range(out.shape[0]):
            out[s] = from_ref[index_ref[k * out.shape[0] + s]]


def pick(index, pool, parts):
    vmem = pl.BlockSpec(memory_space=pltpu.VMEM)
    size = index.shape[0] // parts
    return pl.pallas_call(
        pick_kernel,
        out_shape=(jax.ShapeDtypeStruct((size,) + pool.shape[1:], pool.dtype),) * parts,
        in_specs=[pl.BlockSpec(memory_space=pltpu.SMEM), vmem],
        out_specs=(vmem,) * parts,
        compiler_params=pltpu.CompilerParams(vmem_limit_bytes=24 << 20),
    )(index, pool)


def merge_kernel(place_ref, valid_ref, row_ref, *rest):
    parts, out_ref = rest[:-1], rest[-1]
    out_ref[...] = row_ref[...]
    for k, part in enumerate(parts):
        for s in range(part.shape[0]):
            at = k * part.shape[0] + s

            @pl.when(valid_ref[at] > 0)
            def _():
                place = place_ref[at]
                both = out_ref[place].astype(jnp.float32) + part[s].astype(jnp.float32)
                out_ref[place] = both.astype(jnp.bfloat16)


YN = 4
ZN = 8
ROW = ZN * NBL
SETS = 4
SLOTS = MAXD // SETS
Z_GROUPS = [[y * ZN + z for z in range(ZN)] for y in range(YN)]


def along(x, k):
    pairs = [(y * ZN + z, y * ZN + (z + k) % ZN) for y in range(YN) for z in range(ZN)]
    return lax.ppermute(x, "ctx", pairs)


def up(x, k):
    pairs = [(y * ZN + z, (y + k) * ZN + z) for y in range(YN - k) for z in range(ZN)]
    return lax.ppermute(x, "ctx", pairs)


def down(x, k):
    pairs = [((y + k) * ZN + z, y * ZN + z) for y in range(YN - k) for z in range(ZN)]
    return lax.ppermute(x, "ctx", pairs)


def info_of(ancestors, c, y, z):
    first = c * NBL
    row_first = y * ROW
    lists = lax.dynamic_slice_in_dim(ancestors, first, NBL, 0)
    remote = jnp.sum(((lists >= 0) & (lists < first)).astype(jnp.int32), axis=1)
    crossing = jnp.sum(((lists[0] >= 0) & (lists[0] < row_first)).astype(jnp.int32))
    own = first + jnp.arange(NBL, dtype=jnp.int32)
    flags = jnp.any(lists[:, None, :] == own[None, :, None], axis=2).astype(jnp.int32)
    head = jnp.concatenate(
        [jnp.stack([remote[0], first, row_first, crossing]), jnp.zeros((MAXD - 4,), jnp.int32)]
    )[None]
    rest = jnp.concatenate([remote[:, None], flags, jnp.zeros((NBL, MAXD - 1 - NBL), jnp.int32)], axis=1)
    slot = jnp.arange(MAXD, dtype=jnp.int32)
    turn = (slot // SLOTS - z) % SETS
    base = jnp.array([0, SLOTS, 3 * SLOTS, 2 * SLOTS], jnp.int32)
    place = (base[turn] + slot % SLOTS)[None]
    return jnp.concatenate([head, lists[:1], rest, place], axis=0)


def body(queries, keys, values, out_grad, ancestors, parents):
    tokens = queries.shape[0]
    groups = keys.shape[1]
    c = lax.axis_index("ctx")
    y = c // ZN
    z = c % ZN
    row_lists = ancestors[::ROW]
    slots = lax.dynamic_slice_in_dim(row_lists, (z % SETS) * SLOTS, SLOTS, 1)
    slot_rows = jnp.where(slots >= 0, slots // ROW, -1)
    my_rows = lax.dynamic_index_in_dim(slot_rows, y, 0, keepdims=False)

    kv = jnp.stack([keys, values]).transpose(2, 0, 1, 3)
    kv = lax.all_to_all(kv, "head", split_axis=0, concat_axis=0, tiled=True)
    own = kv.reshape(NBL, 2, 2, BLK // 2, HD)
    row = lax.all_gather(own, "ctx", axis=0, axis_index_groups=Z_GROUPS, tiled=True)
    q = lax.all_to_all(queries.reshape(tokens, -1), "head", split_axis=1, concat_axis=0, tiled=True)
    g = lax.all_to_all(out_grad.reshape(tokens, -1), "head", split_axis=1, concat_axis=0, tiled=True)

    row, q, g = lax.optimization_barrier((row, q, g))

    def of_row(k):
        return lax.dynamic_index_in_dim(slots, jnp.minimum(y + k, YN - 1), 0, keepdims=False)

    wanted = [jnp.clip(of_row(k) - y * ROW, 0, ROW - 1) for k in range(1, YN)]
    sent = pick(jnp.concatenate(wanted), row, YN - 1)
    mine = jnp.zeros((SLOTS,) + own.shape[1:], own.dtype)
    for k in range(1, YN):
        here = (my_rows == y - k)[:, None, None, None, None]
        mine = jnp.where(here, up(sent[k - 1], k), mine)
    half = SLOTS // 2
    cross = (mine, along(mine, -1), along(mine, 1), along(mine[:half], -2), along(mine[half:], 2))

    within = tree_reach_t(parents)
    info = info_of(ancestors, c, y, z)
    o, dq, row_grad, *turns = attention(info, q, g, own, row, cross, within)

    here = turns[0].astype(jnp.float32)
    here = here + along(turns[1], 1).astype(jnp.float32) + along(turns[2], -1).astype(jnp.float32)
    far = jnp.concatenate([along(turns[3], 2), along(turns[4], -2)], axis=0)
    here = (here + far.astype(jnp.float32)).astype(jnp.bfloat16)
    places, valids, parts = [], [], []
    for k in range(1, YN):
        parts.append(down(here, k))
        theirs = of_row(k)
        valid = (theirs >= 0) & (theirs // ROW == y) & (y + k < YN)
        places.append(jnp.where(valid, theirs - y * ROW, 0))
        valids.append(valid.astype(jnp.int32))
    vmem = pl.BlockSpec(memory_space=pltpu.VMEM)
    smem = pl.BlockSpec(memory_space=pltpu.SMEM)
    row_grad = pl.pallas_call(
        merge_kernel,
        out_shape=jax.ShapeDtypeStruct(row_grad.shape, row_grad.dtype),
        in_specs=[smem, smem] + [vmem] * YN,
        out_specs=vmem,
        compiler_params=pltpu.CompilerParams(vmem_limit_bytes=24 << 20),
    )(jnp.concatenate(places), jnp.concatenate(valids), row_grad, *parts)
    row_grad, o, dq = lax.optimization_barrier((row_grad, o, dq))
    grad = lax.psum_scatter(
        row_grad, "ctx", scatter_dimension=0, axis_index_groups=Z_GROUPS, tiled=True
    )
    o = lax.all_to_all(o, "head", split_axis=0, concat_axis=1, tiled=True)
    dq = lax.all_to_all(dq, "head", split_axis=0, concat_axis=1, tiled=True)
    grad, o, dq = lax.optimization_barrier((grad, o, dq))
    grad = grad.reshape(groups, 2, BLK // 2, HD)
    grad = lax.all_to_all(grad, "head", split_axis=0, concat_axis=0, tiled=True)
    grad = grad.transpose(1, 2, 0, 3)
    shape = queries.shape
    return (o.reshape(shape), dq.reshape(shape), grad[0], grad[1])


def solution(mesh):
    rows = P(("ctx", "head"), None, None)
    return jax.shard_map(
        body,
        mesh=mesh,
        in_specs=(rows, rows, rows, rows, P(), P("ctx", None)),
        out_specs=(rows, rows, rows, rows),
        check_vma=False,
    )
```

time: 276 us -> 217 us (0.79)
  waiting for transfers between devices: 152 us -> 79.3 us
  starting transfers between devices: 39.1 us -> 55.4 us
  Pallas kernels: 18.3 us -> 12.8 us
  local copies, waits for them, and re-layouts: 12 us -> 15 us
    reduce_scatter x1, waiting for transfers between devices: 43.5 us -> 5.11 us  [body(): lax.psum_scatter(row_grad, 'ctx', scatter_dimension=0, axis_index_groups=...]
    reduce_scatter x1 -> x0, waiting for transfers between devices: 33.8 us -> none  [body(): lax.psum_scatter(cross_grad, 'ctx', scatter_dimension=0, axis_index_group...]
    all_gather x1, waiting for transfers between devices: 36.7 us -> 6.27 us  [body(): lax.all_gather(own, 'ctx', axis=0, axis_index_groups=Z_GROUPS, tiled=True)]
    ppermute x0 -> x8, starting transfers between devices: none -> 21.2 us  [along(): return lax.ppermute(x, 'ctx', pairs)]
    ppermute x3, waiting for transfers between devices: 4.68 us -> 20.1 us  [down(): return lax.ppermute(x, 'ctx', pairs)]
    ppermute x0 -> x8, waiting for transfers between devices: none -> 12.5 us  [along(): return lax.ppermute(x, 'ctx', pairs)]
    unnamed x21 -> x35, local copies, waits for them, and re-layouts: 3.49 us -> 9.16 us
    pallas_call x2, Pallas kernels: 16.2 us -> 10.7 us  [the longest x1 10.1 us: attention(): pl.pallas_call(kernel, out_shape=tuple(like), in_specs=[smem] + [vmem] *...]
  transfers between devices with their start and end apart: 14 -> 20, of which waited for: 12 -> 13; matrix products, arithmetic and copies ran while one was open for 4% -> 5% of each run, Pallas kernels for 0% -> 0%
where the time goes in v3:
time: 217 us; the launch traced here: 215 us
  waiting for transfers between devices  79.3 us (37%)
  starting transfers between devices  55.4 us (26%)
  blocking collectives  32.7 us (15%)
  local copies, waits for them, and re-layouts  15 us (7%)
  between operations  14.4 us (7%)
  Pallas kernels  12.8 us (6%)
  other arithmetic  3.5 us (2%)
    ppermute x8, starting transfers between devices, along(): return lax.ppermute(x, 'ctx', pairs)  21.2 us
    ppermute x3, waiting for transfers between devices, down(): return lax.ppermute(x, 'ctx', pairs)  20.1 us
    all_to_all x1, blocking collectives, body(): o = lax.all_to_all(o, 'head', split_axis=0, concat_axis=1, tiled=True)  19.9 us
    all_to_all x1, blocking collectives, body(): kv = lax.all_to_all(kv, 'head', split_axis=0, concat_axis=0, tiled=True)  12.8 us
    ppermute x8, waiting for transfers between devices, along(): return lax.ppermute(x, 'ctx', pairs)  12.5 us
    all_to_all x1, waiting for transfers between devices, body(): dq = lax.all_to_all(dq, 'head', split_axis=0, concat_axis=1, tiled=True)  10.8 us
    all_to_all x1, waiting for transfers between devices, body(): lax.all_to_all(out_grad.reshape(tokens, -1), 'head', split_axis=1, concat...  10.1 us
    pallas_call x1, Pallas kernels, attention(): pl.pallas_call(kernel, out_shape=tuple(like), in_specs=[smem] + [vmem] *...  10.1 us
  transfers between devices with their start and end apart: 20, of which 13 were waited for; matrix products, arithmetic and copies ran while one was open for 5% of the time, Pallas kernels for 0%

profile of v3, /device:TPU:1, one launch (start us, length us, event | category | flops | bytes accessed | tf_op | source)
XLA Modules:
  0.0 215.2 jit_solution(9492768420333602157)
XLA Ops:
  7.2 1.1 copy_bitcast_fusion
  8.3 12.8 %all_to_all.86 = bf16[8,2,64,128]{3,2,1,0:T(8,128)(2,1)} all-to-all(bf16[8,2,64,128]{3,2,1,0:T(8,128)(2,1)S(1)} %maximum_bitcast_fusion), channel_id=1, replica_groups=mesh['ctx'=32,'head'=8] {'head'}, dimensions={0} | all-to-all | bytes 524288 | tf_op jit(solution)/shard_map/all_to_all | solution.py:324
  21.2 0.5 all_to_all.63
  21.7 0.9 copy.39
  22.6 4.6 %all-to-all-start.1 = ((bf16[64,8,640]{2,0,1:T(8,128)(2,1)}), bf16[64,8,640]{2,0,1:T(8,128)(2,1)S(1)}, u32[]{:S(2)}, u32[]{:S(2)}) async-start(bf16[64,8,640]{2,0,1:T(8,128)(2,1)} %copy.39), calls=%async_computation.1 | async-start | bytes 1310720 | tf_op jit(solution)/shard_map/all_to_all | solution.py:327
  27.5 0.7 gather_fusion
  28.1 0.2 dynamic-slice_reduce_fusion.2
  28.4 0.7 fusion.23
  29.1 0.5 all_to_all.67
  29.6 0.9 copy.40
  30.5 0.2 compare_reduce_fusion
  30.8 0.4 fusion.1
  31.2 6.9 %all-to-all-done.1 = bf16[64,8,640]{2,0,1:T(8,128)(2,1)S(1)} async-done(((bf16[64,8,640]{2,0,1:T(8,128)(2,1)}), bf16[64,8,640]{2,0,1:T(8,128)(2,1)S(1)}, u32[]{:S(2)}, u32[]{:S(2)}) %all-to-all-start.1) | async-done | bytes 655392 | tf_op jit(solution)/shard_map/all_to_all | solution.py:327
  38.1 4.3 %all-to-all-start.2 = ((bf16[64,8,640]{2,0,1:T(8,128)(2,1)}), bf16[64,8,640]{2,0,1:T(8,128)(2,1)S(1)}, u32[]{:S(2)}, u32[]{:S(2)}) async-start(bf16[64,8,640]{2,0,1:T(8,128)(2,1)} %copy.40), calls=%async_computation.2 | async-start | bytes 1310720 | tf_op jit(solution)/shard_map/all_to_all | solution.py:328
  42.5 0.4 fusion.3
  42.9 0.4 fusion.5
  43.2 10.1 %all-to-all-done.2 = bf16[64,8,640]{2,0,1:T(8,128)(2,1)S(1)} async-done(((bf16[64,8,640]{2,0,1:T(8,128)(2,1)}), bf16[64,8,640]{2,0,1:T(8,128)(2,1)S(1)}, u32[]{:S(2)}, u32[]{:S(2)}) %all-to-all-start.2) | async-done | bytes 655392 | tf_op jit(solution)/shard_map/all_to_all | solution.py:328
  53.3 6.3 %all-gather.2.cloned.1.call-done.from_ref.row_ref = bf16[32,2,2,64,128]{4,3,2,1,0:T(8,128)(2,1)} async-done(((bf16[4,2,2,64,128]{4,3,2,1,0:T(8,128)(2,1)}), bf16[32,2,2,64,128]{4,3,2,1,0:T(8,128)(2,1)}) %all-gather.2.cloned.1.call-update) | async-done | bytes 2097168 | tf_op jit(solution)/shard_map/all_gather | solution.py:326
  59.6 1.6 copy-done
  61.2 0.6 shard_map.102
  61.8 4.3 %collective-permute-start = (bf16[4,2,2,64,128]{4,3,2,1,0:T(8,128)(2,1)S(1)}, bf16[4,2,2,64,128]{4,3,2,1,0:T(8,128)(2,1)S(1)}, u32[]{:S(2)}, u32[]{:S(2)}) collective-permute-start(bf16[4,2,2,64,128]{4,3,2,1,0:T(8,128)(2,1)S(1)} %get-tuple-element.27), channel_id=1, source_target_pairs={{0,192},{8,200},{16,208},{24,216},{32,224},{40,232},{48,240},{56,2... | collective-permute-start | bytes 786440 | tf_op jit(solution)/shard_map/ppermute | solution.py:285
  66.2 1.3 collective-permute-start.1
  67.5 2.5 %collective-permute-start.2 = (bf16[4,2,2,64,128]{4,3,2,1,0:T(8,128)(2,1)S(1)}, bf16[4,2,2,64,128]{4,3,2,1,0:T(8,128)(2,1)S(1)}, u32[]{:S(2)}, u32[]{:S(2)}) collective-permute-start(bf16[4,2,2,64,128]{4,3,2,1,0:T(8,128)(2,1)S(1)} %get-tuple-element.29), channel_id=1, source_target_pairs={{0,64},{8,72},{16,80},{24,88},{32,96},{40,104},{48,112},{56,120},{... | collective-permute-start | bytes 786440 | tf_op jit(solution)/shard_map/ppermute | solution.py:285
  70.0 0.2 compare_reduce_fusion.3
  70.2 0.9 fusion.7.within_ref
  71.1 1.6 collective-permute-done
  72.7 1.3 collective-permute-done.2
  74.0 0.1 select_select_fusion.mine_ref
  74.1 0.8 collective-permute-start.4
  74.9 2.0 collective-permute-start.3
  76.9 2.6 %collective-permute-start.6 = (bf16[2,2,2,64,128]{4,3,2,1,0:T(8,128)(2,1)S(1)}, bf16[2,2,2,64,128]{4,3,2,1,0:T(8,128)(2,1)S(1)}, u32[]{:S(2)}, u32[]{:S(2)}) collective-permute-start(bf16[2,2,2,64,128]{4,3,2,1,0:T(8,128)(2,1)S(1)} %get-tuple-element.66), channel_id=1, source_target_pairs={{0,16},{8,24},{16,32},{24,40},{32,48},{40,56},{48,0},{56,8},{64,80... | collective-permute-start | bytes 393224 | tf_op jit(solution)/shard_map/ppermute | solution.py:280
  79.5 1.0 collective-permute-start.5
  80.5 0.1 convert_reduce_fusion
  80.7 0.1 copy.36
  80.8 0.7 concatenate.26
  81.5 0.7 pad_add_fusion.info_ref
  82.2 0.8 collective-permute-done.6.near_ref
  83.0 4.4 %collective-permute-done.5.far_ref = bf16[2,2,2,64,128]{4,3,2,1,0:T(8,128)(2,1)S(1)} collective-permute-done((bf16[2,2,2,64,128]{4,3,2,1,0:T(8,128)(2,1)S(1)}, bf16[2,2,2,64,128]{4,3,2,1,0:T(8,128)(2,1)S(1)}, u32[]{:S(2)}, u32[]{:S(2)}) %collective-permute-start.5) | collective-permute-done | bytes 131104 | tf_op jit(solution)/shard_map/ppermute | solution.py:280
  87.4 0.6 copy-done.12
  88.2 0.7 copy-done.10
  88.9 10.1 %shard_map.103 = (bf16[512,640]{1,0:T(8,128)(2,1)}, bf16[512,640]{1,0:T(8,128)(2,1)}, bf16[32,2,2,64,128]{4,3,2,1,0:T(8,128)(2,1)}, bf16[4,2,2,64,128]{4,3,2,1,0...) custom-call(s32[7,16]{1,0:T(8,128)} %pad_add_fusion.info_ref, ...), custom_call_target="tpu_custom_call" | custom-call | tf_op jit(solution)/shard_map/pallas_call | solution.py:217
  98.9 5.1 %collective-permute-start.7 = (bf16[4,2,2,64,128]{4,3,2,1,0:T(8,128)(2,1)}, bf16[4,2,2,64,128]{4,3,2,1,0:T(8,128)(2,1)S(1)}, u32[]{:S(2)}, u32[]{:S(2)}) collective-permute-start(bf16[4,2,2,64,128]{4,3,2,1,0:T(8,128)(2,1)} %get-tuple-element.32), channel_id=1, source_target_pairs={{0,8},{8,16},{16,24},{24,32},{32,40},{40,48},{48,56},{56,0},{64,72... | collective-permute-start | bytes 786440 | tf_op jit(solution)/shard_map/ppermute | solution.py:280
  104.0 3.9 %collective-permute-start.8 = (bf16[4,2,2,64,128]{4,3,2,1,0:T(8,128)(2,1)}, bf16[4,2,2,64,128]{4,3,2,1,0:T(8,128)(2,1)S(1)}, u32[]{:S(2)}, u32[]{:S(2)}) collective-permute-start(bf16[4,2,2,64,128]{4,3,2,1,0:T(8,128)(2,1)} %get-tuple-element.33), channel_id=1, source_target_pairs={{0,56},{8,0},{16,8},{24,16},{32,24},{40,32},{48,40},{56,48},{64,12... | collective-permute-start | bytes 786440 | tf_op jit(solution)/shard_map/ppermute | solution.py:280
  107.9 5.8 %collective-permute-start.9 = (bf16[2,2,2,64,128]{4,3,2,1,0:T(8,128)(2,1)}, bf16[2,2,2,64,128]{4,3,2,1,0:T(8,128)(2,1)S(1)}, u32[]{:S(2)}, u32[]{:S(2)}) collective-permute-start(bf16[2,2,2,64,128]{4,3,2,1,0:T(8,128)(2,1)} %get-tuple-element.34), channel_id=1, source_target_pairs={{0,16},{8,24},{16,32},{24,40},{32,48},{40,56},{48,0},{56,8},{64,80... | collective-permute-start | bytes 393224 | tf_op jit(solution)/shard_map/ppermute | solution.py:280
  113.7 2.6 %collective-permute-done.9 = bf16[2,2,2,64,128]{4,3,2,1,0:T(8,128)(2,1)S(1)} collective-permute-done((bf16[2,2,2,64,128]{4,3,2,1,0:T(8,128)(2,1)}, bf16[2,2,2,64,128]{4,3,2,1,0:T(8,128)(2,1)S(1)}, u32[]{:S(2)}, u32[]{:S(2)}) %collective-permute-start.9) | collective-permute-done | bytes 131104 | tf_op jit(solution)/shard_map/ppermute | solution.py:280
  116.4 4.6 %collective-permute-done.10 = bf16[2,2,2,64,128]{4,3,2,1,0:T(8,128)(2,1)S(1)} collective-permute-done((bf16[2,2,2,64,128]{4,3,2,1,0:T(8,128)(2,1)}, bf16[2,2,2,64,128]{4,3,2,1,0:T(8,128)(2,1)S(1)}, u32[]{:S(2)}, u32[]{:S(2)}) %collective-permute-start.10) | collective-permute-done | bytes 131104 | tf_op jit(solution)/shard_map/ppermute | solution.py:280
  120.9 1.1 add_convert_fusion
  122.1 1.3 collective-permute-start.13
  123.4 1.3 collective-permute-start.12
  124.7 1.3 collective-permute-start.11
  126.1 20.1 %collective-permute-done.13.rest_2_ = bf16[4,2,2,64,128]{4,3,2,1,0:T(8,128)(2,1)S(1)} collective-permute-done((bf16[4,2,2,64,128]{4,3,2,1,0:T(8,128)(2,1)S(1)}, bf16[4,2,2,64,128]{4,3,2,1,0:T(8,128)(2,1)S(1)}, u32[]{:S(2)}, u32[]{:S(2)}) %collective-permute-start.13) | collective-permute-done | bytes 262176 | tf_op jit(solution)/shard_map/ppermute | solution.py:290
  146.2 1.6 copy-done.1
  147.8 2.2 %shard_map.104 = bf16[32,2,2,64,128]{4,3,2,1,0:T(8,128)(2,1)} custom-call(s32[12]{0:T(128)S(1)} %pad_add_fusion.1.place_ref, s32[12]{0:T(128)S(1)} %add_convert_fusion.1.valid_ref, bf16[32,2,2,64,128]{4,3,2,1,0:T(8,128)(2,1)S(1)} %copy-done.1, bf16[4,2,2,64,128]{4,3,2,1,0:T(8,128)(2,1)S(1)} %collective-permute-done.11.rest_0_, ...), custom_call_target="tpu_custom_call" | custom-call | tf_op jit(solution)/shard_map/pallas_call | solution.py:361
  150.0 1.1 copy-done.8
  151.1 19.9 %all_to_all.87 = bf16[8,64,640]{2,1,0:T(8,128)(2,1)S(1)} all-to-all(bf16[8,64,640]{2,1,0:T(8,128)(2,1)S(1)} %bitcast.56), channel_id=1, replica_groups=mesh['ctx'=32,'head'=8] {'head'}, dimensions={0} | all-to-all | bytes 1310720 | tf_op jit(solution)/shard_map/all_to_all | solution.py:372
  171.0 4.3 %all-to-all-start.4 = ((bf16[8,64,640]{2,1,0:T(8,128)(2,1)}), bf16[8,64,640]{2,1,0:T(8,128)(2,1)S(1)}, u32[]{:S(2)}, u32[]{:S(2)}) async-start(bf16[8,64,640]{2,1,0:T(8,128)(2,1)} %bitcast.17), calls=%async_computation.5 | async-start | bytes 1310720 | tf_op jit(solution)/shard_map/all_to_all | solution.py:373
  175.4 10.8 %all-to-all-done.4 = bf16[8,64,640]{2,1,0:T(8,128)(2,1)S(1)} async-done(((bf16[8,64,640]{2,1,0:T(8,128)(2,1)}), bf16[8,64,640]{2,1,0:T(8,128)(2,1)S(1)}, u32[]{:S(2)}, u32[]{:S(2)}) %all-to-all-start.4) | async-done | bytes 655392 | tf_op jit(solution)/shard_map/all_to_all | solution.py:373
  186.3 5.1 %reduce-scatter.2.cloned.1.call-done = bf16[4,2,2,64,128]{4,3,2,1,0:T(8,128)(2,1)} async-done(((bf16[32,2,2,64,128]{4,3,2,1,0:T(8,128)(2,1)}), bf16[4,2,2,64,128]{4,3,2,1,0:T(8,128)(2,1)}) %reduce-scatter.2.cloned.1.call-update) | async-done | bytes 262160 | tf_op jit(solution)/shard_map/reduce_scatter | solution.py:369
  191.4 9.0 %all-to-all-start.5 = ((bf16[8,2,64,128]{3,2,1,0:T(8,128)(2,1)}), bf16[8,2,64,128]{3,2,1,0:T(8,128)(2,1)S(1)}, u32[]{:S(2)}, u32[]{:S(2)}) async-start(bf16[8,2,64,128]{3,2,1,0:T(8,128)(2,1)} %bitcast.59), calls=%async_computation.6 | async-start | bytes 524288 | tf_op jit(solution)/shard_map/all_to_all | solution.py:376
  200.4 0.9 copy.48
  201.3 0.9 copy.49
  202.2 4.6 %all-to-all-done.5 = bf16[8,2,64,128]{3,2,1,0:T(8,128)(2,1)S(1)} async-done(((bf16[8,2,64,128]{3,2,1,0:T(8,128)(2,1)}), bf16[8,2,64,128]{3,2,1,0:T(8,128)(2,1)S(1)}, u32[]{:S(2)}, u32[]{:S(2)}) %all-to-all-start.5) | async-done | bytes 262176 | tf_op jit(solution)/shard_map/all_to_all | solution.py:376
  206.9 0.7 copy.44
  207.6 0.7 copy.43
  (59 shorter events, 1.0 us)
Async XLA Ops:
  7.2 14.0 %copy-start.6 = (bf16[64,40,128]{2,1,0:T(8,128)(2,1)S(1)}, bf16[64,40,128]{2,1,0:T(8,128)(2,1)}, u32[]{:S(2)}) copy-start(bf16[64,40,128]{2,1,0:T(8,128)(2,1)} %param.7) | copy-start | bytes 1966084
  7.2 52.4 %all-gather.2.cloned.1.call-start = ((), (), s32[]{:S(2)}) async-start(), calls=%async_computation.7 | async-start | bytes 2359296 | tf_op jit(solution)/shard_map/all_gather | solution.py:326
  21.1 6.1 %copy-start.13 = (s32[128,16]{0,1:T(8,128)S(1)}, s32[128,16]{0,1:T(8,128)}, u32[]{:S(2)}) copy-start(s32[128,16]{0,1:T(8,128)} %param.11) | copy-start | bytes 24580
  21.2 6.3 %copy-start.2 = (s32[4]{0:T(128)S(1)}, s32[4]{0:T(128)}, u32[]{:S(2)}) copy-start(s32[4]{0:T(128)} %constant.182.clone) | copy-start | bytes 52
  21.2 7.9 %copy-start.7 = (bf16[64,40,128]{2,1,0:T(8,128)(2,1)S(1)}, bf16[64,40,128]{2,1,0:T(8,128)(2,1)}, u32[]{:S(2)}) copy-start(bf16[64,40,128]{2,1,0:T(8,128)(2,1)} %param.10) | copy-start | bytes 1966084
  22.6 8.2 %copy-start.14 = (s32[4,128]{1,0:T(4,128)S(1)}, s32[4,128]{1,0:T(4,128)}, u32[]{:S(2)}) copy-start(s32[4,128]{1,0:T(4,128)} %param.12) | copy-start | bytes 6148
  22.6 15.5 %all-to-all-start.1 = ((bf16[64,8,640]{2,0,1:T(8,128)(2,1)}), bf16[64,8,640]{2,0,1:T(8,128)(2,1)S(1)}, u32[]{:S(2)}, u32[]{:S(2)}) async-start(bf16[64,8,640]{2,0,1:T(8,128)(2,1)} %copy.39), calls=%async_computation.1 | async-start | bytes 1310720 | tf_op jit(solution)/shard_map/all_to_all | solution.py:327
  38.1 23.7 %copy-start.3 = (bf16[64,8,640]{2,0,1:T(8,128)(2,1)}, bf16[64,8,640]{2,0,1:T(8,128)(2,1)S(1)}, u32[]{:S(2)}) copy-start(bf16[64,8,640]{2,0,1:T(8,128)(2,1)S(1)} %all-to-all-done.1) | copy-start | bytes 1966084
  38.1 15.2 %all-to-all-start.2 = ((bf16[64,8,640]{2,0,1:T(8,128)(2,1)}), bf16[64,8,640]{2,0,1:T(8,128)(2,1)S(1)}, u32[]{:S(2)}, u32[]{:S(2)}) async-start(bf16[64,8,640]{2,0,1:T(8,128)(2,1)} %copy.40), calls=%async_computation.2 | async-start | bytes 1310720 | tf_op jit(solution)/shard_map/all_to_all | solution.py:328
  42.4 149.0 %reduce-scatter.2.cloned.1.call-start = ((), (), s32[]{:S(2)}) async-start(), calls=%async_computation.8 | async-start | bytes 2359296 | tf_op jit(solution)/shard_map/reduce_scatter | solution.py:369
  53.3 23.5 %copy-start.4 = (bf16[64,8,640]{2,0,1:T(8,128)(2,1)}, bf16[64,8,640]{2,0,1:T(8,128)(2,1)S(1)}, u32[]{:S(2)}) copy-start(bf16[64,8,640]{2,0,1:T(8,128)(2,1)S(1)} %all-to-all-done.2) | copy-start | bytes 1966084
  59.6 1.6 copy-start
  61.8 10.8 %collective-permute-start = (bf16[4,2,2,64,128]{4,3,2,1,0:T(8,128)(2,1)S(1)}, bf16[4,2,2,64,128]{4,3,2,1,0:T(8,128)(2,1)S(1)}, u32[]{:S(2)}, u32[]{:S(2)}) collective-permute-start(bf16[4,2,2,64,128]{4,3,2,1,0:T(8,128)(2,1)S(1)} %get-tuple-element.27), channel_id=1, source_target_pairs={{0,192},{8,200},{16,208},{24,216},{32,224},{40,232},{48,240},{56,2... | collective-permute-start | bytes 786440 | tf_op jit(solution)/shard_map/ppermute | solution.py:285
  66.2 6.5 %collective-permute-start.1 = (bf16[4,2,2,64,128]{4,3,2,1,0:T(8,128)(2,1)S(1)}, bf16[4,2,2,64,128]{4,3,2,1,0:T(8,128)(2,1)S(1)}, u32[]{:S(2)}, u32[]{:S(2)}) collective-permute-start(bf16[4,2,2,64,128]{4,3,2,1,0:T(8,128)(2,1)S(1)} %get-tuple-element.28), channel_id=1, source_target_pairs={{0,128},{8,136},{16,144},{24,152},{32,160},{40,168},{48,176},{56,1... | collective-permute-start | bytes 786440 | tf_op jit(solution)/shard_map/ppermute | solution.py:285
  67.5 6.5 %collective-permute-start.2 = (bf16[4,2,2,64,128]{4,3,2,1,0:T(8,128)(2,1)S(1)}, bf16[4,2,2,64,128]{4,3,2,1,0:T(8,128)(2,1)S(1)}, u32[]{:S(2)}, u32[]{:S(2)}) collective-permute-start(bf16[4,2,2,64,128]{4,3,2,1,0:T(8,128)(2,1)S(1)} %get-tuple-element.29), channel_id=1, source_target_pairs={{0,64},{8,72},{16,80},{24,88},{32,96},{40,104},{48,112},{56,120},{... | collective-permute-start | bytes 786440 | tf_op jit(solution)/shard_map/ppermute | solution.py:285
  74.1 13.3 %copy-start.5 = (bf16[4,2,2,64,128]{4,3,2,1,0:T(8,128)(2,1)}, bf16[4,2,2,64,128]{4,3,2,1,0:T(8,128)(2,1)S(1)}, u32[]{:S(2)}) copy-start(bf16[4,2,2,64,128]{4,3,2,1,0:T(8,128)(2,1)S(1)} %select_select_fusion.mine_ref) | copy-start | bytes 786436
  74.1 13.3 %collective-permute-start.4 = (bf16[4,2,2,64,128]{4,3,2,1,0:T(8,128)(2,1)S(1)}, bf16[4,2,2,64,128]{4,3,2,1,0:T(8,128)(2,1)S(1)}, u32[]{:S(2)}, u32[]{:S(2)}) collective-permute-start(bf16[4,2,2,64,128]{4,3,2,1,0:T(8,128)(2,1)S(1)} %select_select_fusion.mine_ref), channel_id=1, source_target_pairs={{0,8},{8,16},{16,24},{24,32},{32,40},{40,48},{48,56},{56,0},{64,72... | collective-permute-start | bytes 786440 | tf_op jit(solution)/shard_map/ppermute | solution.py:280
  74.9 12.6 %collective-permute-start.3 = (bf16[4,2,2,64,128]{4,3,2,1,0:T(8,128)(2,1)S(1)}, bf16[4,2,2,64,128]{4,3,2,1,0:T(8,128)(2,1)S(1)}, u32[]{:S(2)}, u32[]{:S(2)}) collective-permute-start(bf16[4,2,2,64,128]{4,3,2,1,0:T(8,128)(2,1)S(1)} %select_select_fusion.mine_ref), channel_id=1, source_target_pairs={{0,56},{8,0},{16,8},{24,16},{32,24},{40,32},{48,40},{56,48},{64,12... | collective-permute-start | bytes 786440 | tf_op jit(solution)/shard_map/ppermute | solution.py:280
  76.9 6.1 %collective-permute-start.6 = (bf16[2,2,2,64,128]{4,3,2,1,0:T(8,128)(2,1)S(1)}, bf16[2,2,2,64,128]{4,3,2,1,0:T(8,128)(2,1)S(1)}, u32[]{:S(2)}, u32[]{:S(2)}) collective-permute-start(bf16[2,2,2,64,128]{4,3,2,1,0:T(8,128)(2,1)S(1)} %get-tuple-element.66), channel_id=1, source_target_pairs={{0,16},{8,24},{16,32},{24,40},{32,48},{40,56},{48,0},{56,8},{64,80... | collective-permute-start | bytes 393224 | tf_op jit(solution)/shard_map/ppermute | solution.py:280
  79.5 7.9 %collective-permute-start.5 = (bf16[2,2,2,64,128]{4,3,2,1,0:T(8,128)(2,1)S(1)}, bf16[2,2,2,64,128]{4,3,2,1,0:T(8,128)(2,1)S(1)}, u32[]{:S(2)}, u32[]{:S(2)}) collective-permute-start(bf16[2,2,2,64,128]{4,3,2,1,0:T(8,128)(2,1)S(1)} %get-tuple-element.67), channel_id=1, source_target_pairs={{0,48},{8,56},{16,0},{24,8},{32,16},{40,24},{48,32},{56,40},{64,11... | collective-permute-start | bytes 393224 | tf_op jit(solution)/shard_map/ppermute | solution.py:280
  83.0 4.4 %copy-start.11 = (bf16[2,2,2,64,128]{4,3,2,1,0:T(8,128)(2,1)}, bf16[2,2,2,64,128]{4,3,2,1,0:T(8,128)(2,1)S(1)}, u32[]{:S(2)}) copy-start(bf16[2,2,2,64,128]{4,3,2,1,0:T(8,128)(2,1)S(1)} %collective-permute-done.6.near_ref) | copy-start | bytes 393220
  87.4 0.7 copy-start.12
  87.4 0.7 copy-start.9
  88.2 0.7 copy-start.10
  98.9 22.0 %collective-permute-start.7 = (bf16[4,2,2,64,128]{4,3,2,1,0:T(8,128)(2,1)}, bf16[4,2,2,64,128]{4,3,2,1,0:T(8,128)(2,1)S(1)}, u32[]{:S(2)}, u32[]{:S(2)}) collective-permute-start(bf16[4,2,2,64,128]{4,3,2,1,0:T(8,128)(2,1)} %get-tuple-element.32), channel_id=1, source_target_pairs={{0,8},{8,16},{16,24},{24,32},{32,40},{40,48},{48,56},{56,0},{64,72... | collective-permute-start | bytes 786440 | tf_op jit(solution)/shard_map/ppermute | solution.py:280
  104.0 17.0 %collective-permute-start.8 = (bf16[4,2,2,64,128]{4,3,2,1,0:T(8,128)(2,1)}, bf16[4,2,2,64,128]{4,3,2,1,0:T(8,128)(2,1)S(1)}, u32[]{:S(2)}, u32[]{:S(2)}) collective-permute-start(bf16[4,2,2,64,128]{4,3,2,1,0:T(8,128)(2,1)} %get-tuple-element.33), channel_id=1, source_target_pairs={{0,56},{8,0},{16,8},{24,16},{32,24},{40,32},{48,40},{56,48},{64,12... | collective-permute-start | bytes 786440 | tf_op jit(solution)/shard_map/ppermute | solution.py:280
  107.9 8.5 %collective-permute-start.9 = (bf16[2,2,2,64,128]{4,3,2,1,0:T(8,128)(2,1)}, bf16[2,2,2,64,128]{4,3,2,1,0:T(8,128)(2,1)S(1)}, u32[]{:S(2)}, u32[]{:S(2)}) collective-permute-start(bf16[2,2,2,64,128]{4,3,2,1,0:T(8,128)(2,1)} %get-tuple-element.34), channel_id=1, source_target_pairs={{0,16},{8,24},{16,32},{24,40},{32,48},{40,56},{48,0},{56,8},{64,80... | collective-permute-start | bytes 393224 | tf_op jit(solution)/shard_map/ppermute | solution.py:280
  113.7 7.2 %collective-permute-start.10 = (bf16[2,2,2,64,128]{4,3,2,1,0:T(8,128)(2,1)}, bf16[2,2,2,64,128]{4,3,2,1,0:T(8,128)(2,1)S(1)}, u32[]{:S(2)}, u32[]{:S(2)}) collective-permute-start(bf16[2,2,2,64,128]{4,3,2,1,0:T(8,128)(2,1)} %get-tuple-element.35), channel_id=1, source_target_pairs={{0,48},{8,56},{16,0},{24,8},{32,16},{40,24},{48,32},{56,40},{64,11... | collective-permute-start | bytes 393224 | tf_op jit(solution)/shard_map/ppermute | solution.py:280
  122.1 24.1 %collective-permute-start.13 = (bf16[4,2,2,64,128]{4,3,2,1,0:T(8,128)(2,1)S(1)}, bf16[4,2,2,64,128]{4,3,2,1,0:T(8,128)(2,1)S(1)}, u32[]{:S(2)}, u32[]{:S(2)}) collective-permute-start(bf16[4,2,2,64,128]{4,3,2,1,0:T(8,128)(2,1)S(1)} %add_convert_fusion), channel_id=1, source_target_pairs={{192,0},{200,8},{208,16},{216,24},{224,32},{232,40},{240,48},{248,... | collective-permute-start | bytes 786440 | tf_op jit(solution)/shard_map/ppermute | solution.py:290
  123.4 22.8 %collective-permute-start.12 = (bf16[4,2,2,64,128]{4,3,2,1,0:T(8,128)(2,1)S(1)}, bf16[4,2,2,64,128]{4,3,2,1,0:T(8,128)(2,1)S(1)}, u32[]{:S(2)}, u32[]{:S(2)}) collective-permute-start(bf16[4,2,2,64,128]{4,3,2,1,0:T(8,128)(2,1)S(1)} %add_convert_fusion), channel_id=1, source_target_pairs={{128,0},{136,8},{144,16},{152,24},{160,32},{168,40},{176,48},{184,... | collective-permute-start | bytes 786440 | tf_op jit(solution)/shard_map/ppermute | solution.py:290
  124.7 21.5 %collective-permute-start.11 = (bf16[4,2,2,64,128]{4,3,2,1,0:T(8,128)(2,1)S(1)}, bf16[4,2,2,64,128]{4,3,2,1,0:T(8,128)(2,1)S(1)}, u32[]{:S(2)}, u32[]{:S(2)}) collective-permute-start(bf16[4,2,2,64,128]{4,3,2,1,0:T(8,128)(2,1)S(1)} %add_convert_fusion), channel_id=1, source_target_pairs={{64,0},{72,8},{80,16},{88,24},{96,32},{104,40},{112,48},{120,56},{... | collective-permute-start | bytes 786440 | tf_op jit(solution)/shard_map/ppermute | solution.py:290
  146.2 1.6 copy-start.1
  150.0 1.1 copy-start.8
  171.0 15.2 %all-to-all-start.4 = ((bf16[8,64,640]{2,1,0:T(8,128)(2,1)}), bf16[8,64,640]{2,1,0:T(8,128)(2,1)S(1)}, u32[]{:S(2)}, u32[]{:S(2)}) async-start(bf16[8,64,640]{2,1,0:T(8,128)(2,1)} %bitcast.17), calls=%async_computation.5 | async-start | bytes 1310720 | tf_op jit(solution)/shard_map/all_to_all | solution.py:373
  191.4 15.5 %all-to-all-start.5 = ((bf16[8,2,64,128]{3,2,1,0:T(8,128)(2,1)}), bf16[8,2,64,128]{3,2,1,0:T(8,128)(2,1)S(1)}, u32[]{:S(2)}, u32[]{:S(2)}) async-start(bf16[8,2,64,128]{3,2,1,0:T(8,128)(2,1)} %bitcast.59), calls=%async_computation.6 | async-start | bytes 524288 | tf_op jit(solution)/shard_map/all_to_all | solution.py:376
Sparse Core Ops, SparseCore 0:
  21.3 38.2 all-gather.1
  150.1 41.1 reduce-scatter.1

commit v4 on v3

v4 whole, which is shorter than its diff:
```python
import math

import jax
import jax.numpy as jnp
from jax import lax
from jax.experimental import pallas as pl
from jax.experimental.pallas import tpu as pltpu
from jax.sharding import PartitionSpec as P

HD = 128
GROUP = 5
BLK = 128
NBL = 4
MAXD = 16
QN = GROUP * BLK
SCALE = 1.0 / math.sqrt(HD)
LOG2E = 1.0 / math.log(2.0)
NEG = -1e30
OWNP = NBL // 2
NPAIR = OWNP + MAXD // 2 + 1
WIDE = NBL * QN


def tree_reach_t(parents):
    block_width = parents.shape[-1]
    hops = parents[:, None, :] == jnp.arange(block_width, dtype=jnp.int32)[None, :, None]
    eye = jnp.eye(block_width, dtype=jnp.bool_)[None]
    reached = (hops | eye).astype(jnp.bfloat16)
    for _ in range(max(1, (block_width - 1).bit_length())):
        product = jnp.einsum("bts,bsu->btu", reached, reached, preferred_element_type=jnp.float32)
        reached = jnp.minimum(product, 1.0).astype(jnp.bfloat16)
    return reached.astype(jnp.float32)


def dot(a, b, dims):
    return lax.dot_general(a, b, (dims, ((), ())), preferred_element_type=jnp.float32)


def gather(ref):
    return jnp.concatenate(
        [ref[i * BLK:(i + 1) * BLK, r * HD:(r + 1) * HD] for i in range(NBL) for r in range(GROUP)],
        axis=0,
    )


def fold(x, op):
    return op(x.reshape(-1, 8, x.shape[-1]), axis=0)


def limits(counts, p):
    row_id = lax.broadcasted_iota(jnp.int32, (2 * BLK, 1), 0)
    return [jnp.where(row_id + 2 * BLK * p < BLK * n, 0.0, NEG) for n in counts]


def masked(raw, bias):
    return jnp.concatenate([raw[:, i * QN:(i + 1) * QN] + bias[i] for i in range(NBL)], axis=1)


def own_kernel(
    info_ref, q_ref, g_ref, own_ref, within_ref,
    q_out, g_out, qt_out, gt_out, e_ref, max_ref, sum_ref,
):
    q = gather(q_ref)
    g = gather(g_ref)
    qt = q.T
    q_out[...] = q
    g_out[...] = g
    qt_out[...] = qt
    gt_out[...] = g.T
    mx = jnp.full((8, WIDE), NEG, jnp.float32)
    for p in range(OWNP):
        k = own_ref[2 * p:2 * p + 2, :, 0].reshape(2 * BLK, HD)
        raw = dot(k, qt, ((1,), (0,))) * (SCALE * LOG2E)
        parts = []
        for half in range(2):
            j = 2 * p + half
            pieces = []
            for i in range(NBL):
                piece = raw[half * BLK:(half + 1) * BLK, i * QN:(i + 1) * QN]
                if j < i:
                    piece = piece + jnp.where(info_ref[2 + i, 1 + j] > 0, 0.0, NEG)
                elif j == i:
                    bias = jnp.where(within_ref[i] > 0.5, 0.0, NEG)
                    piece = piece + jnp.concatenate([bias] * GROUP, axis=1)
                else:
                    piece = jnp.full_like(piece, NEG)
                pieces.append(piece)
            parts.append(jnp.concatenate(pieces, axis=1))
        s = jnp.concatenate(parts, axis=0)
        e_ref[p] = s
        mx = jnp.maximum(mx, fold(s, jnp.max))
    m = jnp.max(mx, axis=0, keepdims=True)
    total = jnp.zeros((8, WIDE), jnp.float32)
    for p in range(OWNP):
        e = jnp.exp2(e_ref[p] - m)
        e_ref[p] = e
        total = total + fold(e, jnp.sum)
    max_ref[...] = m
    sum_ref[...] = jnp.sum(total, axis=0, keepdims=True)


def row_kernel(info_ref, qt_ref, row_ref, e_ref, max_ref, sum_ref, s_s, sems):
    remote = info_ref[0, 0]
    row_first = info_ref[0, 2]
    crossing = info_ref[0, 3]
    pairs = (remote - crossing + 1) // 2
    counts = [info_ref[2 + i, 0] - crossing for i in range(NBL)]

    def scores(p, mx):
        ks = []
        for half in range(2):
            block = info_ref[1, jnp.minimum(crossing + 2 * p + half, MAXD - 1)]
            ks.append(row_ref[jnp.maximum(block - row_first, 0), :, 0].reshape(BLK, HD))
        k = jnp.concatenate(ks, axis=0)
        raw = dot(k, qt_ref[...], ((1,), (0,))) * (SCALE * LOG2E)
        s = masked(raw, limits(counts, p))
        s_s[p] = s
        return jnp.maximum(mx, fold(s, jnp.max))

    mx = lax.fori_loop(0, pairs, scores, jnp.full((8, WIDE), NEG, jnp.float32))
    m = jnp.max(mx, axis=0, keepdims=True)

    def expo(p, total):
        e = jnp.exp2(s_s[p] - m)
        s_s[p] = e
        pltpu.make_async_copy(s_s.at[p], e_ref.at[p], sems.at[p]).start()
        return total + fold(e, jnp.sum)

    total = lax.fori_loop(0, pairs, expo, jnp.zeros((8, WIDE), jnp.float32))
    max_ref[...] = m
    sum_ref[...] = jnp.sum(total, axis=0, keepdims=True)

    def finish(p, carry):
        pltpu.make_async_copy(s_s.at[p], e_ref.at[p], sems.at[p]).wait()
        return carry

    lax.fori_loop(0, pairs, finish, 0)


def kernel(
    info_ref, q_ref, g_ref, qt_ref, gt_ref, own_ref, row_ref,
    mine_ref, next_ref, last_ref, far_ref, near_ref,
    own_max, own_sum, row_max, row_sum, own_e, row_e,
    o_ref, dq_ref, row_grad_ref, mine_grad_ref, next_grad_ref, last_grad_ref, far_grad_ref, near_grad_ref,
    k_s, v_s, kt_s, vt_s, s_s, dk_s, dv_s, acc_s, fac_s, cross_s, cross_grad_s, sems,
):
    remote = info_ref[0, 0]
    row_first = info_ref[0, 2]
    crossing = info_ref[0, 3]
    row_pairs = (remote - crossing + 1) // 2
    cross_pairs = (crossing + 1) // 2
    cross_at = OWNP + row_pairs
    pairs = cross_at + cross_pairs

    def own_copy(p):
        return pltpu.make_async_copy(own_e.at[p], s_s.at[p], sems.at[p])

    def row_copy(p):
        return pltpu.make_async_copy(row_e.at[p], s_s.at[OWNP + p], sems.at[OWNP + p])

    for p in range(OWNP):
        own_copy(p).start()

    def begin(p, carry):
        row_copy(p).start()
        return carry

    lax.fori_loop(0, row_pairs, begin, 0)

    row_grad_ref[...] = jnp.zeros_like(row_grad_ref)
    cross_grad_s[...] = jnp.zeros_like(cross_grad_s)
    at = 0
    for ref in (mine_ref, next_ref, last_ref, far_ref, near_ref):
        cross_s[at:at + ref.shape[0]] = ref[...]
        at += ref.shape[0]

    def row_place(slot):
        return jnp.maximum(info_ref[1, jnp.minimum(slot, MAXD - 1)] - row_first, 0)

    def take(p, half, kv):
        k = kv[:, 0].reshape(BLK, HD)
        v = kv[:, 1].reshape(BLK, HD)
        k_s[p, half * BLK:(half + 1) * BLK, :] = k
        v_s[p, half * BLK:(half + 1) * BLK, :] = v
        kt_s[p, :, half * BLK:(half + 1) * BLK] = k.T
        vt_s[p, :, half * BLK:(half + 1) * BLK] = v.T

    for j in range(NBL):
        take(j // 2, j % 2, own_ref[j])

    def load_row(p, carry):
        for half in range(2):
            take(OWNP + p, half, row_ref[row_place(crossing + 2 * p + half)])
        return carry

    lax.fori_loop(0, row_pairs, load_row, 0)

    def load_cross(p, carry):
        for half in range(2):
            take(cross_at + p, half, cross_s[info_ref[6, 2 * p + half]])
        return carry

    lax.fori_loop(0, cross_pairs, load_cross, 0)

    counts = [jnp.minimum(info_ref[2 + i, 0], crossing) for i in range(NBL)]

    def scores(p, mx):
        raw = dot(k_s[cross_at + p], qt_ref[...], ((1,), (0,))) * (SCALE * LOG2E)
        s = masked(raw, limits(counts, p))
        s_s[cross_at + p] = s
        return jnp.maximum(mx, fold(s, jnp.max))

    mx = lax.fori_loop(0, cross_pairs, scores, jnp.full((8, WIDE), NEG, jnp.float32))
    m = jnp.max(mx, axis=0, keepdims=True)
    m = jnp.maximum(m, jnp.maximum(own_max[...], row_max[...]))

    def expo(p, total):
        e = jnp.exp2(s_s[cross_at + p] - m)
        s_s[cross_at + p] = e
        return total + fold(e, jnp.sum)

    total = lax.fori_loop(0, cross_pairs, expo, jnp.zeros((8, WIDE), jnp.float32))
    own_f = jnp.exp2(own_max[...] - m)
    row_f = jnp.exp2(row_max[...] - m)
    total = jnp.sum(total, axis=0, keepdims=True) + own_sum[...] * own_f + row_sum[...] * row_f
    inv = 1.0 / total
    fac_s[0] = own_f * inv
    fac_s[1] = row_f * inv
    fac_s[2] = inv

    acc_s[...] = jnp.zeros_like(acc_s)

    def attend(p, carry):
        @pl.when(p < cross_at)
        def _():
            pltpu.make_async_copy(own_e.at[0], s_s.at[p], sems.at[p]).wait()

        kind = jnp.where(p < OWNP, 0, jnp.where(p < cross_at, 1, 2))
        prob = s_s[p] * fac_s[kind]
        s_s[p] = prob
        w = prob.astype(jnp.bfloat16)
        dv_s[p] = dot(w, g_ref[...], ((1,), (0,)))
        acc_s[...] += dot(vt_s[p], w, ((1,), (0,)))
        return carry

    lax.fori_loop(0, pairs, attend, 0)
    ot = acc_s[...].astype(jnp.bfloat16)
    delta = jnp.sum(
        gt_ref[...].astype(jnp.float32) * ot.astype(jnp.float32), axis=0, keepdims=True
    )

    def spread(ref, x):
        for i in range(NBL):
            for r in range(GROUP):
                at = (i * GROUP + r) * BLK
                ref[i * BLK:(i + 1) * BLK, r * HD:(r + 1) * HD] = x[:, at:at + BLK].T

    spread(o_ref, ot)
    acc_s[...] = jnp.zeros_like(acc_s)

    def back(p, carry):
        dprob = dot(v_s[p], gt_ref[...], ((1,), (0,)))
        ds = (s_s[p] * (dprob - delta)).astype(jnp.bfloat16)
        dk_s[p] = dot(ds, q_ref[...], ((1,), (0,)))
        acc_s[...] += dot(kt_s[p], ds, ((1,), (0,)))
        return carry

    lax.fori_loop(0, pairs, back, 0)
    spread(dq_ref, (acc_s[...] * SCALE).astype(jnp.bfloat16))

    def put(out_ref, place, p, half):
        dk = dk_s[p, pl.ds(half * BLK, BLK), :] * SCALE
        dv = dv_s[p, pl.ds(half * BLK, BLK), :]
        out_ref[place, :, 0] = dk.astype(jnp.bfloat16).reshape(2, BLK // 2, HD)
        out_ref[place, :, 1] = dv.astype(jnp.bfloat16).reshape(2, BLK // 2, HD)

    for j in range(NBL):
        put(row_grad_ref, info_ref[0, 1] - row_first + j, j // 2, j % 2)

    def put_row(p, carry):
        for half in range(2):
            slot = crossing + 2 * p + half

            @pl.when(slot < remote)
            def _():
                put(row_grad_ref, row_place(slot), OWNP + p, half)

        return carry

    lax.fori_loop(0, row_pairs, put_row, 0)

    def put_cross(p, carry):
        for half in range(2):
            slot = 2 * p + half

            @pl.when(slot < crossing)
            def _():
                put(cross_grad_s, info_ref[6, slot], cross_at + p, half)

        return carry

    lax.fori_loop(0, cross_pairs, put_cross, 0)
    at = 0
    for ref in (mine_grad_ref, next_grad_ref, last_grad_ref, far_grad_ref, near_grad_ref):
        ref[...] = cross_grad_s[at:at + ref.shape[0]]
        at += ref.shape[0]


VM = pl.BlockSpec(memory_space=pltpu.VMEM)
SM = pl.BlockSpec(memory_space=pltpu.SMEM)
ANY = pl.BlockSpec(memory_space=pl.ANY)
LIMIT = pltpu.CompilerParams(vmem_limit_bytes=58 << 20)


def like(shape, dtype=jnp.bfloat16):
    return jax.ShapeDtypeStruct(shape, dtype)


def own_part(info, q, g, own, within):
    line = like((1, WIDE), jnp.float32)
    return pl.pallas_call(
        own_kernel,
        out_shape=(
            like((WIDE, HD)), like((WIDE, HD)), like((HD, WIDE)), like((HD, WIDE)),
            like((OWNP, 2 * BLK, WIDE), jnp.float32), line, line,
        ),
        in_specs=[SM] + [VM] * 4,
        out_specs=(VM,) * 7,
        compiler_params=LIMIT,
    )(info, q, g, own, within)


def row_part(info, qt, row):
    line = like((1, WIDE), jnp.float32)
    tiles = (MAXD // 2, 2 * BLK, WIDE)
    return pl.pallas_call(
        row_kernel,
        out_shape=(like(tiles, jnp.float32), line, line),
        in_specs=[SM, VM, VM],
        out_specs=(ANY, VM, VM),
        scratch_shapes=[pltpu.VMEM(tiles, jnp.float32), pltpu.SemaphoreType.DMA((MAXD // 2,))],
        compiler_params=LIMIT,
    )(info, qt, row)


def last_part(info, q, own, row, cross, own_stuff, row_stuff):
    qs, gs, qt, gt, own_e, own_max, own_sum = own_stuff
    row_e, row_max, row_sum = row_stuff
    outs = tuple(like(a.shape) for a in (q, q, row, *cross))
    return pl.pallas_call(
        kernel,
        out_shape=outs,
        in_specs=[SM] + [VM] * (10 + len(cross)) + [ANY] * 2,
        out_specs=(VM,) * len(outs),
        scratch_shapes=[
            pltpu.VMEM((NPAIR, 2 * BLK, HD), jnp.bfloat16),
            pltpu.VMEM((NPAIR, 2 * BLK, HD), jnp.bfloat16),
            pltpu.VMEM((NPAIR, HD, 2 * BLK), jnp.bfloat16),
            pltpu.VMEM((NPAIR, HD, 2 * BLK), jnp.bfloat16),
            pltpu.VMEM((NPAIR, 2 * BLK, WIDE), jnp.float32),
            pltpu.VMEM((NPAIR, 2 * BLK, HD), jnp.float32),
            pltpu.VMEM((NPAIR, 2 * BLK, HD), jnp.float32),
            pltpu.VMEM((HD, WIDE), jnp.float32),
            pltpu.VMEM((3, 1, WIDE), jnp.float32),
            pltpu.VMEM((MAXD,) + own.shape[1:], jnp.bfloat16),
            pltpu.VMEM((MAXD,) + own.shape[1:], jnp.bfloat16),
            pltpu.SemaphoreType.DMA((NPAIR,)),
        ],
        compiler_params=LIMIT,
    )(info, qs, gs, qt, gt, own, row, *cross, own_max, own_sum, row_max, row_sum, own_e, row_e)


def pick_kernel(index_ref, from_ref, *outs):
    for k, out in enumerate(outs):
        for s in range(out.shape[0]):
            out[s] = from_ref[index_ref[k * out.shape[0] + s]]


def pick(index, pool, parts):
    vmem = pl.BlockSpec(memory_space=pltpu.VMEM)
    size = index.shape[0] // parts
    return pl.pallas_call(
        pick_kernel,
        out_shape=(jax.ShapeDtypeStruct((size,) + pool.shape[1:], pool.dtype),) * parts,
        in_specs=[pl.BlockSpec(memory_space=pltpu.SMEM), vmem],
        out_specs=(vmem,) * parts,
        compiler_params=pltpu.CompilerParams(vmem_limit_bytes=24 << 20),
    )(index, pool)


def merge_kernel(place_ref, valid_ref, row_ref, *rest):
    parts, out_ref = rest[:-1], rest[-1]
    out_ref[...] = row_ref[...]
    for k, part in enumerate(parts):
        for s in range(part.shape[0]):
            at = k * part.shape[0] + s

            @pl.when(valid_ref[at] > 0)
            def _():
                place = place_ref[at]
                both = out_ref[place].astype(jnp.float32) + part[s].astype(jnp.float32)
                out_ref[place] = both.astype(jnp.bfloat16)


YN = 4
ZN = 8
ROW = ZN * NBL
SETS = 4
SLOTS = MAXD // SETS
Z_GROUPS = [[y * ZN + z for z in range(ZN)] for y in range(YN)]


def along(x, k):
    pairs = [(y * ZN + z, y * ZN + (z + k) % ZN) for y in range(YN) for z in range(ZN)]
    return lax.ppermute(x, "ctx", pairs)


def up(x, k):
    pairs = [(y * ZN + z, (y + k) * ZN + z) for y in range(YN - k) for z in range(ZN)]
    return lax.ppermute(x, "ctx", pairs)


def down(x, k):
    pairs = [((y + k) * ZN + z, y * ZN + z) for y in range(YN - k) for z in range(ZN)]
    return lax.ppermute(x, "ctx", pairs)


def info_of(ancestors, c, y, z):
    first = c * NBL
    row_first = y * ROW
    lists = lax.dynamic_slice_in_dim(ancestors, first, NBL, 0)
    remote = jnp.sum(((lists >= 0) & (lists < first)).astype(jnp.int32), axis=1)
    crossing = jnp.sum(((lists[0] >= 0) & (lists[0] < row_first)).astype(jnp.int32))
    own = first + jnp.arange(NBL, dtype=jnp.int32)
    flags = jnp.any(lists[:, None, :] == own[None, :, None], axis=2).astype(jnp.int32)
    head = jnp.concatenate(
        [jnp.stack([remote[0], first, row_first, crossing]), jnp.zeros((MAXD - 4,), jnp.int32)]
    )[None]
    rest = jnp.concatenate([remote[:, None], flags, jnp.zeros((NBL, MAXD - 1 - NBL), jnp.int32)], axis=1)
    slot = jnp.arange(MAXD, dtype=jnp.int32)
    turn = (slot // SLOTS - z) % SETS
    base = jnp.array([0, SLOTS, 3 * SLOTS, 2 * SLOTS], jnp.int32)
    place = (base[turn] + slot % SLOTS)[None]
    return jnp.concatenate([head, lists[:1], rest, place], axis=0)


def body(queries, keys, values, out_grad, ancestors, parents):
    tokens = queries.shape[0]
    groups = keys.shape[1]
    c = lax.axis_index("ctx")
    y = c // ZN
    z = c % ZN
    row_lists = ancestors[::ROW]
    slots = lax.dynamic_slice_in_dim(row_lists, (z % SETS) * SLOTS, SLOTS, 1)
    slot_rows = jnp.where(slots >= 0, slots // ROW, -1)
    my_rows = lax.dynamic_index_in_dim(slot_rows, y, 0, keepdims=False)

    kv = jnp.stack([keys, values]).transpose(2, 0, 1, 3)
    kv = lax.all_to_all(kv, "head", split_axis=0, concat_axis=0, tiled=True)
    own = kv.reshape(NBL, 2, 2, BLK // 2, HD)
    row = lax.all_gather(own, "ctx", axis=0, axis_index_groups=Z_GROUPS, tiled=True)
    q = lax.all_to_all(queries.reshape(tokens, -1), "head", split_axis=1, concat_axis=0, tiled=True)
    g = lax.all_to_all(out_grad.reshape(tokens, -1), "head", split_axis=1, concat_axis=0, tiled=True)

    row, q, g = lax.optimization_barrier((row, q, g))

    def of_row(k):
        return lax.dynamic_index_in_dim(slots, jnp.minimum(y + k, YN - 1), 0, keepdims=False)

    within = tree_reach_t(parents)
    info = info_of(ancestors, c, y, z)
    wanted = [jnp.clip(of_row(k) - y * ROW, 0, ROW - 1) for k in range(1, YN)]
    sent = pick(jnp.concatenate(wanted), row, YN - 1)
    sent, q, g = lax.optimization_barrier((sent, q, g))
    moved = [up(sent[k - 1], k) for k in range(1, YN)]
    own_stuff = own_part(info, q, g, own, within)
    moved, own_stuff = lax.optimization_barrier((moved, own_stuff))
    mine = jnp.zeros((SLOTS,) + own.shape[1:], own.dtype)
    for k in range(1, YN):
        here = (my_rows == y - k)[:, None, None, None, None]
        mine = jnp.where(here, moved[k - 1], mine)
    half = SLOTS // 2
    cross = (mine, along(mine, -1), along(mine, 1), along(mine[:half], -2), along(mine[half:], 2))
    row_stuff = row_part(info, own_stuff[2], row)
    o, dq, row_grad, *turns = last_part(info, q, own, row, cross, own_stuff, row_stuff)

    here = turns[0].astype(jnp.float32)
    here = here + along(turns[1], 1).astype(jnp.float32) + along(turns[2], -1).astype(jnp.float32)
    far = jnp.concatenate([along(turns[3], 2), along(turns[4], -2)], axis=0)
    here = (here + far.astype(jnp.float32)).astype(jnp.bfloat16)
    places, valids, parts = [], [], []
    for k in range(1, YN):
        parts.append(down(here, k))
        theirs = of_row(k)
        valid = (theirs >= 0) & (theirs // ROW == y) & (y + k < YN)
        places.append(jnp.where(valid, theirs - y * ROW, 0))
        valids.append(valid.astype(jnp.int32))
    vmem = pl.BlockSpec(memory_space=pltpu.VMEM)
    smem = pl.BlockSpec(memory_space=pltpu.SMEM)
    row_grad = pl.pallas_call(
        merge_kernel,
        out_shape=jax.ShapeDtypeStruct(row_grad.shape, row_grad.dtype),
        in_specs=[smem, smem] + [vmem] * YN,
        out_specs=vmem,
        compiler_params=pltpu.CompilerParams(vmem_limit_bytes=24 << 20),
    )(jnp.concatenate(places), jnp.concatenate(valids), row_grad, *parts)
    row_grad, o, dq = lax.optimization_barrier((row_grad, o, dq))
    grad = lax.psum_scatter(
        row_grad, "ctx", scatter_dimension=0, axis_index_groups=Z_GROUPS, tiled=True
    )
    o = lax.all_to_all(o, "head", split_axis=0, concat_axis=1, tiled=True)
    dq = lax.all_to_all(dq, "head", split_axis=0, concat_axis=1, tiled=True)
    grad, o, dq = lax.optimization_barrier((grad, o, dq))
    grad = grad.reshape(groups, 2, BLK // 2, HD)
    grad = lax.all_to_all(grad, "head", split_axis=0, concat_axis=0, tiled=True)
    grad = grad.transpose(1, 2, 0, 3)
    shape = queries.shape
    return (o.reshape(shape), dq.reshape(shape), grad[0], grad[1])


def solution(mesh):
    rows = P(("ctx", "head"), None, None)
    return jax.shard_map(
        body,
        mesh=mesh,
        in_specs=(rows, rows, rows, rows, P(), P("ctx", None)),
        out_specs=(rows, rows, rows, rows),
        check_vma=False,
    )
```

time: 217 us -> 214 us (0.986); the launches traced: 215 us -> 215 us
  waiting for transfers between devices: 79.3 us -> 60.3 us
  Pallas kernels: 12.8 us -> 22.2 us
  starting transfers between devices: 55.4 us -> 61.7 us
  blocking collectives: 32.7 us -> 36.1 us
    ppermute x3, waiting for transfers between devices: 20.1 us -> 9.27 us  [down(): return lax.ppermute(x, 'ctx', pairs)]
    pallas_call x1 -> x3, Pallas kernels: 10.1 us -> 19.4 us  [the longest x1 10.8 us: last_part(): pl.pallas_call(kernel, out_shape=outs, in_specs=[SM] + [VM] * (10 + len(c...]
    ppermute x8, waiting for transfers between devices: 12.5 us -> 5.75 us  [along(): return lax.ppermute(x, 'ctx', pairs)]
    ppermute x8, starting transfers between devices: 21.2 us -> 27 us  [along(): return lax.ppermute(x, 'ctx', pairs)]
    all_to_all x1, blocking collectives: 19.9 us -> 23.3 us  [body(): o = lax.all_to_all(o, 'head', split_axis=0, concat_axis=1, tiled=True)]
    reduce_scatter x1, waiting for transfers between devices: 5.11 us -> 8.11 us  [body(): lax.psum_scatter(row_grad, 'ctx', scatter_dimension=0, axis_index_groups=...]
    ppermute x3, waiting for transfers between devices: 2.87 us -> 0.01 us  [up(): return lax.ppermute(x, 'ctx', pairs)]
  transfers between devices with their start and end apart: 20 -> 20, of which waited for: 13 -> 12; matrix products, arithmetic and copies ran while one was open for 5% -> 5% of each run, Pallas kernels for 0% -> 4%
where the time goes in v4:
time: 214 us; the launch traced here: 215 us
  starting transfers between devices  61.7 us (29%)
  waiting for transfers between devices  60.3 us (28%)
  blocking collectives  36.1 us (17%)
  Pallas kernels  22.2 us (10%)
  local copies, waits for them, and re-layouts  14.4 us (7%)
  between operations  14.4 us (7%)
  other arithmetic  3.48 us (2%)
    ppermute x8, starting transfers between devices, along(): return lax.ppermute(x, 'ctx', pairs)  27 us
    all_to_all x1, blocking collectives, body(): o = lax.all_to_all(o, 'head', split_axis=0, concat_axis=1, tiled=True)  23.3 us
    all_to_all x1, blocking collectives, body(): kv = lax.all_to_all(kv, 'head', split_axis=0, concat_axis=0, tiled=True)  12.8 us
    all_to_all x1, waiting for transfers between devices, body(): dq = lax.all_to_all(dq, 'head', split_axis=0, concat_axis=1, tiled=True)  10.8 us
    pallas_call x1, Pallas kernels, last_part(): pl.pallas_call(kernel, out_shape=outs, in_specs=[SM] + [VM] * (10 + len(c...  10.8 us
    all_to_all x1, waiting for transfers between devices, body(): lax.all_to_all(out_grad.reshape(tokens, -1), 'head', split_axis=1, concat...  10.1 us
    ppermute x3, waiting for transfers between devices, down(): return lax.ppermute(x, 'ctx', pairs)  9.27 us
    ppermute x3, starting transfers between devices, up(): return lax.ppermute(x, 'ctx', pairs)  8.79 us
  transfers between devices with their start and end apart: 20, of which 12 were waited for; matrix products, arithmetic and copies ran while one was open for 5% of the time, Pallas kernels for 4%

profile of v4, /device:TPU:1, one launch (start us, length us, event | category | flops | bytes accessed | tf_op | source)
XLA Modules:
  0.0 214.6 jit_solution(9930185318580083107)
XLA Ops:
  7.2 1.1 copy_bitcast_fusion
  8.3 12.8 %all_to_all.86 = bf16[8,2,64,128]{3,2,1,0:T(8,128)(2,1)} all-to-all(bf16[8,2,64,128]{3,2,1,0:T(8,128)(2,1)S(1)} %maximum_bitcast_fusion), channel_id=1, replica_groups=mesh['ctx'=32,'head'=8] {'head'}, dimensions={0} | all-to-all | bytes 524288 | tf_op jit(solution)/shard_map/all_to_all | solution.py:459
  21.2 0.5 all_to_all.63
  21.7 0.9 copy.39
  22.6 4.6 %all-to-all-start.1 = ((bf16[64,8,640]{2,0,1:T(8,128)(2,1)}), bf16[64,8,640]{2,0,1:T(8,128)(2,1)S(1)}, u32[]{:S(2)}, u32[]{:S(2)}) async-start(bf16[64,8,640]{2,0,1:T(8,128)(2,1)} %copy.39), calls=%async_computation.1 | async-start | bytes 1310720 | tf_op jit(solution)/shard_map/all_to_all | solution.py:462
  27.7 0.2 compare_reduce_fusion
  27.9 0.7 gather_fusion
  28.6 0.6 fusion.23
  29.2 0.8 concatenate.26
  30.0 0.2 dynamic-slice_reduce_fusion.2
  30.3 0.7 pad_add_fusion.info_ref
  31.0 0.5 all_to_all.67
  31.4 0.9 copy.40
  32.4 0.4 fusion.1
  32.8 5.3 %all-to-all-done.1 = bf16[64,8,640]{2,0,1:T(8,128)(2,1)S(1)} async-done(((bf16[64,8,640]{2,0,1:T(8,128)(2,1)}), bf16[64,8,640]{2,0,1:T(8,128)(2,1)S(1)}, u32[]{:S(2)}, u32[]{:S(2)}) %all-to-all-start.1) | async-done | bytes 655392 | tf_op jit(solution)/shard_map/all_to_all | solution.py:462
  38.1 4.3 %all-to-all-start.2 = ((bf16[64,8,640]{2,0,1:T(8,128)(2,1)}), bf16[64,8,640]{2,0,1:T(8,128)(2,1)S(1)}, u32[]{:S(2)}, u32[]{:S(2)}) async-start(bf16[64,8,640]{2,0,1:T(8,128)(2,1)} %copy.40), calls=%async_computation.2 | async-start | bytes 1310720 | tf_op jit(solution)/shard_map/all_to_all | solution.py:463
  42.5 0.4 fusion.3
  42.9 0.4 fusion.5
  43.3 10.1 %all-to-all-done.2 = bf16[64,8,640]{2,0,1:T(8,128)(2,1)S(1)} async-done(((bf16[64,8,640]{2,0,1:T(8,128)(2,1)}), bf16[64,8,640]{2,0,1:T(8,128)(2,1)S(1)}, u32[]{:S(2)}, u32[]{:S(2)}) %all-to-all-start.2) | async-done | bytes 655392 | tf_op jit(solution)/shard_map/all_to_all | solution.py:463
  53.3 6.3 %all-gather.2.cloned.1.call-done.from_ref.row_ref = bf16[32,2,2,64,128]{4,3,2,1,0:T(8,128)(2,1)} async-done(((bf16[4,2,2,64,128]{4,3,2,1,0:T(8,128)(2,1)}), bf16[32,2,2,64,128]{4,3,2,1,0:T(8,128)(2,1)}) %all-gather.2.cloned.1.call-update) | async-done | bytes 2097168 | tf_op jit(solution)/shard_map/all_gather | solution.py:461
  59.6 1.6 copy-done
  61.2 0.6 shard_map.102
  61.8 3.2 %collective-permute-start = (bf16[4,2,2,64,128]{4,3,2,1,0:T(8,128)(2,1)S(1)}, bf16[4,2,2,64,128]{4,3,2,1,0:T(8,128)(2,1)S(1)}, u32[]{:S(2)}, u32[]{:S(2)}) collective-permute-start(bf16[4,2,2,64,128]{4,3,2,1,0:T(8,128)(2,1)S(1)} %get-tuple-element.55), channel_id=1, source_target_pairs={{0,64},{8,72},{16,80},{24,88},{32,96},{40,104},{48,112},{56,120},{... | collective-permute-start | bytes 786440 | tf_op jit(solution)/shard_map/ppermute | solution.py:420
  65.0 4.3 %collective-permute-start.1 = (bf16[4,2,2,64,128]{4,3,2,1,0:T(8,128)(2,1)S(1)}, bf16[4,2,2,64,128]{4,3,2,1,0:T(8,128)(2,1)S(1)}, u32[]{:S(2)}, u32[]{:S(2)}) collective-permute-start(bf16[4,2,2,64,128]{4,3,2,1,0:T(8,128)(2,1)S(1)} %get-tuple-element.56), channel_id=1, source_target_pairs={{0,128},{8,136},{16,144},{24,152},{32,160},{40,168},{48,176},{56,1... | collective-permute-start | bytes 786440 | tf_op jit(solution)/shard_map/ppermute | solution.py:420
  69.3 1.3 collective-permute-start.2
  70.7 0.2 compare_reduce_fusion.3
  70.9 0.9 fusion.7.within_ref
  71.8 6.0 %shard_map.103 = (bf16[2560,128]{1,0:T(8,128)(2,1)}, bf16[2560,128]{1,0:T(8,128)(2,1)}, bf16[128,2560]{1,0:T(8,128)(2,1)}, bf16[128,2560]{1,0:T(8,128)(2,1)}, f3...) custom-call(s32[7,16]{1,0:T(8,128)} %pad_add_fusion.info_ref, bf16[512,640]{1,0:T(8,128)(2,1)} %bitcast.50, ...), custom_call_target="tpu_custom_call" | custom-call | tf_op jit(solution)/shard_map/pallas_call | solution.py:321
  77.8 0.1 select_select_fusion.mine_ref
  77.9 0.4 collective-permute-start.4
  78.3 2.4 %collective-permute-start.3 = (bf16[4,2,2,64,128]{4,3,2,1,0:T(8,128)(2,1)S(1)}, bf16[4,2,2,64,128]{4,3,2,1,0:T(8,128)(2,1)S(1)}, u32[]{:S(2)}, u32[]{:S(2)}) collective-permute-start(bf16[4,2,2,64,128]{4,3,2,1,0:T(8,128)(2,1)S(1)} %select_select_fusion.mine_ref), channel_id=1, source_target_pairs={{0,56},{8,0},{16,8},{24,16},{32,24},{40,32},{48,40},{56,48},{64,12... | collective-permute-start | bytes 786440 | tf_op jit(solution)/shard_map/ppermute | solution.py:415
  80.7 0.6 collective-permute-start.6
  81.3 3.0 %collective-permute-start.5 = (bf16[2,2,2,64,128]{4,3,2,1,0:T(8,128)(2,1)S(1)}, bf16[2,2,2,64,128]{4,3,2,1,0:T(8,128)(2,1)S(1)}, u32[]{:S(2)}, u32[]{:S(2)}) collective-permute-start(bf16[2,2,2,64,128]{4,3,2,1,0:T(8,128)(2,1)S(1)} %get-tuple-element.117), channel_id=1, source_target_pairs={{0,48},{8,56},{16,0},{24,8},{32,16},{40,24},{48,32},{56,40},{64,11... | collective-permute-start | bytes 393224 | tf_op jit(solution)/shard_map/ppermute | solution.py:415
  84.4 2.6 %shard_map.104 = (f32[8,256,2560]{2,1,0:T(8,128)}, f32[1,2560]{1,0:T(1,128)}, f32[1,2560]{1,0:T(1,128)}) custom-call(s32[7,16]{1,0:T(8,128)} %pad_add_fusion.info_ref, bf16[128,2560]{1,0:T(8,128)(2,1)} %get-tuple-element.69.qt_ref, bf16[32,2,2,64,128]{4,3,2,1,0:T(8,128)(2,1)} %all-gather.2.cloned.1.call-done.from_ref.row_ref), custom_call_target="tpu_custom_call" | custom-call | tf_op jit(solution)/shard_map/pallas_call | solution.py:336
  86.9 1.3 collective-permute-done.6.near_ref
  88.2 0.4 collective-permute-done.5.far_ref
  88.7 0.2 copy-done.11
  88.9 0.4 copy-done.12
  89.5 10.8 %shard_map.105 = (bf16[512,640]{1,0:T(8,128)(2,1)}, bf16[512,640]{1,0:T(8,128)(2,1)}, bf16[32,2,2,64,128]{4,3,2,1,0:T(8,128)(2,1)}, bf16[4,2,2,64,128]{4,3,2,1,0...) custom-call(s32[7,16]{1,0:T(8,128)} %pad_add_fusion.info_ref, ...), custom_call_target="tpu_custom_call" | custom-call | tf_op jit(solution)/shard_map/pallas_call | solution.py:350
  100.3 5.0 %collective-permute-start.7 = (bf16[4,2,2,64,128]{4,3,2,1,0:T(8,128)(2,1)}, bf16[4,2,2,64,128]{4,3,2,1,0:T(8,128)(2,1)S(1)}, u32[]{:S(2)}, u32[]{:S(2)}) collective-permute-start(bf16[4,2,2,64,128]{4,3,2,1,0:T(8,128)(2,1)} %get-tuple-element.82), channel_id=1, source_target_pairs={{0,8},{8,16},{16,24},{24,32},{32,40},{40,48},{48,56},{56,0},{64,72... | collective-permute-start | bytes 786440 | tf_op jit(solution)/shard_map/ppermute | solution.py:415
  105.3 12.0 %collective-permute-start.8 = (bf16[4,2,2,64,128]{4,3,2,1,0:T(8,128)(2,1)}, bf16[4,2,2,64,128]{4,3,2,1,0:T(8,128)(2,1)S(1)}, u32[]{:S(2)}, u32[]{:S(2)}) collective-permute-start(bf16[4,2,2,64,128]{4,3,2,1,0:T(8,128)(2,1)} %get-tuple-element.83), channel_id=1, source_target_pairs={{0,56},{8,0},{16,8},{24,16},{32,24},{40,32},{48,40},{56,48},{64,12... | collective-permute-start | bytes 786440 | tf_op jit(solution)/shard_map/ppermute | solution.py:415
  117.3 0.7 collective-permute-start.9
  118.0 2.9 %collective-permute-start.10 = (bf16[2,2,2,64,128]{4,3,2,1,0:T(8,128)(2,1)}, bf16[2,2,2,64,128]{4,3,2,1,0:T(8,128)(2,1)S(1)}, u32[]{:S(2)}, u32[]{:S(2)}) collective-permute-start(bf16[2,2,2,64,128]{4,3,2,1,0:T(8,128)(2,1)} %get-tuple-element.85), channel_id=1, source_target_pairs={{0,48},{8,56},{16,0},{24,8},{32,16},{40,24},{48,32},{56,40},{64,11... | collective-permute-start | bytes 393224 | tf_op jit(solution)/shard_map/ppermute | solution.py:415
  120.9 3.5 %collective-permute-done.9 = bf16[2,2,2,64,128]{4,3,2,1,0:T(8,128)(2,1)S(1)} collective-permute-done((bf16[2,2,2,64,128]{4,3,2,1,0:T(8,128)(2,1)}, bf16[2,2,2,64,128]{4,3,2,1,0:T(8,128)(2,1)S(1)}, u32[]{:S(2)}, u32[]{:S(2)}) %collective-permute-start.9) | collective-permute-done | bytes 131104 | tf_op jit(solution)/shard_map/ppermute | solution.py:415
  124.4 0.5 collective-permute-done.10
  124.9 1.1 add_convert_fusion
  126.1 1.3 collective-permute-start.13
  127.4 1.3 collective-permute-start.12
  128.7 1.3 collective-permute-start.11
  130.1 8.7 %collective-permute-done.13.rest_2_ = bf16[4,2,2,64,128]{4,3,2,1,0:T(8,128)(2,1)S(1)} collective-permute-done((bf16[4,2,2,64,128]{4,3,2,1,0:T(8,128)(2,1)S(1)}, bf16[4,2,2,64,128]{4,3,2,1,0:T(8,128)(2,1)S(1)}, u32[]{:S(2)}, u32[]{:S(2)}) %collective-permute-start.13) | collective-permute-done | bytes 262176 | tf_op jit(solution)/shard_map/ppermute | solution.py:425
  138.8 0.6 collective-permute-done.11.rest_0_
  139.4 1.6 copy-done.1
  141.0 2.2 %shard_map.106 = bf16[32,2,2,64,128]{4,3,2,1,0:T(8,128)(2,1)} custom-call(s32[12]{0:T(128)S(1)} %pad_add_fusion.1.place_ref, s32[12]{0:T(128)S(1)} %add_convert_fusion.1.valid_ref, bf16[32,2,2,64,128]{4,3,2,1,0:T(8,128)(2,1)S(1)} %copy-done.1, bf16[4,2,2,64,128]{4,3,2,1,0:T(8,128)(2,1)S(1)} %collective-permute-done.11.rest_0_, ...), custom_call_target="tpu_custom_call" | custom-call | tf_op jit(solution)/shard_map/pallas_call | solution.py:500
  143.2 1.1 copy-done.8
  144.3 23.3 %all_to_all.87 = bf16[8,64,640]{2,1,0:T(8,128)(2,1)S(1)} all-to-all(bf16[8,64,640]{2,1,0:T(8,128)(2,1)S(1)} %bitcast.57), channel_id=1, replica_groups=mesh['ctx'=32,'head'=8] {'head'}, dimensions={0} | all-to-all | bytes 1310720 | tf_op jit(solution)/shard_map/all_to_all | solution.py:511
  167.6 4.3 %all-to-all-start.4 = ((bf16[8,64,640]{2,1,0:T(8,128)(2,1)}), bf16[8,64,640]{2,1,0:T(8,128)(2,1)S(1)}, u32[]{:S(2)}, u32[]{:S(2)}) async-start(bf16[8,64,640]{2,1,0:T(8,128)(2,1)} %bitcast.17), calls=%async_computation.5 | async-start | bytes 1310720 | tf_op jit(solution)/shard_map/all_to_all | solution.py:512
  171.9 10.8 %all-to-all-done.4 = bf16[8,64,640]{2,1,0:T(8,128)(2,1)S(1)} async-done(((bf16[8,64,640]{2,1,0:T(8,128)(2,1)}), bf16[8,64,640]{2,1,0:T(8,128)(2,1)S(1)}, u32[]{:S(2)}, u32[]{:S(2)}) %all-to-all-start.4) | async-done | bytes 655392 | tf_op jit(solution)/shard_map/all_to_all | solution.py:512
  182.9 8.1 %reduce-scatter.2.cloned.1.call-done = bf16[4,2,2,64,128]{4,3,2,1,0:T(8,128)(2,1)} async-done(((bf16[32,2,2,64,128]{4,3,2,1,0:T(8,128)(2,1)}), bf16[4,2,2,64,128]{4,3,2,1,0:T(8,128)(2,1)}) %reduce-scatter.2.cloned.1.call-update) | async-done | bytes 262160 | tf_op jit(solution)/shard_map/reduce_scatter | solution.py:508
  191.0 8.8 %all-to-all-start.5 = ((bf16[8,2,64,128]{3,2,1,0:T(8,128)(2,1)}), bf16[8,2,64,128]{3,2,1,0:T(8,128)(2,1)S(1)}, u32[]{:S(2)}, u32[]{:S(2)}) async-start(bf16[8,2,64,128]{3,2,1,0:T(8,128)(2,1)} %bitcast.60), calls=%async_computation.6 | async-start | bytes 524288 | tf_op jit(solution)/shard_map/all_to_all | solution.py:515
  199.7 0.9 copy.48
  200.7 0.9 copy.49
  201.6 4.6 %all-to-all-done.5 = bf16[8,2,64,128]{3,2,1,0:T(8,128)(2,1)S(1)} async-done(((bf16[8,2,64,128]{3,2,1,0:T(8,128)(2,1)}), bf16[8,2,64,128]{3,2,1,0:T(8,128)(2,1)S(1)}, u32[]{:S(2)}, u32[]{:S(2)}) %all-to-all-start.5) | async-done | bytes 262176 | tf_op jit(solution)/shard_map/all_to_all | solution.py:515
  206.3 0.7 copy.44
  207.0 0.7 copy.43
  (61 shorter events, 1.3 us)
Async XLA Ops:
  7.2 14.0 %copy-start.6 = (bf16[64,40,128]{2,1,0:T(8,128)(2,1)S(1)}, bf16[64,40,128]{2,1,0:T(8,128)(2,1)}, u32[]{:S(2)}) copy-start(bf16[64,40,128]{2,1,0:T(8,128)(2,1)} %param.7) | copy-start | bytes 1966084
  7.2 52.4 %all-gather.2.cloned.1.call-start = ((), (), s32[]{:S(2)}) async-start(), calls=%async_computation.7 | async-start | bytes 2359296 | tf_op jit(solution)/shard_map/all_gather | solution.py:461
  21.1 6.1 %copy-start.13 = (s32[128,16]{0,1:T(8,128)S(1)}, s32[128,16]{0,1:T(8,128)}, u32[]{:S(2)}) copy-start(s32[128,16]{0,1:T(8,128)} %param.11) | copy-start | bytes 24580
  21.2 6.8 %copy-start.2 = (s32[4]{0:T(128)S(1)}, s32[4]{0:T(128)}, u32[]{:S(2)}) copy-start(s32[4]{0:T(128)} %constant.182.clone) | copy-start | bytes 52
  21.2 9.8 %copy-start.7 = (bf16[64,40,128]{2,1,0:T(8,128)(2,1)S(1)}, bf16[64,40,128]{2,1,0:T(8,128)(2,1)}, u32[]{:S(2)}) copy-start(bf16[64,40,128]{2,1,0:T(8,128)(2,1)} %param.10) | copy-start | bytes 1966084
  22.6 9.8 %copy-start.14 = (s32[4,128]{1,0:T(4,128)S(1)}, s32[4,128]{1,0:T(4,128)}, u32[]{:S(2)}) copy-start(s32[4,128]{1,0:T(4,128)} %param.12) | copy-start | bytes 6148
  22.6 15.5 %all-to-all-start.1 = ((bf16[64,8,640]{2,0,1:T(8,128)(2,1)}), bf16[64,8,640]{2,0,1:T(8,128)(2,1)S(1)}, u32[]{:S(2)}, u32[]{:S(2)}) async-start(bf16[64,8,640]{2,0,1:T(8,128)(2,1)} %copy.39), calls=%async_computation.1 | async-start | bytes 1310720 | tf_op jit(solution)/shard_map/all_to_all | solution.py:462
  38.1 23.7 %copy-start.3 = (bf16[64,8,640]{2,0,1:T(8,128)(2,1)}, bf16[64,8,640]{2,0,1:T(8,128)(2,1)S(1)}, u32[]{:S(2)}) copy-start(bf16[64,8,640]{2,0,1:T(8,128)(2,1)S(1)} %all-to-all-done.1) | copy-start | bytes 1966084
  38.1 15.2 %all-to-all-start.2 = ((bf16[64,8,640]{2,0,1:T(8,128)(2,1)}), bf16[64,8,640]{2,0,1:T(8,128)(2,1)S(1)}, u32[]{:S(2)}, u32[]{:S(2)}) async-start(bf16[64,8,640]{2,0,1:T(8,128)(2,1)} %copy.40), calls=%async_computation.2 | async-start | bytes 1310720 | tf_op jit(solution)/shard_map/all_to_all | solution.py:463
  42.4 148.5 %reduce-scatter.2.cloned.1.call-start = ((), (), s32[]{:S(2)}) async-start(), calls=%async_computation.8 | async-start | bytes 2359296 | tf_op jit(solution)/shard_map/reduce_scatter | solution.py:508
  53.3 18.4 %copy-start.4 = (bf16[64,8,640]{2,0,1:T(8,128)(2,1)}, bf16[64,8,640]{2,0,1:T(8,128)(2,1)S(1)}, u32[]{:S(2)}) copy-start(bf16[64,8,640]{2,0,1:T(8,128)(2,1)S(1)} %all-to-all-done.2) | copy-start | bytes 1966084
  59.6 1.6 copy-start
  61.8 15.9 %collective-permute-start = (bf16[4,2,2,64,128]{4,3,2,1,0:T(8,128)(2,1)S(1)}, bf16[4,2,2,64,128]{4,3,2,1,0:T(8,128)(2,1)S(1)}, u32[]{:S(2)}, u32[]{:S(2)}) collective-permute-start(bf16[4,2,2,64,128]{4,3,2,1,0:T(8,128)(2,1)S(1)} %get-tuple-element.55), channel_id=1, source_target_pairs={{0,64},{8,72},{16,80},{24,88},{32,96},{40,104},{48,112},{56,120},{... | collective-permute-start | bytes 786440 | tf_op jit(solution)/shard_map/ppermute | solution.py:420
  65.0 12.8 %collective-permute-start.1 = (bf16[4,2,2,64,128]{4,3,2,1,0:T(8,128)(2,1)S(1)}, bf16[4,2,2,64,128]{4,3,2,1,0:T(8,128)(2,1)S(1)}, u32[]{:S(2)}, u32[]{:S(2)}) collective-permute-start(bf16[4,2,2,64,128]{4,3,2,1,0:T(8,128)(2,1)S(1)} %get-tuple-element.56), channel_id=1, source_target_pairs={{0,128},{8,136},{16,144},{24,152},{32,160},{40,168},{48,176},{56,1... | collective-permute-start | bytes 786440 | tf_op jit(solution)/shard_map/ppermute | solution.py:420
  69.3 8.5 %collective-permute-start.2 = (bf16[4,2,2,64,128]{4,3,2,1,0:T(8,128)(2,1)S(1)}, bf16[4,2,2,64,128]{4,3,2,1,0:T(8,128)(2,1)S(1)}, u32[]{:S(2)}, u32[]{:S(2)}) collective-permute-start(bf16[4,2,2,64,128]{4,3,2,1,0:T(8,128)(2,1)S(1)} %get-tuple-element.57), channel_id=1, source_target_pairs={{0,192},{8,200},{16,208},{24,216},{32,224},{40,232},{48,240},{56,2... | collective-permute-start | bytes 786440 | tf_op jit(solution)/shard_map/ppermute | solution.py:420
  77.9 10.7 %copy-start.5 = (bf16[4,2,2,64,128]{4,3,2,1,0:T(8,128)(2,1)}, bf16[4,2,2,64,128]{4,3,2,1,0:T(8,128)(2,1)S(1)}, u32[]{:S(2)}) copy-start(bf16[4,2,2,64,128]{4,3,2,1,0:T(8,128)(2,1)S(1)} %select_select_fusion.mine_ref) | copy-start | bytes 786436
  77.9 10.7 %collective-permute-start.4 = (bf16[4,2,2,64,128]{4,3,2,1,0:T(8,128)(2,1)S(1)}, bf16[4,2,2,64,128]{4,3,2,1,0:T(8,128)(2,1)S(1)}, u32[]{:S(2)}, u32[]{:S(2)}) collective-permute-start(bf16[4,2,2,64,128]{4,3,2,1,0:T(8,128)(2,1)S(1)} %select_select_fusion.mine_ref), channel_id=1, source_target_pairs={{0,8},{8,16},{16,24},{24,32},{32,40},{40,48},{48,56},{56,0},{64,72... | collective-permute-start | bytes 786440 | tf_op jit(solution)/shard_map/ppermute | solution.py:415
  78.3 10.3 %collective-permute-start.3 = (bf16[4,2,2,64,128]{4,3,2,1,0:T(8,128)(2,1)S(1)}, bf16[4,2,2,64,128]{4,3,2,1,0:T(8,128)(2,1)S(1)}, u32[]{:S(2)}, u32[]{:S(2)}) collective-permute-start(bf16[4,2,2,64,128]{4,3,2,1,0:T(8,128)(2,1)S(1)} %select_select_fusion.mine_ref), channel_id=1, source_target_pairs={{0,56},{8,0},{16,8},{24,16},{32,24},{40,32},{48,40},{56,48},{64,12... | collective-permute-start | bytes 786440 | tf_op jit(solution)/shard_map/ppermute | solution.py:415
  80.7 7.5 %collective-permute-start.6 = (bf16[2,2,2,64,128]{4,3,2,1,0:T(8,128)(2,1)S(1)}, bf16[2,2,2,64,128]{4,3,2,1,0:T(8,128)(2,1)S(1)}, u32[]{:S(2)}, u32[]{:S(2)}) collective-permute-start(bf16[2,2,2,64,128]{4,3,2,1,0:T(8,128)(2,1)S(1)} %get-tuple-element.116), channel_id=1, source_target_pairs={{0,16},{8,24},{16,32},{24,40},{32,48},{40,56},{48,0},{56,8},{64,80... | collective-permute-start | bytes 393224 | tf_op jit(solution)/shard_map/ppermute | solution.py:415
  81.3 7.3 %collective-permute-start.5 = (bf16[2,2,2,64,128]{4,3,2,1,0:T(8,128)(2,1)S(1)}, bf16[2,2,2,64,128]{4,3,2,1,0:T(8,128)(2,1)S(1)}, u32[]{:S(2)}, u32[]{:S(2)}) collective-permute-start(bf16[2,2,2,64,128]{4,3,2,1,0:T(8,128)(2,1)S(1)} %get-tuple-element.117), channel_id=1, source_target_pairs={{0,48},{8,56},{16,0},{24,8},{32,16},{40,24},{48,32},{56,40},{64,11... | collective-permute-start | bytes 393224 | tf_op jit(solution)/shard_map/ppermute | solution.py:415
  88.2 0.7 copy-start.11
  88.6 0.7 copy-start.12
  88.6 0.7 copy-start.9
  88.6 0.8 copy-start.10
  100.3 24.6 %collective-permute-start.7 = (bf16[4,2,2,64,128]{4,3,2,1,0:T(8,128)(2,1)}, bf16[4,2,2,64,128]{4,3,2,1,0:T(8,128)(2,1)S(1)}, u32[]{:S(2)}, u32[]{:S(2)}) collective-permute-start(bf16[4,2,2,64,128]{4,3,2,1,0:T(8,128)(2,1)} %get-tuple-element.82), channel_id=1, source_target_pairs={{0,8},{8,16},{16,24},{24,32},{32,40},{40,48},{48,56},{56,0},{64,72... | collective-permute-start | bytes 786440 | tf_op jit(solution)/shard_map/ppermute | solution.py:415
  105.3 19.6 %collective-permute-start.8 = (bf16[4,2,2,64,128]{4,3,2,1,0:T(8,128)(2,1)}, bf16[4,2,2,64,128]{4,3,2,1,0:T(8,128)(2,1)S(1)}, u32[]{:S(2)}, u32[]{:S(2)}) collective-permute-start(bf16[4,2,2,64,128]{4,3,2,1,0:T(8,128)(2,1)} %get-tuple-element.83), channel_id=1, source_target_pairs={{0,56},{8,0},{16,8},{24,16},{32,24},{40,32},{48,40},{56,48},{64,12... | collective-permute-start | bytes 786440 | tf_op jit(solution)/shard_map/ppermute | solution.py:415
  117.3 7.1 %collective-permute-start.9 = (bf16[2,2,2,64,128]{4,3,2,1,0:T(8,128)(2,1)}, bf16[2,2,2,64,128]{4,3,2,1,0:T(8,128)(2,1)S(1)}, u32[]{:S(2)}, u32[]{:S(2)}) collective-permute-start(bf16[2,2,2,64,128]{4,3,2,1,0:T(8,128)(2,1)} %get-tuple-element.84), channel_id=1, source_target_pairs={{0,16},{8,24},{16,32},{24,40},{32,48},{40,56},{48,0},{56,8},{64,80... | collective-permute-start | bytes 393224 | tf_op jit(solution)/shard_map/ppermute | solution.py:415
  118.0 6.9 %collective-permute-start.10 = (bf16[2,2,2,64,128]{4,3,2,1,0:T(8,128)(2,1)}, bf16[2,2,2,64,128]{4,3,2,1,0:T(8,128)(2,1)S(1)}, u32[]{:S(2)}, u32[]{:S(2)}) collective-permute-start(bf16[2,2,2,64,128]{4,3,2,1,0:T(8,128)(2,1)} %get-tuple-element.85), channel_id=1, source_target_pairs={{0,48},{8,56},{16,0},{24,8},{32,16},{40,24},{48,32},{56,40},{64,11... | collective-permute-start | bytes 393224 | tf_op jit(solution)/shard_map/ppermute | solution.py:415
  126.1 12.7 %collective-permute-start.13 = (bf16[4,2,2,64,128]{4,3,2,1,0:T(8,128)(2,1)S(1)}, bf16[4,2,2,64,128]{4,3,2,1,0:T(8,128)(2,1)S(1)}, u32[]{:S(2)}, u32[]{:S(2)}) collective-permute-start(bf16[4,2,2,64,128]{4,3,2,1,0:T(8,128)(2,1)S(1)} %add_convert_fusion), channel_id=1, source_target_pairs={{192,0},{200,8},{208,16},{216,24},{224,32},{232,40},{240,48},{248,... | collective-permute-start | bytes 786440 | tf_op jit(solution)/shard_map/ppermute | solution.py:425
  127.4 11.4 %collective-permute-start.12 = (bf16[4,2,2,64,128]{4,3,2,1,0:T(8,128)(2,1)S(1)}, bf16[4,2,2,64,128]{4,3,2,1,0:T(8,128)(2,1)S(1)}, u32[]{:S(2)}, u32[]{:S(2)}) collective-permute-start(bf16[4,2,2,64,128]{4,3,2,1,0:T(8,128)(2,1)S(1)} %add_convert_fusion), channel_id=1, source_target_pairs={{128,0},{136,8},{144,16},{152,24},{160,32},{168,40},{176,48},{184,... | collective-permute-start | bytes 786440 | tf_op jit(solution)/shard_map/ppermute | solution.py:425
  128.7 10.7 %collective-permute-start.11 = (bf16[4,2,2,64,128]{4,3,2,1,0:T(8,128)(2,1)S(1)}, bf16[4,2,2,64,128]{4,3,2,1,0:T(8,128)(2,1)S(1)}, u32[]{:S(2)}, u32[]{:S(2)}) collective-permute-start(bf16[4,2,2,64,128]{4,3,2,1,0:T(8,128)(2,1)S(1)} %add_convert_fusion), channel_id=1, source_target_pairs={{64,0},{72,8},{80,16},{88,24},{96,32},{104,40},{112,48},{120,56},{... | collective-permute-start | bytes 786440 | tf_op jit(solution)/shard_map/ppermute | solution.py:425
  139.4 1.6 copy-start.1
  143.2 1.1 copy-start.8
  167.6 15.2 %all-to-all-start.4 = ((bf16[8,64,640]{2,1,0:T(8,128)(2,1)}), bf16[8,64,640]{2,1,0:T(8,128)(2,1)S(1)}, u32[]{:S(2)}, u32[]{:S(2)}) async-start(bf16[8,64,640]{2,1,0:T(8,128)(2,1)} %bitcast.17), calls=%async_computation.5 | async-start | bytes 1310720 | tf_op jit(solution)/shard_map/all_to_all | solution.py:512
  191.0 15.3 %all-to-all-start.5 = ((bf16[8,2,64,128]{3,2,1,0:T(8,128)(2,1)}), bf16[8,2,64,128]{3,2,1,0:T(8,128)(2,1)S(1)}, u32[]{:S(2)}, u32[]{:S(2)}) async-start(bf16[8,2,64,128]{3,2,1,0:T(8,128)(2,1)} %bitcast.60), calls=%async_computation.6 | async-start | bytes 524288 | tf_op jit(solution)/shard_map/all_to_all | solution.py:515
Sparse Core Ops, SparseCore 0:
  21.3 38.2 all-gather.1
  143.3 47.6 reduce-scatter.1
